TPU v7x, 256 devices: a whole 4x4x8 slice. The times are simulated.
256 devices in a mesh: gx: 8 (over z_hi, x), gy: 32 (over z_lo, y, core).
Axes of the slice: x: 4, y: 4, z: 8 (z_hi: 2, z_lo: 4; z = z_hi * 4 + z_lo), core: 2. Of those that a mesh axis runs over, the one named last changes fastest.
Arguments:
- features: bfloat16 [100352, 512], P(('gx', 'gy')), may hold values from -24 to 24
- weight: bfloat16 [512, 2048], replicated, may hold values from -0.25 to 0.25
- cotangent: bfloat16 [100352, 2048], P(('gx', 'gy')), may hold values from -6 to 6
- pre_act: bfloat16 [100352, 2048], P(('gx', 'gy')), may hold values from -6 to 6
- bn_params: float32 [2, 2048], replicated, may hold values from 0.45 to 1.55
- master_weight: float32 [512, 2048], P(('gx', 'gy')), may hold values from -0.19 to 0.19
- weight_momentum: float32 [512, 2048], P(('gx', 'gy')), may hold values from -0.2 to 0.2
- bn_momentum: float32 [2, 2048], P(None, ('gx', 'gy')), may hold values from 0.6 to 1.6
Outputs:
- grad_input: bfloat16 [100352, 512], P(('gx', 'gy'))
- grad_skip: bfloat16 [100352, 2048], P(('gx', 'gy'))
- new_master: float32 [512, 2048], P(('gx', 'gy'))
- new_momentum: float32 [512, 2048], P(('gx', 'gy'))
- new_weight: bfloat16 [512, 2048], replicated
- new_bn_master: float32 [2, 2048], P(None, ('gx', 'gy'))
- new_bn_momentum: float32 [2, 2048], P(None, ('gx', 'gy'))
- new_bn: bfloat16 [2, 2048], replicated
All inputs are finite; a program needn't handle non-finite values.
Results may differ from a plain program's by a relative error of at most 0.011.
Values may be sent and summed in bfloat16 or wider, within the bound.
No kernel may reach another device: no remote copies, remote signals or barrier semaphores. Data moves between devices by JAX's collectives and lax.ppermute only.
A program may use at most 64 MiB of HBM per device.

v0:
```python
import jax
import jax.numpy as jnp
from jax import lax
from jax.sharding import PartitionSpec as P

eps_norm = 1e-05
momentum_rate = 0.9
learn_rate = 4.0
trust_coef = 0.001
decay_rate = 5e-05


def shards(
    features, weight, cotangent, pre_act, bn_params, master_weight, weight_momentum, bn_momentum
):
    rows = features.shape[0]
    width = weight.shape[1]
    devices_all = lax.axis_size(("gx", "gy"))
    mine = lax.axis_index(("gx", "gy"))
    bn_width = width // devices_all
    own_bn = lax.dynamic_slice_in_dim(bn_params, mine * bn_width, bn_width, 1)
    master_sq = jnp.stack(
        [
            jnp.sum(master_weight * master_weight),
            jnp.sum(own_bn[0] * own_bn[0]),
            jnp.sum(own_bn[1] * own_bn[1]),
        ]
    )
    conv = jnp.dot(features, weight, preferred_element_type=jnp.float32)
    sums, squares = lax.psum((jnp.sum(conv, axis=0), jnp.sum(conv * conv, axis=0)), "gx")
    count = jnp.float32(rows * lax.axis_size("gx"))
    mean = sums / count
    inv_std = lax.rsqrt(squares / count - mean * mean + eps_norm)
    normed = (conv - mean) * inv_std
    upstream = jnp.where(pre_act > 0, cotangent.astype(jnp.float32), jnp.float32(0.0))
    grad_skip = upstream.astype(jnp.bfloat16)
    local_b = jnp.sum(upstream, axis=0)
    local_g = jnp.sum(upstream * normed, axis=0)
    sum_b, sum_g = lax.psum((local_b, local_g), "gx")
    grad_conv = (
        bn_params[0] * inv_std * (upstream - sum_b / count - normed * sum_g / count)
    ).astype(jnp.bfloat16)
    weight_grad = lax.psum_scatter(
        lax.dot_general(
            features, grad_conv, (((0,), (0,)), ((), ())), preferred_element_type=jnp.float32
        ),
        ("gx", "gy"),
        scatter_dimension=0,
        tiled=True,
    )
    grad_input = lax.dot_general(
        grad_conv, weight, (((1,), (1,)), ((), ())), preferred_element_type=jnp.float32
    ).astype(jnp.bfloat16)
    bn_grad = lax.psum_scatter(
        jnp.stack([local_g, local_b]), ("gx", "gy"), scatter_dimension=1, tiled=True
    )
    grad_sq = jnp.stack(
        [
            jnp.sum(weight_grad * weight_grad),
            jnp.sum(bn_grad[0] * bn_grad[0]),
            jnp.sum(bn_grad[1] * bn_grad[1]),
        ]
    )
    joined_sq = lax.psum(jnp.concatenate([master_sq, grad_sq]), ("gx", "gy"))
    w_sq = joined_sq[0:3]
    g_sq = joined_sq[3:6]
    w_norm = jnp.sqrt(w_sq)
    trust = trust_coef * w_norm / (jnp.sqrt(g_sq) + decay_rate * w_norm)
    new_momentum = momentum_rate * weight_momentum + learn_rate * trust[0] * (
        weight_grad + decay_rate * master_weight
    )
    new_master = master_weight - new_momentum
    new_bn_momentum = momentum_rate * bn_momentum + learn_rate * trust[1:3][:, None] * (
        bn_grad + decay_rate * own_bn
    )
    new_bn_master = own_bn - new_bn_momentum
    new_weight, new_bn = (
        lax.all_gather(new_master.astype(jnp.bfloat16), ("gx", "gy"), axis=0, tiled=True),
        lax.all_gather(new_bn_master.astype(jnp.bfloat16), ("gx", "gy"), axis=1, tiled=True),
    )
    return (
        grad_input,
        grad_skip,
        new_master,
        new_momentum,
        new_weight,
        new_bn_master,
        new_bn_momentum,
        new_bn,
    )


def solution(mesh):
    in_specs = (
        P(("gx", "gy"), None),
        P(),
        P(("gx", "gy"), None),
        P(("gx", "gy"), None),
        P(),
        P(("gx", "gy"), None),
        P(("gx", "gy"), None),
        P(None, ("gx", "gy")),
    )
    out_specs = (
        P(("gx", "gy"), None),
        P(("gx", "gy"), None),
        P(("gx", "gy"), None),
        P(("gx", "gy"), None),
        P(),
        P(None, ("gx", "gy")),
        P(None, ("gx", "gy")),
        P(),
    )
    return jax.shard_map(shards, mesh=mesh, in_specs=in_specs, out_specs=out_specs, check_vma=False)
```

profile of v0, /device:TPU:1, one launch (start us, length us, event | category | flops | bytes accessed | tf_op | source)
XLA Modules:
  0.0 889.7 jit_solution(16039410837286981718)
XLA Ops:
  7.2 0.0 copy-start
  7.2 0.0 copy-start.2
  7.2 0.0 all-reduce.6.cloned.1.call-start
  7.2 4.1 fusion
  11.3 0.0 copy-done
  11.3 0.0 copy-done.2
  11.3 0.0 slice-start
  11.3 2.7 fusion.3
  14.0 49.1 %all-reduce.3 = (f32[2048]{0:T(1024)S(1)}, f32[2048]{0:T(1024)S(1)}) all-reduce(f32[2048]{0:T(1024)S(1)} %get-tuple-element.33, f32[2048]{0:T(1024)S(1)} %get-tuple-element.32), channel_id=1, replica_groups=mesh['gx'=8,'gy'=32] {'gx'}, use_global_device_ids=true, to_apply=%region_1.0 | all-reduce | flops 4096 | bytes 32768 | tf_op jit(solution)/shard_map/psum | solution.py:30
  63.1 0.0 slice-done
  63.1 3.4 fusion.1
  66.5 39.3 %all-reduce.2 = (f32[2048]{0:T(1024)S(1)}, f32[2048]{0:T(1024)S(1)}) all-reduce(f32[2048]{0:T(1024)S(1)} %get-tuple-element.35, f32[2048]{0:T(1024)S(1)} %get-tuple-element.34), channel_id=1, replica_groups=mesh['gx'=8,'gy'=32] {'gx'}, use_global_device_ids=true, to_apply=%region_7.8 | all-reduce | flops 4096 | bytes 32768 | tf_op jit(solution)/shard_map/psum | solution.py:39
  105.8 3.6 multiply_convert_fusion
  109.4 0.0 copy-start.1
  109.4 1.1 copy-done.1
  110.6 3.3 convolution_bitcast_fusion
  113.9 0.0 copy-start.4
  113.9 0.0 copy-start.3
  113.9 0.0 copy-start.5
  113.9 0.0 all-reduce.6.cloned.1.call-update
  113.9 0.0 all-gather.4.cloned.1.call-start
  114.0 88.5 %all-reduce.1 = f32[2,2048]{1,0:T(2,128)S(1)} all-reduce(f32[2,2048]{1,0:T(2,128)S(1)} %pad_maximum_fusion), channel_id=3, replica_groups=mesh['gx'=8,'gy'=32] {'gx','gy'}, use_global_device_ids=true, to_apply=%region_13.14.clone | all-reduce | flops 4096 | bytes 32768
  202.5 0.0 copy-done.4
  202.5 0.1 constant_dynamic-slice_fusion.2
  202.6 0.1 constant_dynamic-slice_fusion
  202.7 0.6 multiply_reduce_fusion.6
  203.3 0.6 multiply_reduce_fusion.4
  203.9 0.0 copy-done.3
  203.9 0.6 multiply_reduce_fusion.3
  204.5 186.3 %all-reduce.6.cloned.1.call-done = f32[512,2048]{0,1:T(8,128)} async-done(((f32[512,2048]{0,1:T(8,128)}), f32[512,2048]{0,1:T(8,128)}) %all-reduce.6.cloned.1.call-update) | async-done | bytes 4194320
  390.8 2.2 multiply_reduce_fusion.2
  392.9 4.0 concatenate.3
  396.9 0.3 copy.41
  397.2 77.7 %psum.39 = f32[6]{0:T(128)S(1)} all-reduce(f32[6]{0:T(128)S(1)} %concatenate.3), channel_id=1, replica_groups=mesh['gx'=8,'gy'=32] {'gx','gy'}, use_global_device_ids=true, to_apply=%region_16.17 | all-reduce | flops 6 | bytes 48 | tf_op jit(solution)/shard_map/psum | solution.py:64
  474.9 0.1 add_divide_fusion
  475.1 0.0 copy-done.5
  475.1 0.6 convert_bitcast_fusion
  475.7 0.0 all-gather.4.cloned.1.call-update
  475.8 0.0 copy-start.6
  475.8 3.2 convolution_convert_fusion
  479.0 0.1 slice_multiply_fusion
  479.0 0.0 copy-done.6
  479.1 0.6 convert_bitcast_fusion.1
  479.7 339.1 %all-gather.1 = bf16[256,8,2]{1,2,0:T(2,128)(2,1)S(1)} all-gather(bf16[1,8,2]{1,2,0:T(2,128)(2,1)S(1)} %get-tuple-element.44), channel_id=1, replica_groups=mesh['gx'=8,'gy'=32] {'gx','gy'}, dimensions={0}, use_global_device_ids=true | all-gather | bytes 8224 | tf_op jit(solution)/shard_map/all_gather | solution.py:79
  818.8 0.8 reshape.32
  819.5 59.2 %all-gather.4.cloned.1.call-done = bf16[256,2,2048]{2,1,0:T(2,128)(2,1)} async-done(((bf16[1,2,2048]{2,1,0:T(2,128)(2,1)}), bf16[256,2,2048]{2,1,0:T(2,128)(2,1)}) %all-gather.4.cloned.1.call-update) | async-done | bytes 2097168 | tf_op jit(solution)/shard_map/all_gather | solution.py:78
  878.7 4.1 reshape.30
  (4 shorter events, 0.1 us)
Async XLA Ops:
  7.2 4.2 copy-start
  7.2 4.2 copy-start.2
  7.2 383.6 %all-reduce.6.cloned.1.call-start = ((), (), s32[]{:S(2)}) async-start(), calls=%async_computation.1 | async-start | bytes 8388608
  11.3 51.8 %slice-start = ((f32[2,2048]{1,0:T(2,128)}), f32[1,2048]{1,0:T(1,128)S(1)}, s32[]{:S(2)}) async-start(f32[2,2048]{1,0:T(2,128)} %param.12), calls=%async_computation.2 | async-start | bytes 16384 | tf_op jit(solution)/shard_map/slice | solution.py:41
  109.4 1.2 copy-start.1
  113.9 88.6 %copy-start.4 = (f32[2,2048]{1,0:T(2,128)S(1)}, f32[2,2048]{1,0:T(2,128)}, u32[]{:S(2)}) copy-start(f32[2,2048]{1,0:T(2,128)} %param.12) | copy-start | bytes 49156
  113.9 90.0 %copy-start.3 = (f32[2,2048]{1,0:T(2,128)S(1)}, f32[2,2048]{1,0:T(2,128)}, u32[]{:S(2)}) copy-start(f32[2,2048]{1,0:T(2,128)} %param.13) | copy-start | bytes 49156
  113.9 361.2 %copy-start.5 = (f32[2,2048]{1,0:T(2,128)S(1)}, f32[2,2048]{1,0:T(2,128)}, u32[]{:S(2)}) copy-start(f32[2,2048]{1,0:T(2,128)} %param.14) | copy-start | bytes 49156
  113.9 764.8 %all-gather.4.cloned.1.call-start = ((), (), s32[]{:S(2)}) async-start(), calls=%async_computation | async-start | bytes 2105344 | tf_op jit(solution)/shard_map/all_gather | solution.py:78
  475.8 3.3 copy-start.6
Sparse Core Ops, SparseCore 0:
  114.0 276.7 all-reduce.5
  475.9 402.7 all-gather.3
where the time goes:
time: 890 us
  blocking collectives  594 us (67%)
  waiting for transfers between devices  245 us (28%)
  other arithmetic  16.5 us (2%)
  between operations  14.2 us (2%)
  local copies, waits for them, and re-layouts  10.5 us (1%)
  matrix products  9.18 us (1%)
    all_gather x1, blocking collectives, shards(): lax.all_gather(new_bn_master.astype(jnp.bfloat16), ('gx', 'gy'), axis=1,...  339 us
    unnamed x3, waiting for transfers between devices  186 us
    unnamed x1, blocking collectives  88.5 us
    psum x1, blocking collectives, shards(): joined_sq = lax.psum(jnp.concatenate([master_sq, grad_sq]), ('gx', 'gy'))  77.7 us
    all_gather x1, waiting for transfers between devices, shards(): lax.all_gather(new_master.astype(jnp.bfloat16), ('gx', 'gy'), axis=0, til...  59.2 us
    psum x1, blocking collectives, shards(): lax.psum((jnp.sum(conv, axis=0), jnp.sum(conv * conv, axis=0)), 'gx')  49.1 us
    psum x1, blocking collectives, shards(): sum_b, sum_g = lax.psum((local_b, local_g), 'gx')  39.3 us
  transfers between devices with their start and end apart: 2, of which 2 were waited for; matrix products, arithmetic and copies ran while one was open for 1% of the time, Pallas kernels for 0%

commit v1 on v0

v1 whole, which is shorter than its diff:
```python
import jax
import jax.numpy as jnp
from jax import lax
from jax.sharding import Mesh, PartitionSpec as P

eps_norm = 1e-05
momentum_rate = 0.9
learn_rate = 4.0
trust_coef = 0.001
decay_rate = 5e-05

AXES = ("zh", "x", "zl", "y", "c")
SIZES = (2, 4, 4, 4, 2)
GX = ("zh", "x")
YZ = ("zh", "zl", "y")
BF = jnp.bfloat16
F32 = jnp.float32


def index_of(zh, x, zl, y, c):
    return (((zh * 4 + x) * 4 + zl) * 4 + y) * 2 + c


def pairs(move):
    out = []
    for zh in range(2):
        for x in range(4):
            for zl in range(4):
                for y in range(4):
                    for c in range(2):
                        out.append((index_of(zh, x, zl, y, c), index_of(*move(zh, x, zl, y, c))))
    return out


SIBLING = pairs(lambda zh, x, zl, y, c: (zh, x, zl, y, 1 - c))


def to_x(k):
    return pairs(lambda zh, x, zl, y, c: (zh, (x + k) % 4, zl, y, c))


def select(rows, x, c):
    t = lax.broadcasted_iota(jnp.int32, (rows, 512), 1)
    r = lax.broadcasted_iota(jnp.int32, (rows, 512), 0)
    cc = c ^ (t >> 8)
    xx = (x + (t >> 6)) & 3
    want = ((t >> 5) & 1) * 256 + xx * 64 + ((t >> 3) & 3) * 16 + ((t >> 1) & 3) * 4 + cc * 2 + (t & 1)
    return (r == want).astype(BF)


def hi_lo(v):
    hi = v.astype(BF)
    lo = (v - hi.astype(F32)).astype(BF)
    return hi, lo


def shards(features, weight, cotangent, pre_act, bn_params, master, momentum, bn_momentum):
    x = lax.axis_index("x")
    c = lax.axis_index("c")
    mine = lax.axis_index(AXES)
    rows = features.shape[0]
    count = jnp.float32(rows * 8)
    sel = select(512, x, c)
    own_bn = lax.dynamic_slice_in_dim(bn_params, mine * 8, 8, 1)

    conv = jnp.dot(features, weight, preferred_element_type=F32)
    up = jnp.where(pre_act > 0, cotangent, jnp.zeros_like(cotangent))
    upf = up.astype(F32)
    local = jnp.stack([jnp.sum(conv, 0), jnp.sum(conv * conv, 0), jnp.sum(upf, 0), jnp.sum(upf * conv, 0)])
    sent = jnp.broadcast_to(local.reshape(1, 8, 1024), (8, 8, 1024))
    got = lax.all_to_all(sent, GX, 0, 0, tiled=True)
    sums = jnp.sum(got, axis=0).reshape(4, 2048)
    mean = sums[0] / count
    inv_std = lax.rsqrt(sums[1] / count - mean * mean + eps_norm)
    sum_b = sums[2]
    sum_g = inv_std * (sums[3] - mean * sums[2])
    local_b = local[2]
    local_g = inv_std * (local[3] - mean * local[2])
    normed = (conv - mean) * inv_std
    grad_conv = (bn_params[0] * inv_std * (upf - sum_b / count - normed * sum_g / count)).astype(BF)
    grad_input = lax.dot_general(
        grad_conv, weight, (((1,), (1,)), ((), ())), preferred_element_type=F32
    ).astype(BF)

    feat = jnp.dot(features, sel, preferred_element_type=F32).astype(BF)
    g = lax.dot_general(feat, grad_conv, (((0,), (0,)), ((), ())), preferred_element_type=F32)
    bn_rows = jnp.stack([local_g, local_b]).reshape(2, 256, 8).transpose(1, 0, 2).reshape(512, 8).astype(BF)
    extra = lax.dot_general(sel, bn_rows, (((0,), (0,)), ((), ())), preferred_element_type=F32)
    g = jnp.concatenate([g, jnp.pad(extra, ((0, 0), (0, 120)))], axis=1)
    half = g[:256] + lax.ppermute(g[256:].astype(BF), AXES, SIBLING).astype(F32)
    chunk = half[:64]
    for k in (1, 2, 3):
        part = lax.ppermute(half[64 * k : 64 * k + 64].astype(BF), AXES, to_x(k))
        chunk = chunk + part.astype(F32)
    base = master - momentum_rate * momentum
    pieces = chunk[:, :2048].reshape(32, 16, 256).astype(BF)
    bases = jnp.broadcast_to(base.reshape(1, 16, 256).astype(BF), (32, 16, 256))
    extras = jnp.pad(chunk[:, 2048:].reshape(32, 2, 128), ((0, 0), (0, 14), (0, 0))).astype(BF)
    got = lax.all_to_all(jnp.concatenate([pieces, bases, extras], axis=2), YZ, 0, 0, tiled=True)
    weight_grad = jnp.sum(got[:, :, :256].astype(F32), axis=0).reshape(2, 2048)
    bn_grad = jnp.sum(got[:, :2, 512:520].astype(F32), axis=0)
    base_chunk = got[:, :, 256:512].reshape(64, 2048)
    step = weight_grad + decay_rate * master
    bn_step = bn_grad + decay_rate * own_bn
    bn_base = own_bn - momentum_rate * bn_momentum
    squares = jnp.stack(
        [
            jnp.stack([jnp.sum(weight_grad * weight_grad), jnp.sum(master * master)]),
            jnp.zeros((2,), F32),
        ]
    )
    squares = jnp.concatenate([squares, jnp.sum(bn_grad * bn_grad, 1)[:, None], jnp.sum(own_bn * own_bn, 1)[:, None]], axis=1)
    own_extra = jnp.concatenate([*hi_lo(bn_step), *hi_lo(bn_base), *hi_lo(squares)], axis=1)
    own_piece = jnp.concatenate([step.reshape(16, 256).astype(BF), jnp.pad(own_extra, ((0, 14), (0, 88)))], axis=1)
    got = lax.all_to_all(jnp.broadcast_to(own_piece[None], (32, 16, 384)), YZ, 0, 0, tiled=True)
    chunk = jnp.concatenate([got[:, :, :256].reshape(64, 2048), got[:, :2, 256:].reshape(64, 128)], axis=1)

    def spread(block):
        parts = [block] + [lax.ppermute(block, AXES, to_x(-k % 4)) for k in (1, 2, 3)]
        mine_half = jnp.concatenate(parts, axis=0)
        other = lax.ppermute(mine_half, AXES, SIBLING)
        return jnp.concatenate([mine_half, other], axis=0)

    base_all = spread(base_chunk)
    step_all = spread(chunk)
    tail = jnp.dot(sel, step_all[:, 2048:], preferred_element_type=F32)
    sq = jnp.sum((tail[:, 32:36] + tail[:, 36:40]).reshape(256, 2, 4), axis=0)
    g_sq = jnp.concatenate([sq[:1, 0], sq[:, 2]])
    w_sq = jnp.concatenate([sq[:1, 1], sq[:, 3]])
    w_norm = jnp.sqrt(w_sq)
    trust = trust_coef * w_norm / (jnp.sqrt(g_sq) + decay_rate * w_norm)
    rate = learn_rate * trust
    moved = (base_all.astype(F32) - rate[0] * step_all[:, :2048].astype(F32)).astype(BF)
    new_weight = jnp.dot(sel, moved, preferred_element_type=F32).astype(BF)
    tail = tail.reshape(256, 2, 128)
    bn_all = (tail[:, :, 16:24] + tail[:, :, 24:32]) - rate[1:][None, :, None] * (tail[:, :, 0:8] + tail[:, :, 8:16])
    new_bn = bn_all.transpose(1, 0, 2).reshape(2, 2048).astype(BF)
    new_momentum = momentum_rate * momentum + rate[0] * step
    new_master = master - new_momentum
    new_bn_momentum = momentum_rate * bn_momentum + rate[1:][:, None] * bn_step
    new_bn_master = own_bn - new_bn_momentum
    return (grad_input, up, new_master, new_momentum, new_weight, new_bn_master, new_bn_momentum, new_bn)


def solution(mesh):
    fine = Mesh(mesh.devices.reshape(SIZES), AXES)
    rows = P(AXES, None)
    cols = P(None, AXES)
    return jax.shard_map(
        shards,
        mesh=fine,
        in_specs=(rows, P(), rows, rows, P(), rows, rows, cols),
        out_specs=(rows, rows, rows, rows, P(), cols, cols, P()),
        check_vma=False,
    )
```

time: 890 us -> 158 us (0.18)
  blocking collectives: 594 us -> 0 us
  waiting for transfers between devices: 245 us -> 54.1 us
  starting transfers between devices: 0.08 us -> 44 us
  between operations: 14.2 us -> 1.08 us
  matrix products: 9.18 us -> 19.7 us
    all_gather x1 -> x0, blocking collectives: 339 us -> none  [shards(): lax.all_gather(new_bn_master.astype(jnp.bfloat16), ('gx', 'gy'), axis=1,...]
    unnamed x3 -> x0, waiting for transfers between devices: 186 us -> none
    psum x3 -> x0, blocking collectives: 166 us -> none  [the longest x1 77.7 us: shards(): joined_sq = lax.psum(jnp.concatenate([master_sq, grad_sq]), ('gx', 'gy'))]
    unnamed x1 -> x0, blocking collectives: 88.5 us -> none
    all_gather x1 -> x0, waiting for transfers between devices: 59.2 us -> none  [shards(): lax.all_gather(new_master.astype(jnp.bfloat16), ('gx', 'gy'), axis=0, til...]
    all_to_all x0 -> x3, waiting for transfers between devices: none -> 29.5 us  [the longest x1 18.6 us: shards(): lax.all_to_all(jnp.concatenate([pieces, bases, extras], axis=2), YZ, 0, 0...]
    all_to_all x0 -> x3, starting transfers between devices: none -> 25.2 us  [the longest x1 11.5 us: shards(): got = lax.all_to_all(sent, GX, 0, 0, tiled=True)]
    ppermute x0 -> x12, waiting for transfers between devices: none -> 24.6 us  [the longest x3 14.8 us: shards(): part = lax.ppermute(half[64 * k:64 * k + 64].astype(BF), AXES, to_x(k))]
  transfers between devices with their start and end apart: 2 -> 15, of which waited for: 2 -> 10; matrix products, arithmetic and copies ran while one was open for 1% -> 11% of each run, Pallas kernels for 0% -> 0%
where the time goes in v1:
time: 158 us; the launch traced here: 157 us
  waiting for transfers between devices  54.1 us (34%)
  starting transfers between devices  44 us (28%)
  other arithmetic  22.6 us (14%)
  matrix products  19.7 us (12%)
  local copies, waits for them, and re-layouts  15.5 us (10%)
    all_to_all x1, waiting for transfers between devices, shards(): lax.all_to_all(jnp.concatenate([pieces, bases, extras], axis=2), YZ, 0, 0...  18.6 us
    ppermute x3, waiting for transfers between devices, shards(): part = lax.ppermute(half[64 * k:64 * k + 64].astype(BF), AXES, to_x(k))  14.8 us
    all_to_all x1, starting transfers between devices, shards(): got = lax.all_to_all(sent, GX, 0, 0, tiled=True)  11.5 us
    all_to_all x1, waiting for transfers between devices, shards(): got = lax.all_to_all(sent, GX, 0, 0, tiled=True)  9.75 us
    ppermute x2, starting transfers between devices, spread(): other = lax.ppermute(mine_half, AXES, SIBLING)  8.77 us
    all_to_all x1, starting transfers between devices, shards(): lax.all_to_all(jnp.concatenate([pieces, bases, extras], axis=2), YZ, 0, 0...  8.2 us
    ppermute x6, waiting for transfers between devices, spread(): lax.ppermute(block, AXES, to_x(-k % 4))  7.4 us
    unnamed x33, local copies, waits for them, and re-layouts  6.59 us
  transfers between devices with their start and end apart: 15, of which 10 were waited for; matrix products, arithmetic and copies ran while one was open for 11% of the time, Pallas kernels for 0%

profile of v1, /device:TPU:1, one launch (start us, length us, event | category | flops | bytes accessed | tf_op | source)
XLA Modules:
  0.0 157.0 jit_solution(16629336260774289204)
XLA Ops:
  0.6 1.6 %copy-done = bf16[512,2048]{1,0:T(8,128)(2,1)S(1)} copy-done((bf16[512,2048]{1,0:T(8,128)(2,1)S(1)}, bf16[512,2048]{1,0:T(8,128)(2,1)}, u32[]{:S(2)}) %copy-start) | copy-done | bytes 2097176
  2.2 5.7 %fusion.39 = (f32[2048]{0:T(1024)S(1)}, f32[2048]{0:T(1024)S(1)}, f32[2048]{0:T(1024)S(1)}, f32[2048]{0:T(1024)S(1)}, bf16[392,2048]{1,0:T(8,128)(2,1)}, /*index=5*/f32[392,2048]{1,0:T(8,128)}) fusion(bf16[392,2048]{1,0:T(8,128)(2,1)} %param.10, bf16[392,2048]{1,0:T(8,128)(2,1)} %param.11, bf16[392,512]{1,0:T(8,128)(2,1)} %param.8, ...), kind=kOutput, calls=%fused_computation.108 | convolution fusion | flops 829300736 | bytes 10559488 | tf_op jit(solution)/shard_map/dot_general | solution.py:66
  8.0 0.7 broadcast_in_dim.13
  8.7 11.5 %all-to-all-start = ((f32[8,8,1024]{2,1,0:T(8,128)}), f32[8,8,1024]{2,1,0:T(8,128)S(1)}, u32[]{:S(2)}, u32[]{:S(2)}) async-start(f32[8,8,1024]{2,1,0:T(8,128)} %broadcast_in_dim.13), calls=%async_computation | async-start | bytes 524288 | tf_op jit(solution)/shard_map/all_to_all | solution.py:71
  20.5 9.7 %all-to-all-done = f32[8,8,1024]{2,1,0:T(8,128)S(1)} async-done(((f32[8,8,1024]{2,1,0:T(8,128)}), f32[8,8,1024]{2,1,0:T(8,128)S(1)}, u32[]{:S(2)}, u32[]{:S(2)}) %all-to-all-start) | async-done | bytes 262176 | tf_op jit(solution)/shard_map/all_to_all | solution.py:71
  30.7 0.2 copy.47
  30.9 0.5 fusion.9
  31.4 4.5 %fusion.3 = bf16[392,2048]{1,0:T(8,128)(2,1)} fusion(bf16[392,2048]{1,0:T(8,128)(2,1)} %get-tuple-element.25, f32[392,2048]{1,0:T(8,128)} %get-tuple-element.52, f32[2048]{0:T(1024)S(1)} %get-tuple-element.47, f32[2048]{0:T(1024)S(1)} %get-tuple-element.46, f32[2048]{0:T(1024)S(1)} %bitcast.76, f32[2048]{0:T(1024)S(1)} %get-tuple-element.48, f32[2048]{0:T(1024)S(1)} %bitcast.75), kind=kLoop, calls=%fused_computation.9 | loop fusion | flops 7225344 | bytes 6463488 | tf_op jit(solution)/shard_map/convert_element_type | solution.py:80
  35.9 5.0 %fusion.7 = f32[512,2048]{1,0:T(8,128)} fusion(bf16[392,2048]{1,0:T(8,128)(2,1)} %fusion.3, bf16[392,512]{1,0:T(8,128)(2,1)S(1)} %copy-done.11, s32[512]{0:T(512)S(1)} %and_add_fusion), kind=kOutput, calls=%fused_computation.21 | convolution fusion | flops 1028067328 | bytes 6203392 | tf_op jit(solution)/shard_map/dot_general | solution.py:86
  40.9 2.5 %select_maximum_fusion = f32[512,2176]{1,0:T(8,128)S(1)} fusion(f32[512,8]{1,0:T(8,128)S(1)} %fusion.9, f32[512,2048]{1,0:T(8,128)} %fusion.7), kind=kLoop, calls=%fused_computation.3 | loop fusion | flops 3342336 | bytes 8667136 | tf_op jit(solution)/shard_map/concatenate | solution.py:89
  43.6 2.2 %collective-permute-start = (bf16[256,2176]{1,0:T(8,128)(2,1)S(1)}, bf16[256,2176]{1,0:T(8,128)(2,1)S(1)}, u32[]{:S(2)}, u32[]{:S(2)}) collective-permute-start(bf16[256,2176]{1,0:T(8,128)(2,1)S(1)} %slice.226), channel_id=1, source_target_pairs={{0,1},{1,0},{2,3},{3,2},{4,5},{5,4},{6,7},{7,6},{8,9},{9,8},{10,11... | collective-permute-start | bytes 3342344 | tf_op jit(solution)/shard_map/ppermute | solution.py:90
  45.8 2.4 %collective-permute-done = bf16[256,2176]{1,0:T(8,128)(2,1)S(1)} collective-permute-done((bf16[256,2176]{1,0:T(8,128)(2,1)S(1)}, bf16[256,2176]{1,0:T(8,128)(2,1)S(1)}, u32[]{:S(2)}, u32[]{:S(2)}) %collective-permute-start) | collective-permute-done | bytes 1114144 | tf_op jit(solution)/shard_map/ppermute | solution.py:90
  48.2 1.6 %fusion.41 = (bf16[256,2176]{1,0:T(8,128)(2,1)S(1)}, f32[256,2176]{1,0:T(8,128)}) fusion(bf16[256,2176]{1,0:T(8,128)(2,1)S(1)} %collective-permute-done, f32[512,2176]{1,0:T(8,128)S(1)} %select_maximum_fusion), kind=kLoop, calls=%fused_computation.110 | loop fusion | flops 1671168 | bytes 6684672 | tf_op jit(solution)/shard_map/convert.7
  49.8 0.8 fusion.42
  50.6 0.5 collective-permute-start.3
  51.1 1.2 collective-permute-start.2
  52.4 6.3 %collective-permute-done.3 = bf16[64,2176]{1,0:T(8,128)(2,1)S(1)} collective-permute-done((bf16[64,2176]{1,0:T(8,128)(2,1)}, bf16[64,2176]{1,0:T(8,128)(2,1)S(1)}, u32[]{:S(2)}, u32[]{:S(2)}) %collective-permute-start.3) | collective-permute-done | bytes 278560 | tf_op jit(solution)/shard_map/ppermute | solution.py:93
  58.7 1.6 collective-permute-done.2
  60.2 7.0 %collective-permute-done.1 = bf16[64,2176]{1,0:T(8,128)(2,1)S(1)} collective-permute-done((bf16[64,2176]{1,0:T(8,128)(2,1)S(1)}, bf16[64,2176]{1,0:T(8,128)(2,1)S(1)}, u32[]{:S(2)}, u32[]{:S(2)}) %collective-permute-start.1) | collective-permute-done | bytes 278560 | tf_op jit(solution)/shard_map/ppermute | solution.py:93
  67.2 1.2 fusion.13
  68.4 0.1 convert_element_type.129
  68.6 0.9 fusion.10
  69.5 8.2 %all-to-all-start.1 = ((bf16[32,16,640]{2,1,0:T(8,128)(2,1)}), bf16[32,16,640]{2,1,0:T(8,128)(2,1)S(1)}, u32[]{:S(2)}, u32[]{:S(2)}) async-start(bf16[32,16,640]{2,1,0:T(8,128)(2,1)} %fusion.10), calls=%async_computation.1 | async-start | bytes 1310720 | tf_op jit(solution)/shard_map/all_to_all | solution.py:99
  77.7 18.6 %all-to-all-done.1 = bf16[32,16,640]{2,1,0:T(8,128)(2,1)S(1)} async-done(((bf16[32,16,640]{2,1,0:T(8,128)(2,1)}), bf16[32,16,640]{2,1,0:T(8,128)(2,1)S(1)}, u32[]{:S(2)}, u32[]{:S(2)}) %all-to-all-start.1) | async-done | bytes 655392 | tf_op jit(solution)/shard_map/all_to_all | solution.py:99
  96.4 0.6 reshape.210
  97.0 0.6 multiply_reduce_fusion.2
  97.6 0.1 reshape.214
  97.8 1.3 collective-permute-start.9
  99.1 0.8 collective-permute-start.10
  99.9 1.5 subtract_convert_fusion.4
  101.6 1.3 fusion.34
  102.9 1.4 maximum_bitcast_fusion.1
  104.5 0.8 broadcast_in_dim.17
  105.3 5.6 %all-to-all-start.2 = ((bf16[32,16,384]{2,1,0:T(8,128)(2,1)}), bf16[32,16,384]{2,1,0:T(8,128)(2,1)S(1)}, u32[]{:S(2)}, u32[]{:S(2)}) async-start(bf16[32,16,384]{2,1,0:T(8,128)(2,1)} %broadcast_in_dim.17), calls=%async_computation.2 | async-start | bytes 786432 | tf_op jit(solution)/shard_map/all_to_all | solution.py:115
  110.9 3.2 %convolution_convert_fusion.1 = bf16[392,512]{1,0:T(8,128)(2,1)} fusion(bf16[392,2048]{1,0:T(8,128)(2,1)} %fusion.3, bf16[512,2048]{1,0:T(8,128)(2,1)S(1)} %copy-done), kind=kOutput, calls=%fused_computation.19 | convolution fusion | flops 822284288 | bytes 4104192 | tf_op jit(solution)/shard_map/dot_general | solution.py:81
  114.1 0.7 constant_dynamic-update-slice_fusion.9
  114.8 2.0 %pad_maximum_fusion.1 = bf16[256,2048]{1,0:T(8,128)(2,1)} fusion(bf16[64,2048]{1,0:T(8,128)(2,1)S(1)} %collective-permute-done.10, bf16[64,2048]{1,0:T(8,128)(2,1)S(1)} %collective-permute-done.9, bf16[64,2048]{1,0:T(8,128)(2,1)} %collective-permute-done.8, bf16[64,2048]{1,0:T(8,128)(2,1)S(1)} %reshape.214), kind=kLoop, calls=%fused_computation.23 | loop fusion | flops 4194304 | bytes 2097152 | tf_op jit(solution)/shard_map/concatenate | solution.py:120
  116.8 2.8 %collective-permute-start.11 = (bf16[256,2048]{1,0:T(8,128)(2,1)}, bf16[256,2048]{1,0:T(8,128)(2,1)}, u32[]{:S(2)}, u32[]{:S(2)}) collective-permute-start(bf16[256,2048]{1,0:T(8,128)(2,1)} %pad_maximum_fusion.1), channel_id=1, source_target_pairs={{0,1},{1,0},{2,3},{3,2},{4,5},{5,4},{6,7},{7,6},{8,9},{9,8},{10,11... | collective-permute-start | bytes 3145736 | tf_op jit(solution)/shard_map/ppermute | solution.py:121
  119.6 1.7 %constant_dynamic-update-slice_fusion.8 = bf16[512,2048]{1,0:T(8,128)(2,1)} fusion(bf16[512,2048]{1,0:T(8,128)(2,1)} %constant_dynamic-update-slice_fusion.9, bf16[64,2048]{1,0:T(8,128)(2,1)} %collective-permute-done.8), kind=kLoop, calls=%fused_computation.58 | loop fusion | bytes 524288
  121.3 1.2 all-to-all-done.2
  122.4 0.1 reshape.211
  122.6 2.1 %collective-permute-start.4 = (bf16[64,2176]{1,0:T(8,128)(2,1)S(1)}, bf16[64,2176]{1,0:T(8,128)(2,1)S(1)}, u32[]{:S(2)}, u32[]{:S(2)}) collective-permute-start(bf16[64,2176]{1,0:T(8,128)(2,1)S(1)} %get-tuple-element.29), channel_id=1, source_target_pairs={{0,96},{1,97},{2,98},{3,99},{4,100},{5,101},{6,102},{7,103},{8,104... | collective-permute-start | bytes 835592 | tf_op jit(solution)/shard_map/ppermute | solution.py:119
  124.7 1.1 collective-permute-start.5
  125.8 0.8 collective-permute-start.6
  126.6 0.7 constant_dynamic-update-slice_fusion.7
  127.3 0.7 constant_dynamic-update-slice_fusion.6
  128.0 3.7 %collective-permute-done.4 = bf16[64,2176]{1,0:T(8,128)(2,1)S(1)} collective-permute-done((bf16[64,2176]{1,0:T(8,128)(2,1)S(1)}, bf16[64,2176]{1,0:T(8,128)(2,1)S(1)}, u32[]{:S(2)}, u32[]{:S(2)}) %collective-permute-start.4) | collective-permute-done | bytes 278560 | tf_op jit(solution)/shard_map/ppermute | solution.py:119
  131.7 3.7 %collective-permute-done.6 = bf16[64,2176]{1,0:T(8,128)(2,1)S(1)} collective-permute-done((bf16[64,2176]{1,0:T(8,128)(2,1)S(1)}, bf16[64,2176]{1,0:T(8,128)(2,1)S(1)}, u32[]{:S(2)}, u32[]{:S(2)}) %collective-permute-start.6) | collective-permute-done | bytes 278560 | tf_op jit(solution)/shard_map/ppermute | solution.py:119
  135.5 6.0 %collective-permute-start.7 = (bf16[256,2176]{1,0:T(8,128)(2,1)S(1)}, bf16[256,2176]{1,0:T(8,128)(2,1)S(1)}, u32[]{:S(2)}, u32[]{:S(2)}) collective-permute-start(bf16[256,2176]{1,0:T(8,128)(2,1)S(1)} %pad_maximum_fusion), channel_id=1, source_target_pairs={{0,1},{1,0},{2,3},{3,2},{4,5},{5,4},{6,7},{7,6},{8,9},{9,8},{10,11... | collective-permute-start | bytes 3342344 | tf_op jit(solution)/shard_map/ppermute | solution.py:121
  141.6 2.3 %constant_dynamic-update-slice_fusion.5 = bf16[512,2048]{1,0:T(8,128)(2,1)} fusion(bf16[512,2048]{1,0:T(8,128)(2,1)} %constant_dynamic-update-slice_fusion.6, bf16[256,2048]{1,0:T(8,128)(2,1)} %collective-permute-done.11), kind=kLoop, calls=%fused_computation.55 | loop fusion | bytes 2097152 | tf_op jit(solution)/shard_map/concatenate | solution.py:122
  144.0 0.1 constant_dynamic-update-slice_fusion
  144.1 0.3 fusion.8
  144.5 1.0 copy-done.5
  145.5 0.1 copy.51
  145.7 0.3 reduce_sum.125
  145.9 0.2 slice_reduce_fusion.1
  146.2 0.6 fusion.43
  146.8 0.1 copy.52
  146.9 1.4 fusion.33
  148.3 0.7 fusion.40
  149.0 4.9 %convolution_convert_fusion = bf16[512,2048]{1,0:T(8,128)(2,1)} fusion(bf16[512,2048]{1,0:T(8,128)(2,1)} %constant_dynamic-update-slice_fusion.5, bf16[512,2176]{1,0:T(8,128)(2,1)} %copy-done.5, f32[]{:T(128)S(1)} %bitcast.83, s32[512]{0:T(512)S(1)} %copy-done.10), kind=kOutput, calls=%fused_computation.12 | convolution fusion | flops 1080295424 | bytes 6293508 | tf_op jit(solution)/shard_map/dot_general | solution.py:134
  154.0 1.3 fusion.36
  155.3 0.9 fusion.23
  156.2 0.8 convert_element_type.151
  (73 shorter events, 2.0 us)
Async XLA Ops:
  0.6 1.6 %copy-start = (bf16[512,2048]{1,0:T(8,128)(2,1)S(1)}, bf16[512,2048]{1,0:T(8,128)(2,1)}, u32[]{:S(2)}) copy-start(bf16[512,2048]{1,0:T(8,128)(2,1)} %param.9) | copy-start | bytes 6291460
  8.0 23.0 %copy-start.6 = (f32[2,2048]{1,0:T(2,128)S(1)}, f32[2,2048]{1,0:T(2,128)}, u32[]{:S(2)}) copy-start(f32[2,2048]{1,0:T(2,128)} %param.12) | copy-start | bytes 49156
  8.7 21.6 %all-to-all-start = ((f32[8,8,1024]{2,1,0:T(8,128)}), f32[8,8,1024]{2,1,0:T(8,128)S(1)}, u32[]{:S(2)}, u32[]{:S(2)}) async-start(f32[8,8,1024]{2,1,0:T(8,128)} %broadcast_in_dim.13), calls=%async_computation | async-start | bytes 524288 | tf_op jit(solution)/shard_map/all_to_all | solution.py:71
  20.5 15.4 %copy-start.9 = (s32[512]{0:T(512)}, s32[512]{0:T(512)S(1)}, u32[]{:S(2)}) copy-start(s32[512]{0:T(512)S(1)} %and_add_fusion) | copy-start | bytes 6148
  31.4 4.5 %copy-start.11 = (bf16[392,512]{1,0:T(8,128)(2,1)S(1)}, bf16[392,512]{1,0:T(8,128)(2,1)}, u32[]{:S(2)}) copy-start(bf16[392,512]{1,0:T(8,128)(2,1)} %param.8) | copy-start | bytes 1204228
  43.6 8.7 %copy-start.1 = (f32[2,2048]{1,0:T(2,128)S(1)}, f32[2,2048]{1,0:T(2,128)}, u32[]{:S(2)}) copy-start(f32[2,2048]{1,0:T(2,128)} %param.13) | copy-start | bytes 49156
  43.6 8.7 %copy-start.3 = (f32[2,2048]{1,0:T(2,128)S(1)}, f32[2,2048]{1,0:T(2,128)}, u32[]{:S(2)}) copy-start(f32[2,2048]{1,0:T(2,128)} %param.14) | copy-start | bytes 49156
  43.6 4.6 %collective-permute-start = (bf16[256,2176]{1,0:T(8,128)(2,1)S(1)}, bf16[256,2176]{1,0:T(8,128)(2,1)S(1)}, u32[]{:S(2)}, u32[]{:S(2)}) collective-permute-start(bf16[256,2176]{1,0:T(8,128)(2,1)S(1)} %slice.226), channel_id=1, source_target_pairs={{0,1},{1,0},{2,3},{3,2},{4,5},{5,4},{6,7},{7,6},{8,9},{9,8},{10,11... | collective-permute-start | bytes 3342344 | tf_op jit(solution)/shard_map/ppermute | solution.py:90
  50.6 8.1 %collective-permute-start.3 = (bf16[64,2176]{1,0:T(8,128)(2,1)}, bf16[64,2176]{1,0:T(8,128)(2,1)S(1)}, u32[]{:S(2)}, u32[]{:S(2)}) collective-permute-start(bf16[64,2176]{1,0:T(8,128)(2,1)} %get-tuple-element.27), channel_id=1, source_target_pairs={{0,96},{1,97},{2,98},{3,99},{4,100},{5,101},{6,102},{7,103},{8,104... | collective-permute-start | bytes 835592 | tf_op jit(solution)/shard_map/ppermute | solution.py:93
  51.1 9.1 %collective-permute-start.2 = (bf16[64,2176]{1,0:T(8,128)(2,1)S(1)}, bf16[64,2176]{1,0:T(8,128)(2,1)S(1)}, u32[]{:S(2)}, u32[]{:S(2)}) collective-permute-start(bf16[64,2176]{1,0:T(8,128)(2,1)S(1)} %get-tuple-element.28), channel_id=1, source_target_pairs={{0,64},{1,65},{2,66},{3,67},{4,68},{5,69},{6,70},{7,71},{8,72},{9,... | collective-permute-start | bytes 835592 | tf_op jit(solution)/shard_map/ppermute | solution.py:93
  52.3 14.9 %collective-permute-start.1 = (bf16[64,2176]{1,0:T(8,128)(2,1)S(1)}, bf16[64,2176]{1,0:T(8,128)(2,1)S(1)}, u32[]{:S(2)}, u32[]{:S(2)}) collective-permute-start(bf16[64,2176]{1,0:T(8,128)(2,1)S(1)} %get-tuple-element.26), channel_id=1, source_target_pairs={{0,32},{1,33},{2,34},{3,35},{4,36},{5,37},{6,38},{7,39},{8,40},{9,... | collective-permute-start | bytes 835592 | tf_op jit(solution)/shard_map/ppermute | solution.py:93
  69.5 26.8 %all-to-all-start.1 = ((bf16[32,16,640]{2,1,0:T(8,128)(2,1)}), bf16[32,16,640]{2,1,0:T(8,128)(2,1)S(1)}, u32[]{:S(2)}, u32[]{:S(2)}) async-start(bf16[32,16,640]{2,1,0:T(8,128)(2,1)} %fusion.10), calls=%async_computation.1 | async-start | bytes 1310720 | tf_op jit(solution)/shard_map/all_to_all | solution.py:99
  97.7 17.1 %collective-permute-start.8 = (bf16[64,2048]{1,0:T(8,128)(2,1)S(1)}, bf16[64,2048]{1,0:T(8,128)(2,1)}, u32[]{:S(2)}, u32[]{:S(2)}) collective-permute-start(bf16[64,2048]{1,0:T(8,128)(2,1)S(1)} %reshape.214), channel_id=1, source_target_pairs={{0,96},{1,97},{2,98},{3,99},{4,100},{5,101},{6,102},{7,103},{8,104... | collective-permute-start | bytes 786440 | tf_op jit(solution)/shard_map/ppermute | solution.py:119
  97.8 17.0 %collective-permute-start.9 = (bf16[64,2048]{1,0:T(8,128)(2,1)S(1)}, bf16[64,2048]{1,0:T(8,128)(2,1)S(1)}, u32[]{:S(2)}, u32[]{:S(2)}) collective-permute-start(bf16[64,2048]{1,0:T(8,128)(2,1)S(1)} %reshape.214), channel_id=1, source_target_pairs={{0,64},{1,65},{2,66},{3,67},{4,68},{5,69},{6,70},{7,71},{8,72},{9,... | collective-permute-start | bytes 786440 | tf_op jit(solution)/shard_map/ppermute | solution.py:119
  99.1 15.7 %collective-permute-start.10 = (bf16[64,2048]{1,0:T(8,128)(2,1)S(1)}, bf16[64,2048]{1,0:T(8,128)(2,1)S(1)}, u32[]{:S(2)}, u32[]{:S(2)}) collective-permute-start(bf16[64,2048]{1,0:T(8,128)(2,1)S(1)} %reshape.214), channel_id=1, source_target_pairs={{0,32},{1,33},{2,34},{3,35},{4,36},{5,37},{6,38},{7,39},{8,40},{9,... | collective-permute-start | bytes 786440 | tf_op jit(solution)/shard_map/ppermute | solution.py:119
  105.3 17.1 %all-to-all-start.2 = ((bf16[32,16,384]{2,1,0:T(8,128)(2,1)}), bf16[32,16,384]{2,1,0:T(8,128)(2,1)S(1)}, u32[]{:S(2)}, u32[]{:S(2)}) async-start(bf16[32,16,384]{2,1,0:T(8,128)(2,1)} %broadcast_in_dim.17), calls=%async_computation.2 | async-start | bytes 786432 | tf_op jit(solution)/shard_map/all_to_all | solution.py:115
  116.8 24.8 %collective-permute-start.11 = (bf16[256,2048]{1,0:T(8,128)(2,1)}, bf16[256,2048]{1,0:T(8,128)(2,1)}, u32[]{:S(2)}, u32[]{:S(2)}) collective-permute-start(bf16[256,2048]{1,0:T(8,128)(2,1)} %pad_maximum_fusion.1), channel_id=1, source_target_pairs={{0,1},{1,0},{2,3},{3,2},{4,5},{5,4},{6,7},{7,6},{8,9},{9,8},{10,11... | collective-permute-start | bytes 3145736 | tf_op jit(solution)/shard_map/ppermute | solution.py:121
  122.6 9.0 %collective-permute-start.4 = (bf16[64,2176]{1,0:T(8,128)(2,1)S(1)}, bf16[64,2176]{1,0:T(8,128)(2,1)S(1)}, u32[]{:S(2)}, u32[]{:S(2)}) collective-permute-start(bf16[64,2176]{1,0:T(8,128)(2,1)S(1)} %get-tuple-element.29), channel_id=1, source_target_pairs={{0,96},{1,97},{2,98},{3,99},{4,100},{5,101},{6,102},{7,103},{8,104... | collective-permute-start | bytes 835592 | tf_op jit(solution)/shard_map/ppermute | solution.py:119
  124.7 7.0 %collective-permute-start.5 = (bf16[64,2176]{1,0:T(8,128)(2,1)S(1)}, bf16[64,2176]{1,0:T(8,128)(2,1)S(1)}, u32[]{:S(2)}, u32[]{:S(2)}) collective-permute-start(bf16[64,2176]{1,0:T(8,128)(2,1)S(1)} %get-tuple-element.29), channel_id=1, source_target_pairs={{0,64},{1,65},{2,66},{3,67},{4,68},{5,69},{6,70},{7,71},{8,72},{9,... | collective-permute-start | bytes 835592 | tf_op jit(solution)/shard_map/ppermute | solution.py:119
  125.8 9.6 %collective-permute-start.6 = (bf16[64,2176]{1,0:T(8,128)(2,1)S(1)}, bf16[64,2176]{1,0:T(8,128)(2,1)S(1)}, u32[]{:S(2)}, u32[]{:S(2)}) collective-permute-start(bf16[64,2176]{1,0:T(8,128)(2,1)S(1)} %get-tuple-element.29), channel_id=1, source_target_pairs={{0,32},{1,33},{2,34},{3,35},{4,36},{5,37},{6,38},{7,39},{8,40},{9,... | collective-permute-start | bytes 835592 | tf_op jit(solution)/shard_map/ppermute | solution.py:119
  135.5 8.4 %collective-permute-start.7 = (bf16[256,2176]{1,0:T(8,128)(2,1)S(1)}, bf16[256,2176]{1,0:T(8,128)(2,1)S(1)}, u32[]{:S(2)}, u32[]{:S(2)}) collective-permute-start(bf16[256,2176]{1,0:T(8,128)(2,1)S(1)} %pad_maximum_fusion), channel_id=1, source_target_pairs={{0,1},{1,0},{2,3},{3,2},{4,5},{5,4},{6,7},{7,6},{8,9},{9,8},{10,11... | collective-permute-start | bytes 3342344 | tf_op jit(solution)/shard_map/ppermute | solution.py:121
  141.6 2.5 %copy-start.10 = (s32[512]{0:T(512)S(1)}, s32[512]{0:T(512)}, u32[]{:S(2)}) copy-start(s32[512]{0:T(512)} %copy-done.9) | copy-start | bytes 6148
  144.0 4.4 %copy-start.2 = (f32[2,2048]{1,0:T(2,128)S(1)}, f32[2,2048]{1,0:T(2,128)}, u32[]{:S(2)}) copy-start(f32[2,2048]{1,0:T(2,128)} %reshape.210) | copy-start | bytes 49156
  144.0 4.4 %copy-start.4 = (f32[2,2048]{1,0:T(2,128)S(1)}, f32[2,2048]{1,0:T(2,128)}, u32[]{:S(2)}) copy-start(f32[2,2048]{1,0:T(2,128)} %param.14) | copy-start | bytes 49156
  144.1 1.4 copy-start.5
  149.0 4.9 %copy-start.7 = (f32[2,8]{1,0:T(2,128)S(1)}, f32[2,8]{1,0:T(2,128)}, u32[]{:S(2)}) copy-start(f32[2,8]{1,0:T(2,128)} %param.15) | copy-start | bytes 196
  149.0 4.9 %copy-start.8 = (f32[2,8]{1,0:T(2,128)S(1)}, f32[2,8]{1,0:T(2,128)}, u32[]{:S(2)}) copy-start(f32[2,8]{1,0:T(2,128)} %get-tuple-element.45) | copy-start | bytes 196

commit v2 on v1

v2 whole, which is shorter than its diff:
```python
import functools

import jax
import jax.numpy as jnp
from jax import lax
from jax.experimental import pallas as pl
from jax.experimental.pallas import tpu as pltpu
from jax.sharding import Mesh, PartitionSpec as P

eps_norm = 1e-05
momentum_rate = 0.9
learn_rate = 4.0
trust_coef = 0.001
decay_rate = 5e-05

AXES = ("zh", "x", "zl", "y", "c")
SIZES = (2, 4, 4, 4, 2)
GX = ("zh", "x")
XY = ("x", "y")
Z = ("zh", "zl")
BF = jnp.bfloat16
F32 = jnp.float32

ROWS = 392
CB = 512
C = 2048
EXT = 128
WIDE = C + EXT
PIECE = 2 * C + 2 * EXT
COLS = 512
STEPS = C // COLS
COUNT = float(ROWS * 8)
VMEM_BYTES = 24 * 1024 * 1024
VMEM_ALL = 60 * 1024 * 1024


def sibling_pairs():
    return [(i, i ^ 1) for i in range(256)]


def natural_row(t, c):
    cc = c ^ (t >> 8)
    return (
        ((t >> 3) & 1) * 256
        + ((t >> 6) & 3) * 64
        + ((t >> 1) & 3) * 16
        + ((t >> 4) & 3) * 4
        + cc * 2
        + (t & 1)
    )


def hi_lo(v):
    hi = v.astype(BF).astype(F32)
    return hi, v - hi


def params(limit=VMEM_BYTES):
    return pltpu.CompilerParams(vmem_limit_bytes=limit)


ANY = pl.BlockSpec(memory_space=pl.ANY)
VMEM = pl.BlockSpec(memory_space=pltpu.VMEM)
SMEM = pl.BlockSpec(memory_space=pltpu.SMEM)
DMA = pltpu.SemaphoreType.DMA


def copy(src, dst, sem):
    made = pltpu.make_async_copy(src, dst, sem)
    made.start()
    return made


def cols(j):
    return pl.ds(j * COLS, COLS)


def own_block(row, mine):
    block = jnp.zeros((2, EXT), F32)
    for q in range(16):
        block = jnp.where((mine >> 4) == q, row[:, EXT * q : EXT * q + EXT], block)
    return block


def stats_kernel(
    mine_ref, f_any, w_any, cot_any, pre_any, m_any, v_any, bn_any, bnm_any,
    up_any, stat_ref, base_ref,
    f, w, cot, pre, up, master, momentum, bn, bnm, sems,
):
    mine = mine_ref[0]
    first = copy(f_any, f, sems.at[0, STEPS])
    loads = []
    for j in range(STEPS):
        loads.append(
            [
                copy(w_any.at[:, cols(j)], w.at[:, cols(j)], sems.at[0, j]),
                copy(cot_any.at[:, cols(j)], cot.at[:, cols(j)], sems.at[1, j]),
                copy(pre_any.at[:, cols(j)], pre.at[:, cols(j)], sems.at[2, j]),
            ]
        )
    small = [
        copy(m_any, master, sems.at[1, STEPS]),
        copy(v_any, momentum, sems.at[2, STEPS]),
        copy(bn_any, bn, sems.at[3, STEPS]),
        copy(bnm_any, bnm, sems.at[4, 0]),
    ]
    first.wait()
    stores = []
    for j in range(STEPS):
        loads[j][0].wait()
        conv = jnp.dot(f[...], w[:, cols(j)], preferred_element_type=F32)
        loads[j][1].wait()
        loads[j][2].wait()
        u = jnp.where(pre[:, cols(j)].astype(F32) > 0, cot[:, cols(j)].astype(F32), 0.0)
        up[:, cols(j)] = u.astype(BF)
        stores.append(copy(up.at[:, cols(j)], up_any.at[:, cols(j)], sems.at[3, j]))
        stat = jnp.concatenate(
            [
                jnp.sum(conv, axis=0, keepdims=True),
                jnp.sum(conv * conv, axis=0, keepdims=True),
                jnp.sum(u, axis=0, keepdims=True),
                jnp.sum(u * conv, axis=0, keepdims=True),
            ],
            axis=0,
        )
        stat_ref[:, :, cols(j)] = jnp.broadcast_to(stat[None], (8, 4, COLS))
    for load in small:
        load.wait()
    base_ref[:, 0:C] = master[...] - momentum_rate * momentum[...]
    base_ref[:, C : 2 * C] = master[...]
    own_bn = own_block(bn[...], mine)
    lane = lax.broadcasted_iota(jnp.int32, (2, EXT), 1)
    bn_base = own_bn - momentum_rate * jnp.concatenate([bnm[...]] * 16, axis=1)
    base_ref[:, 2 * C : 2 * C + EXT] = jnp.where((lane >> 3) == (mine & 15), bn_base, 0.0)
    square = jnp.sum(master[...] * master[...], axis=(0, 1), keepdims=True)
    row = lax.broadcasted_iota(jnp.int32, (2, EXT), 0)
    base_ref[:, 2 * C + EXT :] = jnp.where((row == 0) & (lane == 0), square, 0.0)
    for store in stores:
        store.wait()


def stats_call(mine, features, weight, cotangent, pre_act, master, momentum, bn_params, bn_momentum):
    return pl.pallas_call(
        stats_kernel,
        in_specs=[SMEM] + [ANY] * 8,
        out_specs=[ANY, VMEM, VMEM],
        out_shape=[
            jax.ShapeDtypeStruct((ROWS, C), BF),
            jax.ShapeDtypeStruct((8, 4, C), F32),
            jax.ShapeDtypeStruct((2, PIECE), F32),
        ],
        scratch_shapes=[
            pltpu.VMEM((ROWS, CB), BF),
            pltpu.VMEM((CB, C), BF),
            pltpu.VMEM((ROWS, C), BF),
            pltpu.VMEM((ROWS, C), BF),
            pltpu.VMEM((ROWS, C), BF),
            pltpu.VMEM((2, C), F32),
            pltpu.VMEM((2, C), F32),
            pltpu.VMEM((2, C), F32),
            pltpu.VMEM((2, 8), F32),
            DMA((5, STEPS + 1)),
        ],
        compiler_params=params(VMEM_ALL),
        cost_estimate=pl.CostEstimate(flops=2 * ROWS * CB * C, bytes_accessed=7500000, transcendentals=0),
        name="stats",
    )(mine, features, weight, cotangent, pre_act, master, momentum, bn_params, bn_momentum)


def grad_kernel(
    c_ref, stat_any, f_any, w_any, up_any, bn_any, p1, p2, p3, p4, p5, p6, p7,
    gc_any, send_any, own_any, own_ext_ref,
    stat, bn, f, w, up, gc, send, own, ft, ext_send, ext_own, sems,
):
    c = c_ref[0]
    early = [copy(stat_any, stat, sems.at[3, STEPS]), copy(bn_any, bn, sems.at[4, STEPS])]
    first = copy(f_any, f, sems.at[0, STEPS])
    loads = []
    for j in range(STEPS):
        loads.append(
            [
                copy(w_any.at[:, cols(j)], w.at[:, cols(j)], sems.at[0, j]),
                copy(up_any.at[:, cols(j)], up.at[:, cols(j)], sems.at[1, j]),
            ]
        )
    t = lax.broadcasted_iota(jnp.int32, (CB, CB), 0)
    r = lax.broadcasted_iota(jnp.int32, (CB, CB), 1)
    sel = jnp.where(r == natural_row(t, c), 1.0, 0.0).astype(BF)
    for load in early:
        load.wait()
    sums = jnp.sum(stat[...], axis=0)
    mean = sums[0:1] / COUNT
    inv_std = lax.rsqrt(sums[1:2] / COUNT - mean * mean + eps_norm)
    sum_b = sums[2:3]
    sum_g = inv_std * (sums[3:4] - mean * sum_b)
    alpha = bn[0:1] * inv_std
    slope = alpha * inv_std * (sum_g / COUNT)
    shift = sum_b / COUNT
    scale_row = sum_g * 0.125
    shift_row = sum_b * 0.125
    mine = jnp.where(c == 0, scale_row, shift_row)
    other = jnp.where(c == 0, shift_row, scale_row)
    ext_send[...] = jnp.zeros_like(ext_send)
    ext_own[...] = jnp.zeros_like(ext_own)
    for q in range(16):
        ext_own[16 * q : 16 * q + 1, :] = mine[:, 128 * q : 128 * q + 128]
        ext_send[16 * q : 16 * q + 1, :] = other[:, 128 * q : 128 * q + 128]
    own_ext_ref[...] = ext_own[...]
    send[:, C:] = ext_send[...].astype(BF)
    stores = [copy(send.at[:, pl.ds(C, EXT)], send_any.at[:, pl.ds(C, EXT)], sems.at[2, STEPS])]
    first.wait()
    ft[...] = lax.dot_general(sel, f[...], (((1,), (1,)), ((), ())), preferred_element_type=F32).astype(BF)
    for j in range(STEPS):
        at = slice(j * COLS, j * COLS + COLS)
        loads[j][0].wait()
        conv = jnp.dot(f[...], w[:, at], preferred_element_type=F32)
        loads[j][1].wait()
        grad = alpha[:, at] * (up[:, at].astype(F32) - shift[:, at]) - (conv - mean[:, at]) * slope[:, at]
        grad = grad.astype(BF)
        gc[:, at] = grad
        stores.append(copy(gc.at[:, cols(j)], gc_any.at[:, cols(j)], sems.at[3, j]))
        g = jnp.dot(ft[...], grad, preferred_element_type=F32)
        send[:, at] = g[CB // 2 :].astype(BF)
        stores.append(copy(send.at[:, cols(j)], send_any.at[:, cols(j)], sems.at[2, j]))
        own[:, at] = g[: CB // 2]
        stores.append(copy(own.at[:, cols(j)], own_any.at[:, cols(j)], sems.at[4, j]))
    for store in stores:
        store.wait()


def grad_call(c, stats, features, weight, up, bn_params, pieces):
    return pl.pallas_call(
        grad_kernel,
        in_specs=[SMEM] + [ANY] * 12,
        out_specs=[ANY, ANY, ANY, VMEM],
        out_shape=[
            jax.ShapeDtypeStruct((ROWS, C), BF),
            jax.ShapeDtypeStruct((CB // 2, WIDE), BF),
            jax.ShapeDtypeStruct((CB // 2, C), F32),
            jax.ShapeDtypeStruct((CB // 2, EXT), F32),
        ],
        scratch_shapes=[
            pltpu.VMEM((8, 4, C), F32),
            pltpu.VMEM((2, C), F32),
            pltpu.VMEM((ROWS, CB), BF),
            pltpu.VMEM((CB, C), BF),
            pltpu.VMEM((ROWS, C), BF),
            pltpu.VMEM((ROWS, C), BF),
            pltpu.VMEM((CB // 2, WIDE), BF),
            pltpu.VMEM((CB // 2, C), F32),
            pltpu.VMEM((CB, ROWS), BF),
            pltpu.VMEM((CB // 2, EXT), F32),
            pltpu.VMEM((CB // 2, EXT), F32),
            DMA((5, STEPS + 1)),
        ],
        compiler_params=params(VMEM_ALL),
        cost_estimate=pl.CostEstimate(flops=4 * ROWS * CB * C, bytes_accessed=9000000, transcendentals=0),
        name="grad",
    )(c, stats, features, weight, up, bn_params, *pieces)


def input_kernel(
    z_ref, gc_any, w_any, p0, p1, p2, p3, p4, p5, p6, p7, out_ref, base_ref, rows_ref, sq_ref,
    gc, w, parts, pieces, sems
):
    rows = [copy(p, parts.at[k], sems.at[2, k]) for k, p in enumerate((p0, p1, p2, p3, p4, p5, p6, p7))]
    loads = []
    for j in range(STEPS):
        loads.append(
            [
                copy(gc_any.at[:, cols(j)], gc.at[:, cols(j)], sems.at[0, j]),
                copy(w_any.at[:, cols(j)], w.at[:, cols(j)], sems.at[1, j]),
            ]
        )
    for load in rows:
        load.wait()
    for k in range(8):
        pieces[2 * k : 2 * k + 2, :] = parts[k]
    got = pltpu.roll(pieces[...], 2 * z_ref[0], 0)
    base_ref[:, :C] = got[:, :C].astype(BF)
    base_ref[:, C:] = got[:, 2 * C : 2 * C + EXT].astype(BF)
    rows_ref[...] = got[:, C : 2 * C]
    sq_ref[...] = jnp.sum(got[:, 2 * C + EXT :], axis=(0, 1), keepdims=True)
    total = None
    for j in range(STEPS):
        loads[j][0].wait()
        loads[j][1].wait()
        part = lax.dot_general(
            gc[:, cols(j)], w[:, cols(j)], (((1,), (1,)), ((), ())), preferred_element_type=F32
        )
        total = part if total is None else total + part
    out_ref[...] = total.astype(BF)


def input_call(z, gc, weight, pieces):
    return pl.pallas_call(
        input_kernel,
        in_specs=[SMEM] + [ANY] * 10,
        out_specs=[VMEM] * 4,
        out_shape=[
            jax.ShapeDtypeStruct((ROWS, CB), BF),
            jax.ShapeDtypeStruct((16, WIDE), BF),
            jax.ShapeDtypeStruct((16, C), F32),
            jax.ShapeDtypeStruct((1, 1), F32),
        ],
        scratch_shapes=[
            pltpu.VMEM((ROWS, C), BF),
            pltpu.VMEM((CB, C), BF),
            pltpu.VMEM((8, 2, PIECE), F32),
            pltpu.VMEM((16, PIECE), F32),
            DMA((3, 8)),
        ],
        compiler_params=params(VMEM_ALL),
        cost_estimate=pl.CostEstimate(flops=2 * ROWS * CB * C, bytes_accessed=4000000, transcendentals=0),
        name="ginput",
    )(z, gc, weight, *pieces)


def pair_kernel(own_any, ext_ref, got_any, after_any, out_any, own, got, out, sems):
    rows = [pl.ds(64 * i, 64) for i in range(4)]
    loads = []
    for i in range(4):
        loads.append(
            [
                copy(own_any.at[rows[i]], own.at[rows[i]], sems.at[0, i]),
                copy(got_any.at[rows[i]], got.at[rows[i]], sems.at[1, i]),
            ]
        )
    stores = []
    for i in range(4):
        loads[i][0].wait()
        loads[i][1].wait()
        out[rows[i], :C] = (own[rows[i]] + got[rows[i], :C].astype(F32)).astype(BF)
        out[rows[i], C:] = (ext_ref[rows[i]] + got[rows[i], C:].astype(F32)).astype(BF)
        stores.append(copy(out.at[rows[i]], out_any.at[rows[i]], sems.at[2, i]))
    for store in stores:
        store.wait()


def pair_call(own, ext, got, after):
    return pl.pallas_call(
        pair_kernel,
        in_specs=[ANY, VMEM, ANY, ANY],
        out_specs=ANY,
        out_shape=jax.ShapeDtypeStruct((256, WIDE), BF),
        scratch_shapes=[
            pltpu.VMEM((256, C), F32),
            pltpu.VMEM((256, WIDE), BF),
            pltpu.VMEM((256, WIDE), BF),
            DMA((3, 4)),
        ],
        compiler_params=params(VMEM_ALL),
        cost_estimate=pl.CostEstimate(flops=256 * WIDE, bytes_accessed=4500000, transcendentals=0),
        name="pair",
    )(own, ext, got, after)


def plane_kernel(x_ref, got_any, b0, b1, b2, b3, out_any, base_any, got, out, sems):
    loads = [copy(got_any.at[pl.ds(4 * i, 4)], got.at[pl.ds(4 * i, 4)], sems.at[0, i]) for i in range(4)]
    stores = []
    for k, block in enumerate((b0, b1, b2, b3)):
        stores.append(copy(block, base_any.at[(x_ref[0] + k) & 3], sems.at[2, k]))
    total = None
    for i in range(4):
        loads[i].wait()
        part = jnp.sum(got[4 * i : 4 * i + 4].astype(F32), axis=0)
        total = part if total is None else total + part
    out[...] = total.astype(BF)
    stores += [copy(out, out_any.at[k], sems.at[1, k]) for k in range(8)]
    for store in stores:
        store.wait()


def plane_call(x, got, bases):
    return pl.pallas_call(
        plane_kernel,
        in_specs=[SMEM] + [ANY] * 5,
        out_specs=[ANY, ANY],
        out_shape=[jax.ShapeDtypeStruct((8, 16, WIDE), BF), jax.ShapeDtypeStruct((4, 16, WIDE), BF)],
        scratch_shapes=[pltpu.VMEM((16, 16, WIDE), BF), pltpu.VMEM((16, WIDE), BF), DMA((3, 8))],
        compiler_params=params(),
        cost_estimate=pl.CostEstimate(flops=256 * WIDE, bytes_accessed=1700000, transcendentals=0),
        name="plane",
    )(x, got, *bases)


def column_kernel(z_ref, got_ref, w_ref, sq_ref, b1, b2, b3, out_any, own_ref, send, sems):
    z = z_ref[0]
    total = jnp.sum(got_ref[...].astype(F32), axis=0)
    g = total[:, :C]
    w_hi, w_lo = hi_lo(sq_ref[...])
    g_hi, g_lo = hi_lo(jnp.sum(g * g, axis=(0, 1), keepdims=True))
    row = lax.broadcasted_iota(jnp.int32, (16, EXT), 0)
    lane = lax.broadcasted_iota(jnp.int32, (16, EXT), 1)
    bn_hi, bn_lo = hi_lo(total[0:1, C:])
    ext = jnp.where(row == 0, bn_hi, jnp.where(row == 1, bn_lo, 0.0))
    for k, value in enumerate((g_hi, g_lo, w_hi, w_lo)):
        ext = jnp.where((row == 2) & (lane == k), value, ext)
    send[:, :C] = (g + decay_rate * w_ref[...]).astype(BF)
    send[:, C:] = ext.astype(BF)
    stores = [copy(send, out_any.at[k], sems.at[k]) for k in range(16)]
    own_ref[...] = pltpu.roll(g, (16 - 2 * z) & 15, 0)[0:2]
    for store in stores:
        store.wait()


def column_call(z, got, w_rows, w_sq, bases):
    return pl.pallas_call(
        column_kernel,
        in_specs=[SMEM] + [VMEM] * 3 + [ANY] * 3,
        out_specs=[ANY, VMEM],
        out_shape=[
            jax.ShapeDtypeStruct((16, 16, WIDE), BF),
            jax.ShapeDtypeStruct((2, C), F32),
        ],
        scratch_shapes=[pltpu.VMEM((16, WIDE), BF), DMA((16,))],
        compiler_params=params(),
        cost_estimate=pl.CostEstimate(flops=128 * WIDE, bytes_accessed=1700000, transcendentals=0),
        name="column",
    )(z, got, w_rows, w_sq, *bases)


def basis_kernel(y_ref, b0, b1, b2, b3, after_any, base_any, sems):
    stores = []
    for k, block in enumerate((b0, b1, b2, b3)):
        for x in range(4):
            stores.append(copy(block.at[x], base_any.at[4 * x + ((y_ref[0] + k) & 3)], sems.at[4 * k + x]))
    for store in stores:
        store.wait()


def basis_call(y, bases, after):
    return pl.pallas_call(
        basis_kernel,
        in_specs=[SMEM] + [ANY] * 5,
        out_specs=ANY,
        out_shape=jax.ShapeDtypeStruct((16, 16, WIDE), BF),
        scratch_shapes=[DMA((16,))],
        compiler_params=params(),
        cost_estimate=pl.CostEstimate(flops=0, bytes_accessed=2200000, transcendentals=0),
        name="basis",
    )(y, *bases, after)


def update_kernel(
    at_ref, b0_any, b1_any, a0_any, a1_any, bn_any, g_any, m_any, v_any, bnm_any,
    nw_any, nbn_ref, nm_ref, nv_ref, nbm_ref, nbv_ref,
    b0, b1, a0, a1, nw, bn_v, g_v, m_v, v_v, bnm_v, sems,
):
    c = at_ref[0]
    mine = at_ref[1]
    last = pl.ds(C, EXT)
    main = pl.ds(0, C)
    big = ((b0_any, b0), (b1_any, b1), (a0_any, a0), (a1_any, a1))
    ends = [copy(src.at[:, last], dst.at[:, last], sems.at[4, k]) for k, (src, dst) in enumerate(big)]
    rows = [pl.ds(64 * i, 64) for i in range(4)]
    loads = []
    for i in range(4):
        loads.append(
            [copy(src.at[rows[i], main], dst.at[rows[i], main], sems.at[k, i]) for k, (src, dst) in enumerate(big)]
        )
    small = [
        copy(bn_any, bn_v, sems.at[7, 0]),
        copy(g_any, g_v, sems.at[7, 1]),
        copy(m_any, m_v, sems.at[7, 2]),
        copy(v_any, v_v, sems.at[7, 3]),
        copy(bnm_any, bnm_v, sems.at[8, 0]),
    ]
    r = lax.broadcasted_iota(jnp.int32, (128, 128), 0)
    t = lax.broadcasted_iota(jnp.int32, (128, 128), 1)
    want = (
        ((t >> 3) & 1) * 64 + ((t >> 1) & 3) * 16 + ((t >> 4) & 3) * 4 + (c ^ (t >> 6)) * 2 + (t & 1)
    )
    sel = jnp.where(r == want, 1.0, 0.0).astype(BF)

    for end in ends:
        end.wait()
    e0 = b0[:, C:].astype(F32)
    e1 = b1[:, C:].astype(F32)
    row = lax.broadcasted_iota(jnp.int32, (256, EXT), 0) & 15
    lane = lax.broadcasted_iota(jnp.int32, (256, EXT), 1)
    both = jnp.where(row == 2, e0 + e1, 0.0)
    g_sq = jnp.sum(jnp.where(lane < 2, both, 0.0), axis=(0, 1), keepdims=True)
    w_sq = jnp.sum(jnp.where((lane == 2) | (lane == 3), both, 0.0), axis=(0, 1), keepdims=True)

    def rate_of(w_sq, g_sq):
        w_norm = jnp.sqrt(w_sq)
        return learn_rate * (trust_coef * w_norm / (jnp.sqrt(g_sq) + decay_rate * w_norm))

    rate = rate_of(w_sq, g_sq)
    stores = []
    for i in range(4):
        for load in loads[i]:
            load.wait()
        at = slice(64 * i, 64 * i + 64)
        new = jnp.concatenate(
            [
                (a0[at, :C].astype(F32) - rate * b0[at, :C].astype(F32)).astype(BF),
                (a1[at, :C].astype(F32) - rate * b1[at, :C].astype(F32)).astype(BF),
            ],
            axis=0,
        )
        new = jnp.dot(sel, new, preferred_element_type=F32).astype(BF)
        nw[at, :] = new[:64]
        nw[slice(256 + 64 * i, 320 + 64 * i), :] = new[64:]
        stores.append(copy(nw.at[rows[i]], nw_any.at[rows[i]], sems.at[5, i]))
        far_rows = pl.ds(256 + 64 * i, 64)
        stores.append(copy(nw.at[far_rows], nw_any.at[far_rows], sems.at[6, i]))

    def flat(e):
        return jnp.concatenate([e[16 * q : 16 * q + 1] + e[16 * q + 1 : 16 * q + 2] for q in range(16)], axis=1)

    near, far = flat(e0), flat(e1)
    bn_grad = jnp.concatenate([jnp.where(c == 0, near, far), jnp.where(c == 0, far, near)], axis=0)
    for load in small:
        load.wait()
    bn = bn_v[...]
    bn_rate = rate_of(
        jnp.sum(bn * bn, axis=1, keepdims=True), jnp.sum(bn_grad * bn_grad, axis=1, keepdims=True)
    )
    ends_a = a0[:, C:].astype(F32) + a1[:, C:].astype(F32)
    blocks = [None] * 16
    for x in range(4):
        rows_x = ends_a[64 * x : 64 * x + 16]
        for y in range(1, 4):
            rows_x = rows_x + ends_a[64 * x + 16 * y : 64 * x + 16 * y + 16]
        for high in range(2):
            for half in range(2):
                top = 8 * high + 4 * half
                blocks[8 * high + 2 * x + half] = rows_x[top : top + 2] + rows_x[top + 2 : top + 4]
    bn_base = jnp.concatenate(blocks, axis=1)
    nbn_ref[...] = (bn_base - bn_rate * (bn_grad + decay_rate * bn)).astype(BF)
    master = m_v[...]
    new_v = momentum_rate * v_v[...] + rate * (g_v[...] + decay_rate * master)
    nv_ref[...] = new_v
    nm_ref[...] = master - new_v
    lane = lax.broadcasted_iota(jnp.int32, (2, EXT), 1)

    def own_eight(row):
        kept = jnp.where((lane >> 3) == (mine & 15), own_block(row, mine), 0.0)
        eight = kept[:, 0:8]
        for s in range(1, 16):
            eight = eight + kept[:, 8 * s : 8 * s + 8]
        return eight

    own_bn = own_eight(bn)
    new_bnv = momentum_rate * bnm_v[...] + bn_rate * (own_eight(bn_grad) + decay_rate * own_bn)
    nbv_ref[...] = new_bnv
    nbm_ref[...] = own_bn - new_bnv
    for store in stores:
        store.wait()


def update_call(at, b0, b1, a0, a1, bn_params, g_own, master, momentum, bn_momentum):
    small = [jax.ShapeDtypeStruct((2, C), F32)] * 2 + [jax.ShapeDtypeStruct((2, 8), F32)] * 2
    return pl.pallas_call(
        update_kernel,
        in_specs=[SMEM] + [ANY] * 4 + [ANY] * 5,
        out_specs=[ANY] + [VMEM] * 5,
        out_shape=[jax.ShapeDtypeStruct((CB, C), BF), jax.ShapeDtypeStruct((2, C), BF)] + small,
        scratch_shapes=[pltpu.VMEM((256, WIDE), BF)] * 4
        + [pltpu.VMEM((CB, C), BF)]
        + [pltpu.VMEM((2, C), F32)] * 4
        + [pltpu.VMEM((2, 8), F32), DMA((9, 4))],
        compiler_params=params(),
        cost_estimate=pl.CostEstimate(flops=2 * CB * 128 * C, bytes_accessed=6500000, transcendentals=0),
        name="update",
    )(at, b0, b1, a0, a1, bn_params, g_own, master, momentum, bn_momentum)


def exchange(block, axes):
    return lax.all_to_all(block, axes, 0, 0, tiled=True)


def shift_pairs(move):
    out = []
    for i in range(256):
        c, y, zl, x, zh = i & 1, (i >> 1) & 3, (i >> 3) & 3, (i >> 5) & 3, i >> 7
        x, y, z = move(x, y, 4 * zh + zl)
        out.append((i, ((((z >> 2) * 4 + x) * 4 + (z & 3)) * 4 + y) * 2 + c))
    return out


def ring(block, size, move):
    parts = [block]
    for k in range(1, size):
        parts.append(lax.ppermute(block, AXES, shift_pairs(functools.partial(move, size - k))))
    return parts


def number(*values):
    return jnp.stack(values).astype(jnp.int32)


def shards(features, weight, cotangent, pre_act, bn_params, master, momentum, bn_momentum):
    c, x, y, z = (lax.axis_index(axis) for axis in ("c", "x", "y", Z))
    mine = lax.axis_index(AXES)
    swap = functools.partial(lax.ppermute, axis_name=AXES, perm=sibling_pairs())

    up, stats, piece = stats_call(
        number(mine), features, weight, cotangent, pre_act, master, momentum, bn_params, bn_momentum
    )
    stats = exchange(stats, GX)
    pieces = ring(piece, 8, lambda k, x, y, z: (x, y, (z + k) % 8))
    gc, send, own, own_ext = grad_call(
        number(c), stats, features, weight, up, bn_params, pieces[1:]
    )
    grad_input, base, w_rows, w_sq = input_call(number(z), gc, weight, pieces)
    half = pair_call(own, own_ext, swap(send), grad_input)
    base, half = lax.optimization_barrier((base, half))
    bases = ring(base, 4, lambda k, x, y, z: ((x + k) % 4, y, z))
    part, base = plane_call(number(x), exchange(half.reshape(16, 16, WIDE), XY), bases)
    bases = ring(base, 4, lambda k, x, y, z: (x, (y + k) % 4, z))
    step, g_own = column_call(number(z), exchange(part, Z), w_rows, w_sq, bases[1:])
    a0 = basis_call(number(y), bases, step).reshape(256, WIDE)
    a1 = swap(a0)
    b0 = exchange(step, XY).reshape(256, WIDE)
    b1 = swap(b0)
    new_weight, new_bn, new_master, new_momentum, new_bn_master, new_bn_momentum = update_call(
        number(c, mine), b0, b1, a0, a1, bn_params, g_own, master, momentum, bn_momentum
    )
    return (grad_input, up, new_master, new_momentum, new_weight, new_bn_master, new_bn_momentum, new_bn)


def solution(mesh):
    fine = Mesh(mesh.devices.reshape(SIZES), AXES)
    rows = P(AXES, None)
    cols = P(None, AXES)
    return jax.shard_map(
        shards,
        mesh=fine,
        in_specs=(rows, P(), rows, rows, P(), rows, rows, cols),
        out_specs=(rows, rows, rows, rows, P(), cols, cols, P()),
        check_vma=False,
    )
```

time: 158 us -> 138 us (0.87)
  Pallas kernels: 0 us -> 29.5 us
  other arithmetic: 22.6 us -> 0.07 us
  matrix products: 19.7 us -> 0 us
  starting transfers between devices: 44 us -> 59.2 us
  local copies, waits for them, and re-layouts: 15.5 us -> 1.71 us
  waiting for transfers between devices: 54.1 us -> 46 us
    pallas_call x0 -> x8, Pallas kernels: none -> 29.5 us  [the longest x1 6.98 us: grad_call(): pl.pallas_call(grad_kernel, in_specs=[SMEM] + [ANY] * 12, out_specs=[ANY,...]
    dot_general x6 -> x0, matrix products: 19.7 us -> none  [the longest x1 5.72 us: shards(): conv = jnp.dot(features, weight, preferred_element_type=F32)]
    ppermute x12 -> x16, starting transfers between devices: 18.7 us -> 32.6 us  [the longest x13 24.7 us: ring(): lax.ppermute(block, AXES, shift_pairs(functools.partial(move, size - k)))]
    all_to_all x3 -> x4, waiting for transfers between devices: 29.5 us -> 16.8 us  [exchange(): return lax.all_to_all(block, axes, 0, 0, tiled=True)]
    convert_element_type x7 -> x0, other arithmetic: 8.29 us -> none  [the longest x1 4.5 us: shards(): (bn_params[0] * inv_std * (upf - sum_b / count - normed * sum_g / count))...]
    concatenate x6 -> x0, other arithmetic: 5.58 us -> none  [the longest x1 2.53 us: shards(): g = jnp.concatenate([g, jnp.pad(extra, ((0, 0), (0, 120)))], axis=1)]
    unnamed x33 -> x30, local copies, waits for them, and re-layouts: 6.59 us -> 1.71 us
    ppermute x12 -> x16, waiting for transfers between devices: 24.6 us -> 29.2 us  [the longest x13 26.9 us: ring(): lax.ppermute(block, AXES, shift_pairs(functools.partial(move, size - k)))]
  transfers between devices with their start and end apart: 15 -> 20, of which waited for: 10 -> 11; matrix products, arithmetic and copies ran while one was open for 11% -> 0% of each run, Pallas kernels for 0% -> 4%
where the time goes in v2:
time: 138 us
  starting transfers between devices  59.2 us (43%)
  waiting for transfers between devices  46 us (33%)
  Pallas kernels  29.5 us (21%)
  local copies, waits for them, and re-layouts  1.71 us (1%)
    ppermute x13, waiting for transfers between devices, ring(): lax.ppermute(block, AXES, shift_pairs(functools.partial(move, size - k)))  26.9 us
    all_to_all x4, starting transfers between devices, exchange(): return lax.all_to_all(block, axes, 0, 0, tiled=True)  26.6 us
    ppermute x13, starting transfers between devices, ring(): lax.ppermute(block, AXES, shift_pairs(functools.partial(move, size - k)))  24.7 us
    all_to_all x4, waiting for transfers between devices, exchange(): return lax.all_to_all(block, axes, 0, 0, tiled=True)  16.8 us
    pallas_call x1, Pallas kernels, grad_call(): pl.pallas_call(grad_kernel, in_specs=[SMEM] + [ANY] * 12, out_specs=[ANY,...  6.98 us
    pallas_call x1, Pallas kernels, stats_call(): pl.pallas_call(stats_kernel, in_specs=[SMEM] + [ANY] * 8, out_specs=[ANY,...  5.54 us
    pallas_call x1, Pallas kernels, update_call(): pl.pallas_call(update_kernel, in_specs=[SMEM] + [ANY] * 4 + [ANY] * 5, ou...  4.2 us
    ppermute x1, starting transfers between devices, shards(): half = pair_call(own, own_ext, swap(send), grad_input)  3.82 us
  transfers between devices with their start and end apart: 20, of which 11 were waited for; matrix products, arithmetic and copies ran while one was open for 0% of the time, Pallas kernels for 4%

profile of v2, /device:TPU:1, one launch (start us, length us, event | category | flops | bytes accessed | tf_op | source)
XLA Modules:
  0.0 137.6 jit_solution(3328962464014293295)
XLA Ops:
  0.7 5.5 %stats.1 = (bf16[392,2048]{1,0:T(8,128)(2,1)}, f32[8,4,2048]{2,1,0:T(4,128)}, f32[2,4352]{1,0:T(2,128)}) custom-call(s32[1]{0:T(128)} %bitcast.2.mine_ref, bf16[392,512]{1,0:T(8,128)(2,1)} %f_any.3, bf16[512,2048]{1,0:T(8,128)(2,1)} %w_any.5, bf16[392,2048]{1,0:T(8,128)(2,1)} %cot_any.1, bf16[392,2048]{1,0:T(8,128)(2,1)} %pre_any.1, f32[2,2048]{1,0:T(2,128)} %m_any.3, ...), custom_call_target="tpu_custom_call" | custom-call | flops 822083584 | bytes 7500000 | tf_op jit(solution)/shard_map/stats/pallas_call | solution.py:143
  6.2 11.5 %all-to-all-start = ((f32[8,4,2048]{2,1,0:T(4,128)}), f32[8,4,2048]{2,1,0:T(4,128)S(1)}, u32[]{:S(2)}, u32[]{:S(2)}) async-start(f32[8,4,2048]{2,1,0:T(4,128)} %get-tuple-element.31), calls=%async_computation | async-start | bytes 524288 | tf_op jit(solution)/shard_map/all_to_all | solution.py:572
  17.7 0.7 collective-permute-start.6
  18.4 1.2 collective-permute-start.5
  19.6 4.9 %collective-permute-start.4 = (f32[2,4352]{1,0:T(2,128)}, f32[2,4352]{1,0:T(2,128)S(1)}, u32[]{:S(2)}, u32[]{:S(2)}) collective-permute-start(f32[2,4352]{1,0:T(2,128)} %get-tuple-element.33.p0), channel_id=1, source_target_pairs={{0,24},{1,25},{2,26},{3,27},{4,28},{5,29},{6,30},{7,31},{8,128},{9... | collective-permute-start | bytes 104456 | tf_op jit(solution)/shard_map/ppermute | solution.py:587
  24.5 0.5 collective-permute-start.3
  25.0 4.5 %collective-permute-start.2 = (f32[2,4352]{1,0:T(2,128)}, f32[2,4352]{1,0:T(2,128)S(1)}, u32[]{:S(2)}, u32[]{:S(2)}) collective-permute-start(f32[2,4352]{1,0:T(2,128)} %get-tuple-element.33.p0), channel_id=1, source_target_pairs={{0,136},{1,137},{2,138},{3,139},{4,140},{5,141},{6,142},{7,143},{8... | collective-permute-start | bytes 104456 | tf_op jit(solution)/shard_map/ppermute | solution.py:587
  29.5 0.0 collective-permute-done.6.p7
  29.5 2.4 %collective-permute-start.1 = (f32[2,4352]{1,0:T(2,128)}, f32[2,4352]{1,0:T(2,128)S(1)}, u32[]{:S(2)}, u32[]{:S(2)}) collective-permute-start(f32[2,4352]{1,0:T(2,128)} %get-tuple-element.33.p0), channel_id=1, source_target_pairs={{0,144},{1,145},{2,146},{3,147},{4,148},{5,149},{6,150},{7,151},{8... | collective-permute-start | bytes 104456 | tf_op jit(solution)/shard_map/ppermute | solution.py:587
  31.9 0.0 collective-permute-done.5.p6
  31.9 0.7 collective-permute-start
  32.6 0.0 collective-permute-done.4.p5
  32.6 0.7 collective-permute-done.3.p4
  33.3 0.0 collective-permute-done.2.p3
  33.3 2.0 %collective-permute-done.1.p2 = f32[2,4352]{1,0:T(2,128)S(1)} collective-permute-done((f32[2,4352]{1,0:T(2,128)}, f32[2,4352]{1,0:T(2,128)S(1)}, u32[]{:S(2)}, u32[]{:S(2)}) %collective-permute-start.1) | collective-permute-done | bytes 34848 | tf_op jit(solution)/shard_map/ppermute | solution.py:587
  35.3 0.1 collective-permute-done.p1
  35.4 0.0 all-to-all-done.stat_any
  35.4 0.0 copy-done.9
  35.4 0.0 copy-done.10
  35.4 0.0 copy-done.11
  35.4 0.0 copy-done.12
  35.4 0.5 copy-done.13
  35.9 0.1 copy-done.14
  36.0 0.1 copy-done.7
  36.1 7.0 %grad.1 = (bf16[392,2048]{1,0:T(8,128)(2,1)}, bf16[256,2176]{1,0:T(8,128)(2,1)}, f32[256,2048]{1,0:T(8,128)}, f32[256,128]{1,0:T(8,128)}) custom-call(s32[1]{0:T(128)} %bitcast.1.c_ref, f32[8,4,2048]{2,1,0:T(4,128)} %copy-done.7, bf16[392,512]{1,0:T(8,128)(2,1)} %f_any.3, bf16[512,2048]{1,0:T(8,128)(2,1)} %w_any.5, ...), custom_call_target="tpu_custom_call" | custom-call | flops 1644167168 | bytes 9000000 | tf_op jit(solution)/shard_map/grad/pallas_call | solution.py:232
  43.1 3.8 %collective-permute-start.7 = (bf16[256,2176]{1,0:T(8,128)(2,1)}, bf16[256,2176]{1,0:T(8,128)(2,1)S(1)}, u32[]{:S(2)}, u32[]{:S(2)}) collective-permute-start(bf16[256,2176]{1,0:T(8,128)(2,1)} %get-tuple-element.39), channel_id=1, source_target_pairs={{0,1},{1,0},{2,3},{3,2},{4,5},{5,4},{6,7},{7,6},{8,9},{9,8},{10,11... | collective-permute-start | bytes 3342344 | tf_op jit(solution)/shard_map/ppermute | solution.py:609
  46.9 3.8 %ginput.1 = (bf16[392,512]{1,0:T(8,128)(2,1)}, bf16[16,2176]{1,0:T(8,128)(2,1)}, f32[16,2048]{1,0:T(8,128)}, f32[1,1]{1,0:T(1,128)}) custom-call(s32[1]{0:T(128)} %bitcast.z_ref, bf16[392,2048]{1,0:T(8,128)(2,1)} %get-tuple-element.34.gc_any, bf16[512,2048]{1,0:T(8,128)(2,1)} %w_any.5, f32[2,4352]{1,0:T(2,128)} %get-tuple-element.33.p0, ...), custom_call_target="tpu_custom_call" | custom-call | flops 822083584 | bytes 4000000 | tf_op jit(solution)/shard_map/ginput/pallas_call | solution.py:296
  50.7 0.0 collective-permute-done.7.got_any
  50.7 0.0 copy-start.6
  50.7 1.0 copy-done.6
  51.7 3.6 %pair.1 = bf16[256,2176]{1,0:T(8,128)(2,1)} custom-call(f32[256,2048]{1,0:T(8,128)} %get-tuple-element.37.own_any, f32[256,128]{1,0:T(8,128)} %get-tuple-element.38.ext_ref, bf16[256,2176]{1,0:T(8,128)(2,1)} %copy-done.6, bf16[392,512]{1,0:T(8,128)(2,1)} %get-tuple-element.23.after_any), custom_call_target="tpu_custom_call" | custom-call | flops 557056 | bytes 4500000 | tf_op jit(solution)/shard_map/pair/pallas_call | solution.py:341
  55.3 6.8 %all-to-all-start.1 = ((bf16[16,16,2176]{2,1,0:T(8,128)(2,1)}), bf16[16,16,2176]{2,1,0:T(8,128)(2,1)S(1)}, u32[]{:S(2)}, u32[]{:S(2)}) async-start(bf16[16,16,2176]{2,1,0:T(8,128)(2,1)} %bitcast.12), calls=%async_computation.1 | async-start | bytes 2228224 | tf_op jit(solution)/shard_map/all_to_all | solution.py:572
  62.2 0.0 copy-done.1
  62.2 1.4 %collective-permute-start.10 = (bf16[16,2176]{1,0:T(8,128)(2,1)S(1)}, bf16[16,2176]{1,0:T(8,128)(2,1)S(1)}, u32[]{:S(2)}, u32[]{:S(2)}) collective-permute-start(bf16[16,2176]{1,0:T(8,128)(2,1)S(1)} %copy-done.1), channel_id=1, source_target_pairs={{0,32},{1,33},{2,34},{3,35},{4,36},{5,37},{6,38},{7,39},{8,40},{9,... | collective-permute-start | bytes 208904 | tf_op jit(solution)/shard_map/ppermute | solution.py:587
  63.6 2.4 %collective-permute-start.9 = (bf16[16,2176]{1,0:T(8,128)(2,1)S(1)}, bf16[16,2176]{1,0:T(8,128)(2,1)S(1)}, u32[]{:S(2)}, u32[]{:S(2)}) collective-permute-start(bf16[16,2176]{1,0:T(8,128)(2,1)S(1)} %copy-done.1), channel_id=1, source_target_pairs={{0,64},{1,65},{2,66},{3,67},{4,68},{5,69},{6,70},{7,71},{8,72},{9,... | collective-permute-start | bytes 208904 | tf_op jit(solution)/shard_map/ppermute | solution.py:587
  66.0 1.2 collective-permute-start.8
  67.2 11.3 %collective-permute-done.10.b3 = bf16[16,2176]{1,0:T(8,128)(2,1)S(1)} collective-permute-done((bf16[16,2176]{1,0:T(8,128)(2,1)S(1)}, bf16[16,2176]{1,0:T(8,128)(2,1)S(1)}, u32[]{:S(2)}, u32[]{:S(2)}) %collective-permute-start.10) | collective-permute-done | bytes 69664 | tf_op jit(solution)/shard_map/ppermute | solution.py:587
  78.5 2.3 %collective-permute-done.9.b2 = bf16[16,2176]{1,0:T(8,128)(2,1)S(1)} collective-permute-done((bf16[16,2176]{1,0:T(8,128)(2,1)S(1)}, bf16[16,2176]{1,0:T(8,128)(2,1)S(1)}, u32[]{:S(2)}, u32[]{:S(2)}) %collective-permute-start.9) | collective-permute-done | bytes 69664 | tf_op jit(solution)/shard_map/ppermute | solution.py:587
  80.8 0.0 collective-permute-done.8.b1
  80.8 0.0 all-to-all-done.1.got_any
  80.8 1.7 %plane.1 = (bf16[8,16,2176]{2,1,0:T(8,128)(2,1)}, bf16[4,16,2176]{2,1,0:T(8,128)(2,1)S(1)}) custom-call(s32[1]{0:T(128)} %bitcast.3.x_ref, bf16[16,16,2176]{2,1,0:T(8,128)(2,1)S(1)} %all-to-all-done.1.got_any, bf16[16,2176]{1,0:T(8,128)(2,1)S(1)} %copy-done.1, bf16[16,2176]{1,0:T(8,128)(2,1)S(1)} %collective-permute-done.8.b1, ...), custom_call_target="tpu_custom_call" | custom-call | flops 557056 | bytes 1700000 | tf_op jit(solution)/shard_map/plane/pallas_call | solution.py:375
  82.5 3.5 %all-to-all-start.2 = ((bf16[8,16,2176]{2,1,0:T(8,128)(2,1)}), bf16[8,16,2176]{2,1,0:T(8,128)(2,1)S(1)}, u32[]{:S(2)}, u32[]{:S(2)}) async-start(bf16[8,16,2176]{2,1,0:T(8,128)(2,1)} %get-tuple-element.42), calls=%async_computation.2 | async-start | bytes 1114112 | tf_op jit(solution)/shard_map/all_to_all | solution.py:572
  86.1 1.3 collective-permute-start.13
  87.3 2.4 %collective-permute-start.12 = (bf16[4,16,2176]{2,1,0:T(8,128)(2,1)S(1)}, bf16[4,16,2176]{2,1,0:T(8,128)(2,1)S(1)}, u32[]{:S(2)}, u32[]{:S(2)}) collective-permute-start(bf16[4,16,2176]{2,1,0:T(8,128)(2,1)S(1)} %get-tuple-element.45.b0), channel_id=1, source_target_pairs={{0,4},{1,5},{2,6},{3,7},{4,0},{5,1},{6,2},{7,3},{8,12},{9,13},{10,... | collective-permute-start | bytes 835592 | tf_op jit(solution)/shard_map/ppermute | solution.py:587
  89.7 1.2 collective-permute-start.11
  90.9 3.5 %collective-permute-done.13.b3 = bf16[4,16,2176]{2,1,0:T(8,128)(2,1)S(1)} collective-permute-done((bf16[4,16,2176]{2,1,0:T(8,128)(2,1)S(1)}, bf16[4,16,2176]{2,1,0:T(8,128)(2,1)S(1)}, u32[]{:S(2)}, u32[]{:S(2)}) %collective-permute-start.13) | collective-permute-done | bytes 278560 | tf_op jit(solution)/shard_map/ppermute | solution.py:587
  94.4 6.8 %collective-permute-done.12.b2 = bf16[4,16,2176]{2,1,0:T(8,128)(2,1)S(1)} collective-permute-done((bf16[4,16,2176]{2,1,0:T(8,128)(2,1)S(1)}, bf16[4,16,2176]{2,1,0:T(8,128)(2,1)S(1)}, u32[]{:S(2)}, u32[]{:S(2)}) %collective-permute-start.12) | collective-permute-done | bytes 278560 | tf_op jit(solution)/shard_map/ppermute | solution.py:587
  101.2 0.3 collective-permute-done.11.b1
  101.5 3.2 %all-to-all-done.2.got_ref = bf16[8,16,2176]{2,1,0:T(8,128)(2,1)S(1)} async-done(((bf16[8,16,2176]{2,1,0:T(8,128)(2,1)}), bf16[8,16,2176]{2,1,0:T(8,128)(2,1)S(1)}, u32[]{:S(2)}, u32[]{:S(2)}) %all-to-all-start.2) | async-done | bytes 557088 | tf_op jit(solution)/shard_map/all_to_all | solution.py:572
  104.6 2.0 %column.1 = (bf16[16,16,2176]{2,1,0:T(8,128)(2,1)}, f32[2,2048]{1,0:T(2,128)S(1)}) custom-call(s32[1]{0:T(128)} %bitcast.z_ref, bf16[8,16,2176]{2,1,0:T(8,128)(2,1)S(1)} %all-to-all-done.2.got_ref, f32[16,2048]{1,0:T(8,128)S(1)} %copy-done, f32[1,1]{1,0:T(1,128)} %get-tuple-element.44.sq_ref, bf16[4,16,2176]{2,1,0:T(8,128)(2,1)S(1)} %collective-permute-done.11.b1, ...), custom_call_target="tpu_custom_call" | custom-call | flops 278528 | bytes 1700000 | tf_op jit(solution)/shard_map/column/pallas_call | solution.py:408
  106.6 4.7 %all-to-all-start.3 = ((bf16[16,16,2176]{2,1,0:T(8,128)(2,1)}), bf16[16,16,2176]{2,1,0:T(8,128)(2,1)S(1)}, u32[]{:S(2)}, u32[]{:S(2)}) async-start(bf16[16,16,2176]{2,1,0:T(8,128)(2,1)} %get-tuple-element.46.after_any), calls=%async_computation.3 | async-start | bytes 2228224 | tf_op jit(solution)/shard_map/all_to_all | solution.py:572
  111.3 0.0 copy-start.2
  111.3 0.0 copy-start.3
  111.3 0.0 copy-start.4
  111.3 0.0 copy-start.5
  111.3 1.7 %basis.1 = bf16[16,16,2176]{2,1,0:T(8,128)(2,1)S(1)} custom-call(s32[1]{0:T(128)} %bitcast.6.y_ref, bf16[4,16,2176]{2,1,0:T(8,128)(2,1)S(1)} %get-tuple-element.45.b0, bf16[4,16,2176]{2,1,0:T(8,128)(2,1)S(1)} %collective-permute-done.11.b1, bf16[4,16,2176]{2,1,0:T(8,128)(2,1)S(1)} %collective-permute-done.12.b2, ...), custom_call_target="tpu_custom_call" | custom-call | bytes 2200000 | tf_op jit(solution)/shard_map/basis/pallas_call | solution.py:433
  113.0 0.9 collective-permute-start.15
  113.9 13.6 %all-to-all-done.3 = bf16[16,16,2176]{2,1,0:T(8,128)(2,1)S(1)} async-done(((bf16[16,16,2176]{2,1,0:T(8,128)(2,1)}), bf16[16,16,2176]{2,1,0:T(8,128)(2,1)S(1)}, u32[]{:S(2)}, u32[]{:S(2)}) %all-to-all-start.3) | async-done | bytes 1114144 | tf_op jit(solution)/shard_map/all_to_all | solution.py:572
  127.6 3.2 %collective-permute-start.14 = (bf16[256,2176]{1,0:T(8,128)(2,1)S(1)}, bf16[256,2176]{1,0:T(8,128)(2,1)S(1)}, u32[]{:S(2)}, u32[]{:S(2)}) collective-permute-start(bf16[256,2176]{1,0:T(8,128)(2,1)S(1)} %bitcast.8), channel_id=1, source_target_pairs={{0,1},{1,0},{2,3},{3,2},{4,5},{5,4},{6,7},{7,6},{8,9},{9,8},{10,11... | collective-permute-start | bytes 3342344 | tf_op jit(solution)/shard_map/ppermute | solution.py:618
  130.8 0.1 pad_add_fusion.at_ref
  130.9 0.0 collective-permute-done.15.a1_any
  130.9 2.3 %collective-permute-done.14.b1_any = bf16[256,2176]{1,0:T(8,128)(2,1)S(1)} collective-permute-done((bf16[256,2176]{1,0:T(8,128)(2,1)S(1)}, bf16[256,2176]{1,0:T(8,128)(2,1)S(1)}, u32[]{:S(2)}, u32[]{:S(2)}) %collective-permute-start.14) | collective-permute-done | bytes 1114144 | tf_op jit(solution)/shard_map/ppermute | solution.py:618
  133.2 0.0 copy-done.2
  133.2 4.2 %update.1 = (bf16[512,2048]{1,0:T(8,128)(2,1)}, bf16[2,2048]{1,0:T(2,128)(2,1)}, f32[2,2048]{1,0:T(2,128)}, f32[2,2048]{1,0:T(2,128)}, f32[2,8]{1,0:T(2,128)}, /*index=5*/f32[2,8]{1,0:T(2,128)}) custom-call(s32[2]{0:T(128)S(1)} %pad_add_fusion.at_ref, bf16[256,2176]{1,0:T(8,128)(2,1)S(1)} %bitcast.9, bf16[256,2176]{1,0:T(8,128)(2,1)S(1)} %collective-permute-done.14.b1_any, ...), custom_call_target="tpu_custom_call" | custom-call | flops 268435456 | bytes 6500000 | tf_op jit(solution)/shard_map/update/pallas_call | solution.py:556
  (15 shorter events, 0.0 us)
Async XLA Ops:
  6.2 29.2 %all-to-all-start = ((f32[8,4,2048]{2,1,0:T(4,128)}), f32[8,4,2048]{2,1,0:T(4,128)S(1)}, u32[]{:S(2)}, u32[]{:S(2)}) async-start(f32[8,4,2048]{2,1,0:T(4,128)} %get-tuple-element.31), calls=%async_computation | async-start | bytes 524288 | tf_op jit(solution)/shard_map/all_to_all | solution.py:572
  17.7 11.8 %collective-permute-start.6 = (f32[2,4352]{1,0:T(2,128)}, f32[2,4352]{1,0:T(2,128)S(1)}, u32[]{:S(2)}, u32[]{:S(2)}) collective-permute-start(f32[2,4352]{1,0:T(2,128)} %get-tuple-element.33.p0), channel_id=1, source_target_pairs={{0,8},{1,9},{2,10},{3,11},{4,12},{5,13},{6,14},{7,15},{8,16},{9,17... | collective-permute-start | bytes 104456 | tf_op jit(solution)/shard_map/ppermute | solution.py:587
  18.4 13.4 %collective-permute-start.5 = (f32[2,4352]{1,0:T(2,128)}, f32[2,4352]{1,0:T(2,128)S(1)}, u32[]{:S(2)}, u32[]{:S(2)}) collective-permute-start(f32[2,4352]{1,0:T(2,128)} %get-tuple-element.33.p0), channel_id=1, source_target_pairs={{0,16},{1,17},{2,18},{3,19},{4,20},{5,21},{6,22},{7,23},{8,24},{9,... | collective-permute-start | bytes 104456 | tf_op jit(solution)/shard_map/ppermute | solution.py:587
  19.6 13.0 %collective-permute-start.4 = (f32[2,4352]{1,0:T(2,128)}, f32[2,4352]{1,0:T(2,128)S(1)}, u32[]{:S(2)}, u32[]{:S(2)}) collective-permute-start(f32[2,4352]{1,0:T(2,128)} %get-tuple-element.33.p0), channel_id=1, source_target_pairs={{0,24},{1,25},{2,26},{3,27},{4,28},{5,29},{6,30},{7,31},{8,128},{9... | collective-permute-start | bytes 104456 | tf_op jit(solution)/shard_map/ppermute | solution.py:587
  24.5 8.7 %collective-permute-start.3 = (f32[2,4352]{1,0:T(2,128)}, f32[2,4352]{1,0:T(2,128)S(1)}, u32[]{:S(2)}, u32[]{:S(2)}) collective-permute-start(f32[2,4352]{1,0:T(2,128)} %get-tuple-element.33.p0), channel_id=1, source_target_pairs={{0,128},{1,129},{2,130},{3,131},{4,132},{5,133},{6,134},{7,135},{8... | collective-permute-start | bytes 104456 | tf_op jit(solution)/shard_map/ppermute | solution.py:587
  25.0 8.3 %collective-permute-start.2 = (f32[2,4352]{1,0:T(2,128)}, f32[2,4352]{1,0:T(2,128)S(1)}, u32[]{:S(2)}, u32[]{:S(2)}) collective-permute-start(f32[2,4352]{1,0:T(2,128)} %get-tuple-element.33.p0), channel_id=1, source_target_pairs={{0,136},{1,137},{2,138},{3,139},{4,140},{5,141},{6,142},{7,143},{8... | collective-permute-start | bytes 104456 | tf_op jit(solution)/shard_map/ppermute | solution.py:587
  29.5 5.9 %copy-start.8 = (f32[2,4352]{1,0:T(2,128)}, f32[2,4352]{1,0:T(2,128)S(1)}, u32[]{:S(2)}) copy-start(f32[2,4352]{1,0:T(2,128)S(1)} %collective-permute-done.6.p7) | copy-start | bytes 104452
  29.5 5.8 %collective-permute-start.1 = (f32[2,4352]{1,0:T(2,128)}, f32[2,4352]{1,0:T(2,128)S(1)}, u32[]{:S(2)}, u32[]{:S(2)}) collective-permute-start(f32[2,4352]{1,0:T(2,128)} %get-tuple-element.33.p0), channel_id=1, source_target_pairs={{0,144},{1,145},{2,146},{3,147},{4,148},{5,149},{6,150},{7,151},{8... | collective-permute-start | bytes 104456 | tf_op jit(solution)/shard_map/ppermute | solution.py:587
  31.9 3.5 %copy-start.9 = (f32[2,4352]{1,0:T(2,128)}, f32[2,4352]{1,0:T(2,128)S(1)}, u32[]{:S(2)}) copy-start(f32[2,4352]{1,0:T(2,128)S(1)} %collective-permute-done.5.p6) | copy-start | bytes 104452
  31.9 3.5 %collective-permute-start = (f32[2,4352]{1,0:T(2,128)}, f32[2,4352]{1,0:T(2,128)S(1)}, u32[]{:S(2)}, u32[]{:S(2)}) collective-permute-start(f32[2,4352]{1,0:T(2,128)} %get-tuple-element.33.p0), channel_id=1, source_target_pairs={{0,152},{1,153},{2,154},{3,155},{4,156},{5,157},{6,158},{7,159},{8... | collective-permute-start | bytes 104456 | tf_op jit(solution)/shard_map/ppermute | solution.py:587
  32.6 2.8 %copy-start.10 = (f32[2,4352]{1,0:T(2,128)}, f32[2,4352]{1,0:T(2,128)S(1)}, u32[]{:S(2)}) copy-start(f32[2,4352]{1,0:T(2,128)S(1)} %collective-permute-done.4.p5) | copy-start | bytes 104452
  33.3 2.1 %copy-start.11 = (f32[2,4352]{1,0:T(2,128)}, f32[2,4352]{1,0:T(2,128)S(1)}, u32[]{:S(2)}) copy-start(f32[2,4352]{1,0:T(2,128)S(1)} %collective-permute-done.3.p4) | copy-start | bytes 104452
  33.3 2.1 %copy-start.12 = (f32[2,4352]{1,0:T(2,128)}, f32[2,4352]{1,0:T(2,128)S(1)}, u32[]{:S(2)}) copy-start(f32[2,4352]{1,0:T(2,128)S(1)} %collective-permute-done.2.p3) | copy-start | bytes 104452
  35.3 0.6 copy-start.13
  35.4 0.6 copy-start.14
  35.4 0.7 copy-start.7
  43.1 7.6 %collective-permute-start.7 = (bf16[256,2176]{1,0:T(8,128)(2,1)}, bf16[256,2176]{1,0:T(8,128)(2,1)S(1)}, u32[]{:S(2)}, u32[]{:S(2)}) collective-permute-start(bf16[256,2176]{1,0:T(8,128)(2,1)} %get-tuple-element.39), channel_id=1, source_target_pairs={{0,1},{1,0},{2,3},{3,2},{4,5},{5,4},{6,7},{7,6},{8,9},{9,8},{10,11... | collective-permute-start | bytes 3342344 | tf_op jit(solution)/shard_map/ppermute | solution.py:609
  50.7 1.0 copy-start.6
  55.3 6.9 %copy-start.1 = (bf16[16,2176]{1,0:T(8,128)(2,1)S(1)}, bf16[16,2176]{1,0:T(8,128)(2,1)}, u32[]{:S(2)}) copy-start(bf16[16,2176]{1,0:T(8,128)(2,1)} %get-tuple-element.41.b0) | copy-start | bytes 208900
  55.3 25.5 %all-to-all-start.1 = ((bf16[16,16,2176]{2,1,0:T(8,128)(2,1)}), bf16[16,16,2176]{2,1,0:T(8,128)(2,1)S(1)}, u32[]{:S(2)}, u32[]{:S(2)}) async-start(bf16[16,16,2176]{2,1,0:T(8,128)(2,1)} %bitcast.12), calls=%async_computation.1 | async-start | bytes 2228224 | tf_op jit(solution)/shard_map/all_to_all | solution.py:572
  62.2 16.3 %collective-permute-start.10 = (bf16[16,2176]{1,0:T(8,128)(2,1)S(1)}, bf16[16,2176]{1,0:T(8,128)(2,1)S(1)}, u32[]{:S(2)}, u32[]{:S(2)}) collective-permute-start(bf16[16,2176]{1,0:T(8,128)(2,1)S(1)} %copy-done.1), channel_id=1, source_target_pairs={{0,32},{1,33},{2,34},{3,35},{4,36},{5,37},{6,38},{7,39},{8,40},{9,... | collective-permute-start | bytes 208904 | tf_op jit(solution)/shard_map/ppermute | solution.py:587
  63.6 17.1 %collective-permute-start.9 = (bf16[16,2176]{1,0:T(8,128)(2,1)S(1)}, bf16[16,2176]{1,0:T(8,128)(2,1)S(1)}, u32[]{:S(2)}, u32[]{:S(2)}) collective-permute-start(bf16[16,2176]{1,0:T(8,128)(2,1)S(1)} %copy-done.1), channel_id=1, source_target_pairs={{0,64},{1,65},{2,66},{3,67},{4,68},{5,69},{6,70},{7,71},{8,72},{9,... | collective-permute-start | bytes 208904 | tf_op jit(solution)/shard_map/ppermute | solution.py:587
  66.0 14.7 %collective-permute-start.8 = (bf16[16,2176]{1,0:T(8,128)(2,1)S(1)}, bf16[16,2176]{1,0:T(8,128)(2,1)S(1)}, u32[]{:S(2)}, u32[]{:S(2)}) collective-permute-start(bf16[16,2176]{1,0:T(8,128)(2,1)S(1)} %copy-done.1), channel_id=1, source_target_pairs={{0,96},{1,97},{2,98},{3,99},{4,100},{5,101},{6,102},{7,103},{8,104... | collective-permute-start | bytes 208904 | tf_op jit(solution)/shard_map/ppermute | solution.py:587
  80.8 23.9 %copy-start = (f32[16,2048]{1,0:T(8,128)S(1)}, f32[16,2048]{1,0:T(8,128)}, u32[]{:S(2)}) copy-start(f32[16,2048]{1,0:T(8,128)} %get-tuple-element.43.w_ref) | copy-start | bytes 393220
  82.5 22.1 %all-to-all-start.2 = ((bf16[8,16,2176]{2,1,0:T(8,128)(2,1)}), bf16[8,16,2176]{2,1,0:T(8,128)(2,1)S(1)}, u32[]{:S(2)}, u32[]{:S(2)}) async-start(bf16[8,16,2176]{2,1,0:T(8,128)(2,1)} %get-tuple-element.42), calls=%async_computation.2 | async-start | bytes 1114112 | tf_op jit(solution)/shard_map/all_to_all | solution.py:572
  86.1 8.3 %collective-permute-start.13 = (bf16[4,16,2176]{2,1,0:T(8,128)(2,1)S(1)}, bf16[4,16,2176]{2,1,0:T(8,128)(2,1)S(1)}, u32[]{:S(2)}, u32[]{:S(2)}) collective-permute-start(bf16[4,16,2176]{2,1,0:T(8,128)(2,1)S(1)} %get-tuple-element.45.b0), channel_id=1, source_target_pairs={{0,2},{1,3},{2,4},{3,5},{4,6},{5,7},{6,0},{7,1},{8,10},{9,11},{10,... | collective-permute-start | bytes 835592 | tf_op jit(solution)/shard_map/ppermute | solution.py:587
  87.3 13.9 %collective-permute-start.12 = (bf16[4,16,2176]{2,1,0:T(8,128)(2,1)S(1)}, bf16[4,16,2176]{2,1,0:T(8,128)(2,1)S(1)}, u32[]{:S(2)}, u32[]{:S(2)}) collective-permute-start(bf16[4,16,2176]{2,1,0:T(8,128)(2,1)S(1)} %get-tuple-element.45.b0), channel_id=1, source_target_pairs={{0,4},{1,5},{2,6},{3,7},{4,0},{5,1},{6,2},{7,3},{8,12},{9,13},{10,... | collective-permute-start | bytes 835592 | tf_op jit(solution)/shard_map/ppermute | solution.py:587
  89.7 11.8 %collective-permute-start.11 = (bf16[4,16,2176]{2,1,0:T(8,128)(2,1)S(1)}, bf16[4,16,2176]{2,1,0:T(8,128)(2,1)S(1)}, u32[]{:S(2)}, u32[]{:S(2)}) collective-permute-start(bf16[4,16,2176]{2,1,0:T(8,128)(2,1)S(1)} %get-tuple-element.45.b0), channel_id=1, source_target_pairs={{0,6},{1,7},{2,0},{3,1},{4,2},{5,3},{6,4},{7,5},{8,14},{9,15},{10,... | collective-permute-start | bytes 835592 | tf_op jit(solution)/shard_map/ppermute | solution.py:587
  106.6 20.9 %all-to-all-start.3 = ((bf16[16,16,2176]{2,1,0:T(8,128)(2,1)}), bf16[16,16,2176]{2,1,0:T(8,128)(2,1)S(1)}, u32[]{:S(2)}, u32[]{:S(2)}) async-start(bf16[16,16,2176]{2,1,0:T(8,128)(2,1)} %get-tuple-element.46.after_any), calls=%async_computation.3 | async-start | bytes 2228224 | tf_op jit(solution)/shard_map/all_to_all | solution.py:572
  111.3 21.9 %copy-start.2 = (f32[2,2048]{1,0:T(2,128)S(1)}, f32[2,2048]{1,0:T(2,128)}, u32[]{:S(2)}) copy-start(f32[2,2048]{1,0:T(2,128)} %m_any.3) | copy-start | bytes 49156
  111.3 21.9 %copy-start.3 = (f32[2,2048]{1,0:T(2,128)S(1)}, f32[2,2048]{1,0:T(2,128)}, u32[]{:S(2)}) copy-start(f32[2,2048]{1,0:T(2,128)} %v_any.3) | copy-start | bytes 49156
  111.3 21.9 %copy-start.4 = (f32[2,2048]{1,0:T(2,128)S(1)}, f32[2,2048]{1,0:T(2,128)}, u32[]{:S(2)}) copy-start(f32[2,2048]{1,0:T(2,128)} %bn_any.5) | copy-start | bytes 49156
  111.3 21.9 %copy-start.5 = (f32[2,8]{1,0:T(2,128)S(1)}, f32[2,8]{1,0:T(2,128)}, u32[]{:S(2)}) copy-start(f32[2,8]{1,0:T(2,128)} %bnm_any.3) | copy-start | bytes 196
  113.0 17.8 %collective-permute-start.15 = (bf16[256,2176]{1,0:T(8,128)(2,1)S(1)}, bf16[256,2176]{1,0:T(8,128)(2,1)S(1)}, u32[]{:S(2)}, u32[]{:S(2)}) collective-permute-start(bf16[256,2176]{1,0:T(8,128)(2,1)S(1)} %bitcast.10), channel_id=1, source_target_pairs={{0,1},{1,0},{2,3},{3,2},{4,5},{5,4},{6,7},{7,6},{8,9},{9,8},{10,11... | collective-permute-start | bytes 3342344 | tf_op jit(solution)/shard_map/ppermute | solution.py:616
  127.6 5.6 %collective-permute-start.14 = (bf16[256,2176]{1,0:T(8,128)(2,1)S(1)}, bf16[256,2176]{1,0:T(8,128)(2,1)S(1)}, u32[]{:S(2)}, u32[]{:S(2)}) collective-permute-start(bf16[256,2176]{1,0:T(8,128)(2,1)S(1)} %bitcast.8), channel_id=1, source_target_pairs={{0,1},{1,0},{2,3},{3,2},{4,5},{5,4},{6,7},{7,6},{8,9},{9,8},{10,11... | collective-permute-start | bytes 3342344 | tf_op jit(solution)/shard_map/ppermute | solution.py:618

commit v3 on v2

v3 whole, which is shorter than its diff:
```python
import functools

import jax
import jax.numpy as jnp
from jax import lax
from jax.experimental import pallas as pl
from jax.experimental.pallas import tpu as pltpu
from jax.sharding import Mesh, PartitionSpec as P

eps_norm = 1e-05
momentum_rate = 0.9
learn_rate = 4.0
trust_coef = 0.001
decay_rate = 5e-05

AXES = ("zh", "x", "zl", "y", "c")
SIZES = (2, 4, 4, 4, 2)
GX = ("zh", "x")
XY = ("x", "y")
Z = ("zh", "zl")
BF = jnp.bfloat16
F32 = jnp.float32

ROWS = 392
CB = 512
C = 2048
EXT = 128
WIDE = C + EXT
PIECE = 2 * C + 2 * EXT
COLS = 512
STEPS = C // COLS
COUNT = float(ROWS * 8)
VMEM_BYTES = 24 * 1024 * 1024
VMEM_ALL = 60 * 1024 * 1024


def sibling_pairs():
    return [(i, i ^ 1) for i in range(256)]


def natural_row(t, c):
    cc = c ^ (t >> 8)
    return (
        ((t >> 3) & 1) * 256
        + ((t >> 6) & 3) * 64
        + ((t >> 1) & 3) * 16
        + ((t >> 4) & 3) * 4
        + cc * 2
        + (t & 1)
    )


def hi_lo(v):
    hi = v.astype(BF).astype(F32)
    return hi, v - hi


def params(limit=VMEM_BYTES):
    return pltpu.CompilerParams(vmem_limit_bytes=limit)


ANY = pl.BlockSpec(memory_space=pl.ANY)
VMEM = pl.BlockSpec(memory_space=pltpu.VMEM)
SMEM = pl.BlockSpec(memory_space=pltpu.SMEM)
DMA = pltpu.SemaphoreType.DMA


TOKEN = jax.ShapeDtypeStruct((1, EXT), F32)


def done(token_ref):
    token_ref[...] = jnp.zeros_like(token_ref)


def copy(src, dst, sem):
    made = pltpu.make_async_copy(src, dst, sem)
    made.start()
    return made


def cols(j):
    return pl.ds(j * COLS, COLS)


def own_block(row, mine):
    block = jnp.zeros((2, EXT), F32)
    for q in range(16):
        block = jnp.where((mine >> 4) == q, row[:, EXT * q : EXT * q + EXT], block)
    return block


def stats_kernel(
    mine_ref, f_any, w_any, cot_any, pre_any, m_any, v_any, bn_any, bnm_any,
    stat_ref, base_ref,
    f, w, cot, pre, master, momentum, bn, bnm, sems,
):
    mine = mine_ref[0]
    first = copy(f_any, f, sems.at[0, STEPS])
    loads = []
    for j in range(STEPS):
        loads.append(
            [
                copy(w_any.at[:, cols(j)], w.at[:, cols(j)], sems.at[0, j]),
                copy(cot_any.at[:, cols(j)], cot.at[:, cols(j)], sems.at[1, j]),
                copy(pre_any.at[:, cols(j)], pre.at[:, cols(j)], sems.at[2, j]),
            ]
        )
    small = [
        copy(m_any, master, sems.at[1, STEPS]),
        copy(v_any, momentum, sems.at[2, STEPS]),
        copy(bn_any, bn, sems.at[3, STEPS]),
        copy(bnm_any, bnm, sems.at[4, 0]),
    ]
    first.wait()
    for j in range(STEPS):
        loads[j][0].wait()
        conv = jnp.dot(f[...], w[:, cols(j)], preferred_element_type=F32)
        loads[j][1].wait()
        loads[j][2].wait()
        u = jnp.where(pre[:, cols(j)].astype(F32) > 0, cot[:, cols(j)].astype(F32), 0.0)
        stat = jnp.concatenate(
            [
                jnp.sum(conv, axis=0, keepdims=True),
                jnp.sum(conv * conv, axis=0, keepdims=True),
                jnp.sum(u, axis=0, keepdims=True),
                jnp.sum(u * conv, axis=0, keepdims=True),
            ],
            axis=0,
        )
        stat_ref[:, :, cols(j)] = jnp.broadcast_to(stat[None], (8, 4, COLS))
    for load in small:
        load.wait()
    base_ref[:, 0:C] = master[...] - momentum_rate * momentum[...]
    base_ref[:, C : 2 * C] = master[...]
    own_bn = own_block(bn[...], mine)
    lane = lax.broadcasted_iota(jnp.int32, (2, EXT), 1)
    bn_base = own_bn - momentum_rate * jnp.concatenate([bnm[...]] * 16, axis=1)
    base_ref[:, 2 * C : 2 * C + EXT] = jnp.where((lane >> 3) == (mine & 15), bn_base, 0.0)
    square = jnp.sum(master[...] * master[...], axis=(0, 1), keepdims=True)
    row = lax.broadcasted_iota(jnp.int32, (2, EXT), 0)
    base_ref[:, 2 * C + EXT :] = jnp.where((row == 0) & (lane == 0), square, 0.0)


def stats_call(mine, features, weight, cotangent, pre_act, master, momentum, bn_params, bn_momentum):
    return pl.pallas_call(
        stats_kernel,
        in_specs=[SMEM] + [ANY] * 8,
        out_specs=[VMEM, VMEM],
        out_shape=[
            jax.ShapeDtypeStruct((8, 4, C), F32),
            jax.ShapeDtypeStruct((2, PIECE), F32),
        ],
        scratch_shapes=[
            pltpu.VMEM((ROWS, CB), BF),
            pltpu.VMEM((CB, C), BF),
            pltpu.VMEM((ROWS, C), BF),
            pltpu.VMEM((ROWS, C), BF),
            pltpu.VMEM((2, C), F32),
            pltpu.VMEM((2, C), F32),
            pltpu.VMEM((2, C), F32),
            pltpu.VMEM((2, 8), F32),
            DMA((5, STEPS + 1)),
        ],
        compiler_params=params(VMEM_ALL),
        cost_estimate=pl.CostEstimate(flops=2 * ROWS * CB * C, bytes_accessed=7500000, transcendentals=0),
        name="stats",
    )(mine, features, weight, cotangent, pre_act, master, momentum, bn_params, bn_momentum)


def prep_kernel(
    c_ref, f_any, w_any, cot_any, pre_any, up_any, conv_any, ft_ref, f, w, cot, pre, up, conv, sems
):
    first = copy(f_any, f, sems.at[0, STEPS])
    loads = []
    for j in range(STEPS):
        loads.append(
            [
                copy(w_any.at[:, cols(j)], w.at[:, cols(j)], sems.at[0, j]),
                copy(cot_any.at[:, cols(j)], cot.at[:, cols(j)], sems.at[1, j]),
                copy(pre_any.at[:, cols(j)], pre.at[:, cols(j)], sems.at[2, j]),
            ]
        )
    t = lax.broadcasted_iota(jnp.int32, (CB, CB), 0)
    r = lax.broadcasted_iota(jnp.int32, (CB, CB), 1)
    sel = jnp.where(r == natural_row(t, c_ref[0]), 1.0, 0.0).astype(BF)
    first.wait()
    ft_ref[...] = lax.dot_general(sel, f[...], (((1,), (1,)), ((), ())), preferred_element_type=F32).astype(BF)
    stores = []
    for j in range(STEPS):
        loads[j][0].wait()
        conv[:, cols(j)] = jnp.dot(f[...], w[:, cols(j)], preferred_element_type=F32)
        stores.append(copy(conv.at[:, cols(j)], conv_any.at[:, cols(j)], sems.at[4, j]))
        loads[j][1].wait()
        loads[j][2].wait()
        u = jnp.where(pre[:, cols(j)].astype(F32) > 0, cot[:, cols(j)].astype(F32), 0.0)
        up[:, cols(j)] = u.astype(BF)
        stores.append(copy(up.at[:, cols(j)], up_any.at[:, cols(j)], sems.at[3, j]))
    for store in stores:
        store.wait()


def prep_call(c, features, weight, cotangent, pre_act):
    return pl.pallas_call(
        prep_kernel,
        in_specs=[SMEM] + [ANY] * 4,
        out_specs=[ANY, ANY, VMEM],
        out_shape=[
            jax.ShapeDtypeStruct((ROWS, C), BF),
            jax.ShapeDtypeStruct((ROWS, C), F32),
            jax.ShapeDtypeStruct((CB, ROWS), BF),
        ],
        scratch_shapes=[
            pltpu.VMEM((ROWS, CB), BF),
            pltpu.VMEM((CB, C), BF),
            pltpu.VMEM((ROWS, C), BF),
            pltpu.VMEM((ROWS, C), BF),
            pltpu.VMEM((ROWS, C), BF),
            pltpu.VMEM((ROWS, C), F32),
            DMA((5, STEPS + 1)),
        ],
        compiler_params=params(VMEM_ALL),
        cost_estimate=pl.CostEstimate(flops=3 * ROWS * CB * C, bytes_accessed=7500000, transcendentals=0),
        name="prep",
    )(c, features, weight, cotangent, pre_act)


def grad_kernel(
    at_ref, stat_ref, up_any, conv_any, ft_ref, bn_any, p0, p1, p2, p3,
    gc_any, send_ref, own_ref, own_ext_ref, rows_ref,
    up, conv, gc, bn, ext_send, ext_own, rows, sems,
):
    c, zl = at_ref[0], at_ref[1]
    early = copy(bn_any, bn, sems.at[0, STEPS])
    loads = [
        [
            copy(conv_any.at[:, cols(j)], conv.at[:, cols(j)], sems.at[0, j]),
            copy(up_any.at[:, cols(j)], up.at[:, cols(j)], sems.at[1, j]),
        ]
        for j in range(STEPS)
    ]
    for k, piece in enumerate((p0, p1, p2, p3)):
        rows[2 * k : 2 * k + 2, :] = piece[...]
    rows_ref[...] = pltpu.roll(rows[...], 2 * zl, 0)
    sums = jnp.sum(stat_ref[...], axis=0)
    mean = sums[0:1] / COUNT
    inv_std = lax.rsqrt(sums[1:2] / COUNT - mean * mean + eps_norm)
    sum_b = sums[2:3]
    sum_g = inv_std * (sums[3:4] - mean * sum_b)
    early.wait()
    alpha = bn[0:1] * inv_std
    slope = alpha * inv_std * (sum_g / COUNT)
    shift = sum_b / COUNT
    scale_row = sum_g * 0.125
    shift_row = sum_b * 0.125
    mine = jnp.where(c == 0, scale_row, shift_row)
    other = jnp.where(c == 0, shift_row, scale_row)
    ext_send[...] = jnp.zeros_like(ext_send)
    ext_own[...] = jnp.zeros_like(ext_own)
    for q in range(16):
        ext_own[16 * q : 16 * q + 1, :] = mine[:, 128 * q : 128 * q + 128]
        ext_send[16 * q : 16 * q + 1, :] = other[:, 128 * q : 128 * q + 128]
    own_ext_ref[...] = ext_own[...]
    send_ref[:, C:] = ext_send[...].astype(BF)
    stores = []
    for j in range(STEPS):
        at = slice(j * COLS, j * COLS + COLS)
        for load in loads[j]:
            load.wait()
        grad = alpha[:, at] * (up[:, at].astype(F32) - shift[:, at])
        grad = (grad - (conv[:, at] - mean[:, at]) * slope[:, at]).astype(BF)
        gc[:, at] = grad
        stores.append(copy(gc.at[:, cols(j)], gc_any.at[:, cols(j)], sems.at[2, j]))
        g = jnp.dot(ft_ref[...], grad, preferred_element_type=F32)
        send_ref[:, at] = g[CB // 2 :].astype(BF)
        own_ref[:, at] = g[: CB // 2].astype(BF)
    for store in stores:
        store.wait()


def grad_call(at, stats, up, conv, ft, bn_params, pieces):
    return pl.pallas_call(
        grad_kernel,
        in_specs=[SMEM, VMEM, ANY, ANY, VMEM, ANY] + [VMEM] * 4,
        out_specs=[ANY] + [VMEM] * 4,
        out_shape=[
            jax.ShapeDtypeStruct((ROWS, C), BF),
            jax.ShapeDtypeStruct((CB // 2, WIDE), BF),
            jax.ShapeDtypeStruct((CB // 2, C), BF),
            jax.ShapeDtypeStruct((CB // 2, EXT), F32),
            jax.ShapeDtypeStruct((8, PIECE), F32),
        ],
        scratch_shapes=[
            pltpu.VMEM((ROWS, C), BF),
            pltpu.VMEM((ROWS, C), F32),
            pltpu.VMEM((ROWS, C), BF),
            pltpu.VMEM((2, C), F32),
            pltpu.VMEM((CB // 2, EXT), F32),
            pltpu.VMEM((CB // 2, EXT), F32),
            pltpu.VMEM((8, PIECE), F32),
            DMA((3, STEPS + 1)),
        ],
        compiler_params=params(VMEM_ALL),
        cost_estimate=pl.CostEstimate(flops=2 * ROWS * CB * C, bytes_accessed=9000000, transcendentals=0),
        name="grad",
    )(at, stats, up, conv, ft, bn_params, *pieces)


def input_kernel(gc_any, w_any, after_any, out_ref, token_ref, gc, w, sems):
    done(token_ref)
    loads = [
        [
            copy(gc_any.at[:, cols(j)], gc.at[:, cols(j)], sems.at[0, j]),
            copy(w_any.at[:, cols(j)], w.at[:, cols(j)], sems.at[1, j]),
        ]
        for j in range(STEPS)
    ]
    total = None
    for j in range(STEPS):
        for load in loads[j]:
            load.wait()
        part = lax.dot_general(
            gc[:, cols(j)], w[:, cols(j)], (((1,), (1,)), ((), ())), preferred_element_type=F32
        )
        total = part if total is None else total + part
    out_ref[...] = total.astype(BF)


def input_call(gc, weight, after):
    return pl.pallas_call(
        input_kernel,
        in_specs=[ANY, ANY, ANY],
        out_specs=[VMEM, VMEM],
        out_shape=[jax.ShapeDtypeStruct((ROWS, CB), BF), TOKEN],
        scratch_shapes=[pltpu.VMEM((ROWS, C), BF), pltpu.VMEM((CB, C), BF), DMA((2, STEPS))],
        compiler_params=params(VMEM_ALL),
        cost_estimate=pl.CostEstimate(flops=2 * ROWS * CB * C, bytes_accessed=4000000, transcendentals=0),
        name="ginput",
    )(gc, weight, after)


def rows_kernel(z_ref, near, far, after_any, base_ref, w_any, w, sem):
    first = z_ref[0] == 0
    low = jnp.where(first, near[...], far[...])
    high = jnp.where(first, far[...], near[...])
    both = jnp.concatenate([low, high], axis=0)
    w[:, :C] = both[:, C : 2 * C]
    w[:, C:] = both[:, 2 * C + EXT :]
    store = copy(w, w_any, sem)
    base_ref[:, :C] = both[:, :C].astype(BF)
    base_ref[:, C:] = both[:, 2 * C : 2 * C + EXT].astype(BF)
    store.wait()


def rows_call(zh, near, far, after):
    return pl.pallas_call(
        rows_kernel,
        in_specs=[SMEM, VMEM, VMEM, ANY],
        out_specs=[VMEM, ANY],
        out_shape=[jax.ShapeDtypeStruct((16, WIDE), BF), jax.ShapeDtypeStruct((16, WIDE), F32)],
        scratch_shapes=[pltpu.VMEM((16, WIDE), F32), DMA],
        compiler_params=params(),
        cost_estimate=pl.CostEstimate(flops=16 * PIECE, bytes_accessed=500000, transcendentals=0),
        name="rows",
    )(zh, near, far, after)


def pair_kernel(own_ref, ext_ref, got_ref, out_ref, token_ref):
    done(token_ref)
    out_ref[:, :C] = (own_ref[...].astype(F32) + got_ref[:, :C].astype(F32)).astype(BF)
    out_ref[:, C:] = (ext_ref[...] + got_ref[:, C:].astype(F32)).astype(BF)


def pair_call(own, ext, got):
    return pl.pallas_call(
        pair_kernel,
        in_specs=[VMEM] * 3,
        out_specs=[VMEM, VMEM],
        out_shape=[jax.ShapeDtypeStruct((256, WIDE), BF), TOKEN],
        compiler_params=params(),
        cost_estimate=pl.CostEstimate(flops=256 * WIDE, bytes_accessed=4500000, transcendentals=0),
        name="pair",
    )(own, ext, got)


def plane_kernel(x_ref, got_ref, b0, b1, b2, b3, out_ref, base_any, token_ref, sems):
    done(token_ref)
    stores = []
    for k, block in enumerate((b0, b1, b2, b3)):
        stores.append(copy(block, base_any.at[(x_ref[0] + k) & 3], sems.at[k]))
    total = jnp.sum(got_ref[...].astype(F32), axis=0).astype(BF)
    out_ref[...] = jnp.broadcast_to(total[None], out_ref.shape)
    for store in stores:
        store.wait()


def plane_call(x, got, bases):
    return pl.pallas_call(
        plane_kernel,
        in_specs=[SMEM, VMEM] + [ANY] * 4,
        out_specs=[VMEM, ANY, VMEM],
        out_shape=[
            jax.ShapeDtypeStruct((8, 16, WIDE), BF),
            jax.ShapeDtypeStruct((4, 16, WIDE), BF),
            TOKEN,
        ],
        scratch_shapes=[DMA((4,))],
        compiler_params=params(),
        cost_estimate=pl.CostEstimate(flops=256 * WIDE, bytes_accessed=1700000, transcendentals=0),
        name="plane",
    )(x, got, *bases)


def column_kernel(z_ref, got_ref, w_any, b1, b2, b3, after_any, out_ref, own_ref, token_ref, w, sem):
    done(token_ref)
    load = copy(w_any, w, sem)
    z = z_ref[0]
    total = jnp.sum(got_ref[...].astype(F32), axis=0)
    g = total[:, :C]
    g_hi, g_lo = hi_lo(jnp.sum(g * g, axis=(0, 1), keepdims=True))
    load.wait()
    w_hi, w_lo = hi_lo(jnp.sum(w[:, C:], axis=(0, 1), keepdims=True))
    row = lax.broadcasted_iota(jnp.int32, (16, EXT), 0)
    lane = lax.broadcasted_iota(jnp.int32, (16, EXT), 1)
    bn_hi, bn_lo = hi_lo(total[0:1, C:])
    ext = jnp.where(row == 0, bn_hi, jnp.where(row == 1, bn_lo, 0.0))
    for k, value in enumerate((g_hi, g_lo, w_hi, w_lo)):
        ext = jnp.where((row == 2) & (lane == k), value, ext)
    step = (g + decay_rate * w[:, :C]).astype(BF)
    out_ref[:, :, :C] = jnp.broadcast_to(step[None], (16, 16, C))
    out_ref[:, :, C:] = jnp.broadcast_to(ext.astype(BF)[None], (16, 16, EXT))
    own_ref[...] = pltpu.roll(g, (16 - 2 * z) & 15, 0)[0:2]


def column_call(z, got, w_rows, bases, after):
    return pl.pallas_call(
        column_kernel,
        in_specs=[SMEM, VMEM] + [ANY] * 5,
        out_specs=[VMEM] * 3,
        out_shape=[
            jax.ShapeDtypeStruct((16, 16, WIDE), BF),
            jax.ShapeDtypeStruct((2, C), F32),
            TOKEN,
        ],
        scratch_shapes=[pltpu.VMEM((16, WIDE), F32), DMA],
        compiler_params=params(),
        cost_estimate=pl.CostEstimate(flops=128 * WIDE, bytes_accessed=1700000, transcendentals=0),
        name="column",
    )(z, got, w_rows, *bases, after)


def basis_kernel(y_ref, b0, b1, b2, b3, m_any, v_any, bnm_any, after_any, base_any, keep_ref, bnm, sems):
    stores = [
        copy(m_any, keep_ref.at[:, pl.ds(0, C)], sems.at[16]),
        copy(v_any, keep_ref.at[:, pl.ds(C, C)], sems.at[17]),
    ]
    load = copy(bnm_any, bnm, sems.at[18])
    for k, block in enumerate((b0, b1, b2, b3)):
        for x in range(4):
            stores.append(copy(block.at[x], base_any.at[4 * x + ((y_ref[0] + k) & 3)], sems.at[4 * k + x]))
    load.wait()
    keep_ref[:, 2 * C :] = jnp.concatenate([bnm[...]] * 16, axis=1)
    for store in stores:
        store.wait()


def basis_call(y, bases, master, momentum, bn_momentum, after):
    return pl.pallas_call(
        basis_kernel,
        in_specs=[SMEM] + [ANY] * 8,
        out_specs=[ANY, VMEM],
        out_shape=[jax.ShapeDtypeStruct((16, 16, WIDE), BF), jax.ShapeDtypeStruct((2, 2 * C + EXT), F32)],
        scratch_shapes=[pltpu.VMEM((2, 8), F32), DMA((19,))],
        compiler_params=params(),
        cost_estimate=pl.CostEstimate(flops=0, bytes_accessed=2200000, transcendentals=0),
        name="basis",
    )(y, *bases, master, momentum, bn_momentum, after)


def update_kernel(
    at_ref, b0, b1, a0, a1, bn_v, g_v, keep,
    nw_any, nbn_ref, nm_ref, nv_ref, nbm_ref, nbv_ref,
    nw, sems,
):
    c = at_ref[0]
    mine = at_ref[1]
    rows = [pl.ds(64 * i, 64) for i in range(4)]
    r = lax.broadcasted_iota(jnp.int32, (128, 128), 0)
    t = lax.broadcasted_iota(jnp.int32, (128, 128), 1)
    want = (
        ((t >> 3) & 1) * 64 + ((t >> 1) & 3) * 16 + ((t >> 4) & 3) * 4 + (c ^ (t >> 6)) * 2 + (t & 1)
    )
    sel = jnp.where(r == want, 1.0, 0.0).astype(BF)

    e0 = b0[:, C:].astype(F32)
    e1 = b1[:, C:].astype(F32)
    row = lax.broadcasted_iota(jnp.int32, (256, EXT), 0) & 15
    lane = lax.broadcasted_iota(jnp.int32, (256, EXT), 1)
    both = jnp.where(row == 2, e0 + e1, 0.0)
    g_sq = jnp.sum(jnp.where(lane < 2, both, 0.0), axis=(0, 1), keepdims=True)
    w_sq = jnp.sum(jnp.where((lane == 2) | (lane == 3), both, 0.0), axis=(0, 1), keepdims=True)

    def rate_of(w_sq, g_sq):
        w_norm = jnp.sqrt(w_sq)
        return learn_rate * (trust_coef * w_norm / (jnp.sqrt(g_sq) + decay_rate * w_norm))

    rate = rate_of(w_sq, g_sq)
    stores = []
    for i in range(4):
        at = slice(64 * i, 64 * i + 64)
        new = jnp.concatenate(
            [
                (a0[at, :C].astype(F32) - rate * b0[at, :C].astype(F32)).astype(BF),
                (a1[at, :C].astype(F32) - rate * b1[at, :C].astype(F32)).astype(BF),
            ],
            axis=0,
        )
        new = jnp.dot(sel, new, preferred_element_type=F32).astype(BF)
        nw[at, :] = new[:64]
        nw[slice(256 + 64 * i, 320 + 64 * i), :] = new[64:]
        stores.append(copy(nw.at[rows[i]], nw_any.at[rows[i]], sems.at[0, i]))
        far_rows = pl.ds(256 + 64 * i, 64)
        stores.append(copy(nw.at[far_rows], nw_any.at[far_rows], sems.at[1, i]))

    def flat(e):
        return jnp.concatenate([e[16 * q : 16 * q + 1] + e[16 * q + 1 : 16 * q + 2] for q in range(16)], axis=1)

    near, far = flat(e0), flat(e1)
    bn_grad = jnp.concatenate([jnp.where(c == 0, near, far), jnp.where(c == 0, far, near)], axis=0)
    bn = bn_v[...]
    bn_rate = rate_of(
        jnp.sum(bn * bn, axis=1, keepdims=True), jnp.sum(bn_grad * bn_grad, axis=1, keepdims=True)
    )
    ends_a = a0[:, C:].astype(F32) + a1[:, C:].astype(F32)
    blocks = [None] * 16
    for x in range(4):
        rows_x = ends_a[64 * x : 64 * x + 16]
        for y in range(1, 4):
            rows_x = rows_x + ends_a[64 * x + 16 * y : 64 * x + 16 * y + 16]
        for high in range(2):
            for half in range(2):
                top = 8 * high + 4 * half
                blocks[8 * high + 2 * x + half] = rows_x[top : top + 2] + rows_x[top + 2 : top + 4]
    bn_base = jnp.concatenate(blocks, axis=1)
    nbn_ref[...] = (bn_base - bn_rate * (bn_grad + decay_rate * bn)).astype(BF)
    master = keep[:, 0:C]
    new_v = momentum_rate * keep[:, C : 2 * C] + rate * (g_v[...] + decay_rate * master)
    nv_ref[...] = new_v
    nm_ref[...] = master - new_v
    lane = lax.broadcasted_iota(jnp.int32, (2, EXT), 1)

    def own_eight(row):
        kept = jnp.where((lane >> 3) == (mine & 15), own_block(row, mine), 0.0)
        eight = kept[:, 0:8]
        for s in range(1, 16):
            eight = eight + kept[:, 8 * s : 8 * s + 8]
        return eight

    own_bn = own_eight(bn)
    new_bnv = momentum_rate * keep[:, 2 * C : 2 * C + 8] + bn_rate * (own_eight(bn_grad) + decay_rate * own_bn)
    nbv_ref[...] = new_bnv
    nbm_ref[...] = own_bn - new_bnv
    for store in stores:
        store.wait()


def update_call(at, b0, b1, a0, a1, bn_params, g_own, keep):
    small = [jax.ShapeDtypeStruct((2, C), F32)] * 2 + [jax.ShapeDtypeStruct((2, 8), F32)] * 2
    return pl.pallas_call(
        update_kernel,
        in_specs=[SMEM] + [VMEM] * 7,
        out_specs=[ANY] + [VMEM] * 5,
        out_shape=[jax.ShapeDtypeStruct((CB, C), BF), jax.ShapeDtypeStruct((2, C), BF)] + small,
        scratch_shapes=[pltpu.VMEM((CB, C), BF), DMA((2, 4))],
        compiler_params=params(),
        cost_estimate=pl.CostEstimate(flops=2 * CB * 128 * C, bytes_accessed=6500000, transcendentals=0),
        name="update",
    )(at, b0, b1, a0, a1, bn_params, g_own, keep)


def exchange(block, axes):
    return lax.all_to_all(block, axes, 0, 0, tiled=True)


def shift_pairs(move):
    out = []
    for i in range(256):
        c, y, zl, x, zh = i & 1, (i >> 1) & 3, (i >> 3) & 3, (i >> 5) & 3, i >> 7
        x, y, z = move(x, y, 4 * zh + zl)
        out.append((i, ((((z >> 2) * 4 + x) * 4 + (z & 3)) * 4 + y) * 2 + c))
    return out


def ring(block, size, move):
    parts = [block]
    for k in range(1, size):
        parts.append(lax.ppermute(block, AXES, shift_pairs(functools.partial(move, size - k))))
    return parts


def number(*values):
    return jnp.stack(values).astype(jnp.int32)


def shards(features, weight, cotangent, pre_act, bn_params, master, momentum, bn_momentum):
    c, x, y, z = (lax.axis_index(axis) for axis in ("c", "x", "y", Z))
    mine = lax.axis_index(AXES)
    swap = functools.partial(lax.ppermute, axis_name=AXES, perm=sibling_pairs())

    stats, piece = stats_call(
        number(mine), features, weight, cotangent, pre_act, master, momentum, bn_params, bn_momentum
    )
    pieces = ring(piece, 4, lambda k, x, y, z: (x, y, (z & 4) + ((z + k) & 3)))
    at, stats = lax.optimization_barrier((number(c, z & 3), stats))
    up, conv, ft = prep_call(at[:1], features, weight, cotangent, pre_act)
    stats = exchange(stats, GX)
    gc, send, own, own_ext, near = grad_call(at, stats, up, conv, ft, bn_params, pieces)
    far = lax.ppermute(near, AXES, shift_pairs(lambda x, y, z: (x, y, z ^ 4)))
    half, token = pair_call(own, own_ext, swap(send))
    base, w_rows = rows_call(number(z >> 2), near, far, token)
    bases = ring(base, 4, lambda k, x, y, z: ((x + k) % 4, y, z))
    part, base, token = plane_call(number(x), exchange(half.reshape(16, 16, WIDE), XY), bases)
    bases = ring(base, 4, lambda k, x, y, z: (x, (y + k) % 4, z))
    grad_input, token = input_call(gc, weight, token)
    step, g_own, token = column_call(number(z), exchange(part, Z), w_rows, bases[1:], token)
    a0, keep = basis_call(number(y), bases, master, momentum, bn_momentum, token)
    a0 = a0.reshape(256, WIDE)
    a1 = swap(a0)
    b0 = exchange(step, XY).reshape(256, WIDE)
    b1 = swap(b0)
    new_weight, new_bn, new_master, new_momentum, new_bn_master, new_bn_momentum = update_call(
        number(c, mine), b0, b1, a0, a1, bn_params, g_own, keep
    )
    return (grad_input, up, new_master, new_momentum, new_weight, new_bn_master, new_bn_momentum, new_bn)


def solution(mesh):
    fine = Mesh(mesh.devices.reshape(SIZES), AXES)
    rows = P(AXES, None)
    cols = P(None, AXES)
    return jax.shard_map(
        shards,
        mesh=fine,
        in_specs=(rows, P(), rows, rows, P(), rows, rows, cols),
        out_specs=(rows, rows, rows, rows, P(), cols, cols, P()),
        check_vma=False,
    )
```

time: 138 us -> 126 us (0.913)
  waiting for transfers between devices: 46 us -> 28.5 us
  local copies, waits for them, and re-layouts: 1.71 us -> 4.02 us
  starting transfers between devices: 59.2 us -> 60.8 us
    ppermute x13 -> x9, waiting for transfers between devices: 26.9 us -> 10.3 us  [ring(): lax.ppermute(block, AXES, shift_pairs(functools.partial(move, size - k)))]
    ppermute x13 -> x9, starting transfers between devices: 24.7 us -> 12.9 us  [ring(): lax.ppermute(block, AXES, shift_pairs(functools.partial(move, size - k)))]
    all_to_all x4, waiting for transfers between devices: 16.8 us -> 8.8 us  [exchange(): return lax.all_to_all(block, axes, 0, 0, tiled=True)]
    ppermute x1 -> x2, waiting for transfers between devices: 0.01 us -> 7.06 us  [the longest x1 4.47 us: shards(): far = lax.ppermute(near, AXES, shift_pairs(lambda x, y, z: (x, y, z ^ 4)))]
    ppermute x1 -> x2, starting transfers between devices: 3.82 us -> 8.14 us  [the longest x1 4.09 us: shards(): far = lax.ppermute(near, AXES, shift_pairs(lambda x, y, z: (x, y, z ^ 4)))]
    ppermute x1, starting transfers between devices: 3.24 us -> 6.46 us  [shards(): b1 = swap(b0)]
    ppermute x1, starting transfers between devices: 0.88 us -> 3.99 us  [shards(): a1 = swap(a0)]
    all_to_all x4, starting transfers between devices: 26.6 us -> 29.3 us  [exchange(): return lax.all_to_all(block, axes, 0, 0, tiled=True)]
  transfers between devices with their start and end apart: 20 -> 17, of which waited for: 11 -> 10; matrix products, arithmetic and copies ran while one was open for 0% -> 0% of each run, Pallas kernels for 4% -> 9%
where the time goes in v3:
time: 126 us
  starting transfers between devices  60.8 us (48%)
  Pallas kernels  30.6 us (24%)
  waiting for transfers between devices  28.5 us (23%)
  local copies, waits for them, and re-layouts  4.02 us (3%)
    all_to_all x4, starting transfers between devices, exchange(): return lax.all_to_all(block, axes, 0, 0, tiled=True)  29.3 us
    ppermute x9, starting transfers between devices, ring(): lax.ppermute(block, AXES, shift_pairs(functools.partial(move, size - k)))  12.9 us
    ppermute x9, waiting for transfers between devices, ring(): lax.ppermute(block, AXES, shift_pairs(functools.partial(move, size - k)))  10.3 us
    all_to_all x4, waiting for transfers between devices, exchange(): return lax.all_to_all(block, axes, 0, 0, tiled=True)  8.8 us
    pallas_call x1, Pallas kernels, grad_call(): pl.pallas_call(grad_kernel, in_specs=[SMEM, VMEM, ANY, ANY, VMEM, ANY] +...  6.51 us
    ppermute x1, starting transfers between devices, shards(): b1 = swap(b0)  6.46 us
    pallas_call x1, Pallas kernels, prep_call(): pl.pallas_call(prep_kernel, in_specs=[SMEM] + [ANY] * 4, out_specs=[ANY,...  6.04 us
    pallas_call x1, Pallas kernels, stats_call(): pl.pallas_call(stats_kernel, in_specs=[SMEM] + [ANY] * 8, out_specs=[VMEM...  4.93 us
  transfers between devices with their start and end apart: 17, of which 10 were waited for; matrix products, arithmetic and copies ran while one was open for 0% of the time, Pallas kernels for 9%

profile of v3, /device:TPU:1, one launch (start us, length us, event | category | flops | bytes accessed | tf_op | source)
XLA Modules:
  0.0 125.7 jit_solution(683811471285861294)
XLA Ops:
  0.7 0.6 pad_add_fusion.at_ref
  1.2 4.9 %stats.1 = (f32[8,4,2048]{2,1,0:T(4,128)}, f32[2,4352]{1,0:T(2,128)}) custom-call(s32[1]{0:T(128)} %bitcast.2.mine_ref, bf16[392,512]{1,0:T(8,128)(2,1)} %f_any.3, bf16[512,2048]{1,0:T(8,128)(2,1)} %w_any.5, bf16[392,2048]{1,0:T(8,128)(2,1)} %cot_any.3, bf16[392,2048]{1,0:T(8,128)(2,1)} %pre_any.3, f32[2,2048]{1,0:T(2,128)} %m_any.3, f32[2,2048]{1,0:T(2,128)} %v_any.3, ...), custom_call_target="tpu_custom_call" | custom-call | flops 822083584 | bytes 7500000 | tf_op jit(solution)/shard_map/stats/pallas_call | solution.py:145
  6.2 11.5 %all-to-all-start = ((f32[8,4,2048]{2,1,0:T(4,128)}), f32[8,4,2048]{2,1,0:T(4,128)S(1)}, u32[]{:S(2)}, u32[]{:S(2)}) async-start(f32[8,4,2048]{2,1,0:T(4,128)} %get-tuple-element.42), calls=%async_computation | async-start | bytes 524288 | tf_op jit(solution)/shard_map/all_to_all | solution.py:581
  17.7 0.7 collective-permute-start.2
  18.4 1.2 collective-permute-start.1
  19.6 1.6 %collective-permute-start = (f32[2,4352]{1,0:T(2,128)}, f32[2,4352]{1,0:T(2,128)S(1)}, u32[]{:S(2)}, u32[]{:S(2)}) collective-permute-start(f32[2,4352]{1,0:T(2,128)} %get-tuple-element.46.p0), channel_id=1, source_target_pairs={{0,24},{1,25},{2,26},{3,27},{4,28},{5,29},{6,30},{7,31},{8,0},{9,1... | collective-permute-start | bytes 104456 | tf_op jit(solution)/shard_map/ppermute | solution.py:596
  21.2 6.0 %prep.1 = (bf16[392,2048]{1,0:T(8,128)(2,1)}, f32[392,2048]{1,0:T(8,128)}, bf16[512,392]{1,0:T(8,128)(2,1)}) custom-call(s32[1]{0:T(128)} %bitcast.15, bf16[392,512]{1,0:T(8,128)(2,1)} %f_any.3, bf16[512,2048]{1,0:T(8,128)(2,1)} %w_any.5, bf16[392,2048]{1,0:T(8,128)(2,1)} %cot_any.3, bf16[392,2048]{1,0:T(8,128)(2,1)} %pre_any.3), custom_call_target="tpu_custom_call" | custom-call | flops 1233125376 | bytes 7500000 | tf_op jit(solution)/shard_map/prep/pallas_call | solution.py:203
  27.3 0.0 collective-permute-done.2.p3
  27.3 0.0 copy-start.10
  27.3 0.0 collective-permute-done.1.p2
  27.3 0.0 copy-start.11
  27.3 0.0 collective-permute-done.p1
  27.3 0.4 all-to-all-done.stat_ref
  27.8 0.1 copy-done.10
  27.9 0.0 copy-done.11
  27.9 0.0 copy-done.12
  27.9 0.5 copy-done.9
  28.5 6.5 %grad.1 = (bf16[392,2048]{1,0:T(8,128)(2,1)}, bf16[256,2176]{1,0:T(8,128)(2,1)}, bf16[256,2048]{1,0:T(8,128)(2,1)}, f32[256,128]{1,0:T(8,128)}, f32[8,4352]{1,0:T(8,128)}) custom-call(s32[2]{0:T(128)} %pad_add_fusion.at_ref, f32[8,4,2048]{2,1,0:T(4,128)} %copy-done.9, bf16[392,2048]{1,0:T(8,128)(2,1)} %get-tuple-element.33.up_any, ...), custom_call_target="tpu_custom_call" | custom-call | flops 822083584 | bytes 9000000 | tf_op jit(solution)/shard_map/grad/pallas_call | solution.py:281
  35.0 4.1 %collective-permute-start.3 = (bf16[256,2176]{1,0:T(8,128)(2,1)}, bf16[256,2176]{1,0:T(8,128)(2,1)S(1)}, u32[]{:S(2)}, u32[]{:S(2)}) collective-permute-start(bf16[256,2176]{1,0:T(8,128)(2,1)} %get-tuple-element.50), channel_id=1, source_target_pairs={{0,1},{1,0},{2,3},{3,2},{4,5},{5,4},{6,7},{7,6},{8,9},{9,8},{10,11... | collective-permute-start | bytes 3342344 | tf_op jit(solution)/shard_map/ppermute | solution.py:618
  39.0 2.6 %collective-permute-done.3.got_ref = bf16[256,2176]{1,0:T(8,128)(2,1)S(1)} collective-permute-done((bf16[256,2176]{1,0:T(8,128)(2,1)}, bf16[256,2176]{1,0:T(8,128)(2,1)S(1)}, u32[]{:S(2)}, u32[]{:S(2)}) %collective-permute-start.3) | collective-permute-done | bytes 1114144 | tf_op jit(solution)/shard_map/ppermute | solution.py:618
  41.6 1.2 copy-done
  42.9 0.9 copy-done.3
  43.8 1.3 %pair.1 = (bf16[256,2176]{1,0:T(8,128)(2,1)}, f32[1,128]{1,0:T(1,128)S(1)}) custom-call(bf16[256,2048]{1,0:T(8,128)(2,1)S(1)} %copy-done, f32[256,128]{1,0:T(8,128)S(1)} %copy-done.3, bf16[256,2176]{1,0:T(8,128)(2,1)S(1)} %collective-permute-done.3.got_ref), custom_call_target="tpu_custom_call" | custom-call | flops 557056 | bytes 4500000 | tf_op jit(solution)/shard_map/pair/pallas_call | solution.py:374
  45.1 5.9 %all-to-all-start.1 = ((bf16[16,16,2176]{2,1,0:T(8,128)(2,1)}), bf16[16,16,2176]{2,1,0:T(8,128)(2,1)S(1)}, u32[]{:S(2)}, u32[]{:S(2)}) async-start(bf16[16,16,2176]{2,1,0:T(8,128)(2,1)} %bitcast.4), calls=%async_computation.1 | async-start | bytes 2228224 | tf_op jit(solution)/shard_map/all_to_all | solution.py:581
  51.0 4.1 %collective-permute-start.4 = (f32[8,4352]{1,0:T(8,128)S(1)}, f32[8,4352]{1,0:T(8,128)S(1)}, u32[]{:S(2)}, u32[]{:S(2)}) collective-permute-start(f32[8,4352]{1,0:T(8,128)S(1)} %copy-done.2), channel_id=1, source_target_pairs={{0,128},{1,129},{2,130},{3,131},{4,132},{5,133},{6,134},{7,135},{8... | collective-permute-start | bytes 417800 | tf_op jit(solution)/shard_map/ppermute | solution.py:617
  55.1 4.5 %collective-permute-done.4.far = f32[8,4352]{1,0:T(8,128)S(1)} collective-permute-done((f32[8,4352]{1,0:T(8,128)S(1)}, f32[8,4352]{1,0:T(8,128)S(1)}, u32[]{:S(2)}, u32[]{:S(2)}) %collective-permute-start.4) | collective-permute-done | bytes 139296 | tf_op jit(solution)/shard_map/ppermute | solution.py:617
  59.5 0.2 rows.1
  59.8 1.1 collective-permute-start.7
  60.9 2.4 %collective-permute-start.6 = (bf16[16,2176]{1,0:T(8,128)(2,1)S(1)}, bf16[16,2176]{1,0:T(8,128)(2,1)S(1)}, u32[]{:S(2)}, u32[]{:S(2)}) collective-permute-start(bf16[16,2176]{1,0:T(8,128)(2,1)S(1)} %get-tuple-element.54.b0), channel_id=1, source_target_pairs={{0,64},{1,65},{2,66},{3,67},{4,68},{5,69},{6,70},{7,71},{8,72},{9,... | collective-permute-start | bytes 208904 | tf_op jit(solution)/shard_map/ppermute | solution.py:596
  63.3 1.2 collective-permute-start.5
  64.4 2.5 %collective-permute-done.7.b3 = bf16[16,2176]{1,0:T(8,128)(2,1)S(1)} collective-permute-done((bf16[16,2176]{1,0:T(8,128)(2,1)S(1)}, bf16[16,2176]{1,0:T(8,128)(2,1)S(1)}, u32[]{:S(2)}, u32[]{:S(2)}) %collective-permute-start.7) | collective-permute-done | bytes 69664 | tf_op jit(solution)/shard_map/ppermute | solution.py:596
  67.0 2.1 %collective-permute-done.6.b2 = bf16[16,2176]{1,0:T(8,128)(2,1)S(1)} collective-permute-done((bf16[16,2176]{1,0:T(8,128)(2,1)S(1)}, bf16[16,2176]{1,0:T(8,128)(2,1)S(1)}, u32[]{:S(2)}, u32[]{:S(2)}) %collective-permute-start.6) | collective-permute-done | bytes 69664 | tf_op jit(solution)/shard_map/ppermute | solution.py:596
  69.1 0.0 collective-permute-done.5.b1
  69.1 0.0 all-to-all-done.1.got_ref
  69.1 1.4 %plane.1 = (bf16[8,16,2176]{2,1,0:T(8,128)(2,1)}, bf16[4,16,2176]{2,1,0:T(8,128)(2,1)S(1)}, f32[1,128]{1,0:T(1,128)S(1)}) custom-call(s32[1]{0:T(128)} %bitcast.3.x_ref, bf16[16,16,2176]{2,1,0:T(8,128)(2,1)S(1)} %all-to-all-done.1.got_ref, bf16[16,2176]{1,0:T(8,128)(2,1)S(1)} %get-tuple-element.54.b0, bf16[16,2176]{1,0:T(8,128)(2,1)S(1)} %collective-permute-done.5.b1, ...), custom_call_target="tpu_custom_call" | custom-call | flops 557056 | bytes 1700000 | tf_op jit(solution)/shard_map/plane/pallas_call | solution.py:397
  70.4 0.0 copy-start.8
  70.5 0.5 copy-done.8
  71.0 5.9 %all-to-all-start.2 = ((bf16[8,16,2176]{2,1,0:T(8,128)(2,1)}), bf16[8,16,2176]{2,1,0:T(8,128)(2,1)S(1)}, u32[]{:S(2)}, u32[]{:S(2)}) async-start(bf16[8,16,2176]{2,1,0:T(8,128)(2,1)} %get-tuple-element.57), calls=%async_computation.2 | async-start | bytes 1114112 | tf_op jit(solution)/shard_map/all_to_all | solution.py:581
  76.9 1.1 collective-permute-start.10
  78.0 2.4 %collective-permute-start.9 = (bf16[4,16,2176]{2,1,0:T(8,128)(2,1)S(1)}, bf16[4,16,2176]{2,1,0:T(8,128)(2,1)S(1)}, u32[]{:S(2)}, u32[]{:S(2)}) collective-permute-start(bf16[4,16,2176]{2,1,0:T(8,128)(2,1)S(1)} %get-tuple-element.59.b0), channel_id=1, source_target_pairs={{0,4},{1,5},{2,6},{3,7},{4,0},{5,1},{6,2},{7,3},{8,12},{9,13},{10,... | collective-permute-start | bytes 835592 | tf_op jit(solution)/shard_map/ppermute | solution.py:596
  80.3 1.2 collective-permute-start.8
  81.5 3.5 %ginput.1 = (bf16[392,512]{1,0:T(8,128)(2,1)}, f32[1,128]{1,0:T(1,128)}) custom-call(bf16[392,2048]{1,0:T(8,128)(2,1)} %get-tuple-element.47.gc_any, bf16[512,2048]{1,0:T(8,128)(2,1)} %w_any.5, f32[1,128]{1,0:T(1,128)} %copy-done.8), custom_call_target="tpu_custom_call" | custom-call | flops 822083584 | bytes 4000000 | tf_op jit(solution)/shard_map/ginput/pallas_call | solution.py:329
  85.0 0.0 collective-permute-done.10.b3
  85.0 5.2 %collective-permute-done.9.b2 = bf16[4,16,2176]{2,1,0:T(8,128)(2,1)S(1)} collective-permute-done((bf16[4,16,2176]{2,1,0:T(8,128)(2,1)S(1)}, bf16[4,16,2176]{2,1,0:T(8,128)(2,1)S(1)}, u32[]{:S(2)}, u32[]{:S(2)}) %collective-permute-start.9) | collective-permute-done | bytes 278560 | tf_op jit(solution)/shard_map/ppermute | solution.py:596
  90.3 0.5 collective-permute-done.8.b1
  90.7 1.8 %all-to-all-done.2.got_ref = bf16[8,16,2176]{2,1,0:T(8,128)(2,1)S(1)} async-done(((bf16[8,16,2176]{2,1,0:T(8,128)(2,1)}), bf16[8,16,2176]{2,1,0:T(8,128)(2,1)S(1)}, u32[]{:S(2)}, u32[]{:S(2)}) %all-to-all-start.2) | async-done | bytes 557088 | tf_op jit(solution)/shard_map/all_to_all | solution.py:581
  92.6 0.7 copy-done.7
  93.2 1.5 %column.1 = (bf16[16,16,2176]{2,1,0:T(8,128)(2,1)}, f32[2,2048]{1,0:T(2,128)S(1)}, f32[1,128]{1,0:T(1,128)S(1)}) custom-call(s32[1]{0:T(128)} %bitcast.6.z_ref, bf16[8,16,2176]{2,1,0:T(8,128)(2,1)S(1)} %all-to-all-done.2.got_ref, f32[16,2176]{1,0:T(8,128)S(1)} %get-tuple-element.58.w_any, bf16[4,16,2176]{2,1,0:T(8,128)(2,1)S(1)} %collective-permute-done.8.b1, ...), custom_call_target="tpu_custom_call" | custom-call | flops 278528 | bytes 1700000 | tf_op jit(solution)/shard_map/column/pallas_call | solution.py:435
  94.7 0.0 copy-start.4
  94.7 0.0 copy-start.5
  94.8 0.0 copy-start.6
  94.8 6.0 %all-to-all-start.3 = ((bf16[16,16,2176]{2,1,0:T(8,128)(2,1)}), bf16[16,16,2176]{2,1,0:T(8,128)(2,1)S(1)}, u32[]{:S(2)}, u32[]{:S(2)}) async-start(bf16[16,16,2176]{2,1,0:T(8,128)(2,1)} %get-tuple-element.61), calls=%async_computation.3 | async-start | bytes 2228224 | tf_op jit(solution)/shard_map/all_to_all | solution.py:581
  100.8 0.0 copy-start.1
  100.8 0.0 copy-done.4
  100.8 0.0 copy-done.5
  100.9 0.0 copy-done.6
  100.9 1.9 %basis.1 = (bf16[16,16,2176]{2,1,0:T(8,128)(2,1)S(1)}, f32[2,4224]{1,0:T(2,128)S(1)}) custom-call(s32[1]{0:T(128)} %bitcast.8.y_ref, bf16[4,16,2176]{2,1,0:T(8,128)(2,1)S(1)} %get-tuple-element.59.b0, bf16[4,16,2176]{2,1,0:T(8,128)(2,1)S(1)} %collective-permute-done.8.b1, bf16[4,16,2176]{2,1,0:T(8,128)(2,1)S(1)} %collective-permute-done.9.b2, ...), custom_call_target="tpu_custom_call" | custom-call | bytes 2200000 | tf_op jit(solution)/shard_map/basis/pallas_call | solution.py:467
  102.7 4.0 %collective-permute-start.12 = (bf16[256,2176]{1,0:T(8,128)(2,1)S(1)}, bf16[256,2176]{1,0:T(8,128)(2,1)S(1)}, u32[]{:S(2)}, u32[]{:S(2)}) collective-permute-start(bf16[256,2176]{1,0:T(8,128)(2,1)S(1)} %bitcast.13), channel_id=1, source_target_pairs={{0,1},{1,0},{2,3},{3,2},{4,5},{5,4},{6,7},{7,6},{8,9},{9,8},{10,11... | collective-permute-start | bytes 3342344 | tf_op jit(solution)/shard_map/ppermute | solution.py:627
  106.7 6.5 %all-to-all-done.3 = bf16[16,16,2176]{2,1,0:T(8,128)(2,1)S(1)} async-done(((bf16[16,16,2176]{2,1,0:T(8,128)(2,1)}), bf16[16,16,2176]{2,1,0:T(8,128)(2,1)S(1)}, u32[]{:S(2)}, u32[]{:S(2)}) %all-to-all-start.3) | async-done | bytes 1114144 | tf_op jit(solution)/shard_map/all_to_all | solution.py:581
  113.3 6.5 %collective-permute-start.11 = (bf16[256,2176]{1,0:T(8,128)(2,1)S(1)}, bf16[256,2176]{1,0:T(8,128)(2,1)S(1)}, u32[]{:S(2)}, u32[]{:S(2)}) collective-permute-start(bf16[256,2176]{1,0:T(8,128)(2,1)S(1)} %bitcast.11), channel_id=1, source_target_pairs={{0,1},{1,0},{2,3},{3,2},{4,5},{5,4},{6,7},{7,6},{8,9},{9,8},{10,11... | collective-permute-start | bytes 3342344 | tf_op jit(solution)/shard_map/ppermute | solution.py:629
  119.7 0.1 pad_add_fusion.1.at_ref
  119.8 0.0 collective-permute-done.12.a1
  119.8 2.3 %collective-permute-done.11.b1 = bf16[256,2176]{1,0:T(8,128)(2,1)S(1)} collective-permute-done((bf16[256,2176]{1,0:T(8,128)(2,1)S(1)}, bf16[256,2176]{1,0:T(8,128)(2,1)S(1)}, u32[]{:S(2)}, u32[]{:S(2)}) %collective-permute-start.11) | collective-permute-done | bytes 1114144 | tf_op jit(solution)/shard_map/ppermute | solution.py:629
  122.1 3.4 %update.1 = (bf16[512,2048]{1,0:T(8,128)(2,1)}, bf16[2,2048]{1,0:T(2,128)(2,1)}, f32[2,2048]{1,0:T(2,128)}, f32[2,2048]{1,0:T(2,128)}, f32[2,8]{1,0:T(2,128)}, /*index=5*/f32[2,8]{1,0:T(2,128)}) custom-call(s32[2]{0:T(128)S(1)} %pad_add_fusion.1.at_ref, bf16[256,2176]{1,0:T(8,128)(2,1)S(1)} %bitcast.12, bf16[256,2176]{1,0:T(8,128)(2,1)S(1)} %collective-permute-done.11.b1, ...), custom_call_target="tpu_custom_call" | custom-call | flops 268435456 | bytes 6500000 | tf_op jit(solution)/shard_map/update/pallas_call | solution.py:568
  (8 shorter events, 0.0 us)
Async XLA Ops:
  6.2 21.6 %all-to-all-start = ((f32[8,4,2048]{2,1,0:T(4,128)}), f32[8,4,2048]{2,1,0:T(4,128)S(1)}, u32[]{:S(2)}, u32[]{:S(2)}) async-start(f32[8,4,2048]{2,1,0:T(4,128)} %get-tuple-element.42), calls=%async_computation | async-start | bytes 524288 | tf_op jit(solution)/shard_map/all_to_all | solution.py:581
  17.7 9.6 %collective-permute-start.2 = (f32[2,4352]{1,0:T(2,128)}, f32[2,4352]{1,0:T(2,128)S(1)}, u32[]{:S(2)}, u32[]{:S(2)}) collective-permute-start(f32[2,4352]{1,0:T(2,128)} %get-tuple-element.46.p0), channel_id=1, source_target_pairs={{0,8},{1,9},{2,10},{3,11},{4,12},{5,13},{6,14},{7,15},{8,16},{9,17... | collective-permute-start | bytes 104456 | tf_op jit(solution)/shard_map/ppermute | solution.py:596
  18.4 8.9 %collective-permute-start.1 = (f32[2,4352]{1,0:T(2,128)}, f32[2,4352]{1,0:T(2,128)S(1)}, u32[]{:S(2)}, u32[]{:S(2)}) collective-permute-start(f32[2,4352]{1,0:T(2,128)} %get-tuple-element.46.p0), channel_id=1, source_target_pairs={{0,16},{1,17},{2,18},{3,19},{4,20},{5,21},{6,22},{7,23},{8,24},{9,... | collective-permute-start | bytes 104456 | tf_op jit(solution)/shard_map/ppermute | solution.py:596
  19.6 7.7 %collective-permute-start = (f32[2,4352]{1,0:T(2,128)}, f32[2,4352]{1,0:T(2,128)S(1)}, u32[]{:S(2)}, u32[]{:S(2)}) collective-permute-start(f32[2,4352]{1,0:T(2,128)} %get-tuple-element.46.p0), channel_id=1, source_target_pairs={{0,24},{1,25},{2,26},{3,27},{4,28},{5,29},{6,30},{7,31},{8,0},{9,1... | collective-permute-start | bytes 104456 | tf_op jit(solution)/shard_map/ppermute | solution.py:596
  27.3 0.6 copy-start.10
  27.3 0.6 copy-start.11
  27.3 0.6 copy-start.12
  27.8 0.7 copy-start.9
  35.0 6.6 %collective-permute-start.3 = (bf16[256,2176]{1,0:T(8,128)(2,1)}, bf16[256,2176]{1,0:T(8,128)(2,1)S(1)}, u32[]{:S(2)}, u32[]{:S(2)}) collective-permute-start(bf16[256,2176]{1,0:T(8,128)(2,1)} %get-tuple-element.50), channel_id=1, source_target_pairs={{0,1},{1,0},{2,3},{3,2},{4,5},{5,4},{6,7},{7,6},{8,9},{9,8},{10,11... | collective-permute-start | bytes 3342344 | tf_op jit(solution)/shard_map/ppermute | solution.py:618
  41.6 1.2 copy-start
  42.9 0.9 copy-start.3
  45.1 5.9 %copy-start.2 = (f32[8,4352]{1,0:T(8,128)S(1)}, f32[8,4352]{1,0:T(8,128)}, u32[]{:S(2)}) copy-start(f32[8,4352]{1,0:T(8,128)} %get-tuple-element.52.near) | copy-start | bytes 417796
  45.1 24.0 %all-to-all-start.1 = ((bf16[16,16,2176]{2,1,0:T(8,128)(2,1)}), bf16[16,16,2176]{2,1,0:T(8,128)(2,1)S(1)}, u32[]{:S(2)}, u32[]{:S(2)}) async-start(bf16[16,16,2176]{2,1,0:T(8,128)(2,1)} %bitcast.4), calls=%async_computation.1 | async-start | bytes 2228224 | tf_op jit(solution)/shard_map/all_to_all | solution.py:581
  51.0 8.6 %collective-permute-start.4 = (f32[8,4352]{1,0:T(8,128)S(1)}, f32[8,4352]{1,0:T(8,128)S(1)}, u32[]{:S(2)}, u32[]{:S(2)}) collective-permute-start(f32[8,4352]{1,0:T(8,128)S(1)} %copy-done.2), channel_id=1, source_target_pairs={{0,128},{1,129},{2,130},{3,131},{4,132},{5,133},{6,134},{7,135},{8... | collective-permute-start | bytes 417800 | tf_op jit(solution)/shard_map/ppermute | solution.py:617
  59.8 7.2 %collective-permute-start.7 = (bf16[16,2176]{1,0:T(8,128)(2,1)S(1)}, bf16[16,2176]{1,0:T(8,128)(2,1)S(1)}, u32[]{:S(2)}, u32[]{:S(2)}) collective-permute-start(bf16[16,2176]{1,0:T(8,128)(2,1)S(1)} %get-tuple-element.54.b0), channel_id=1, source_target_pairs={{0,32},{1,33},{2,34},{3,35},{4,36},{5,37},{6,38},{7,39},{8,40},{9,... | collective-permute-start | bytes 208904 | tf_op jit(solution)/shard_map/ppermute | solution.py:596
  60.9 8.2 %collective-permute-start.6 = (bf16[16,2176]{1,0:T(8,128)(2,1)S(1)}, bf16[16,2176]{1,0:T(8,128)(2,1)S(1)}, u32[]{:S(2)}, u32[]{:S(2)}) collective-permute-start(bf16[16,2176]{1,0:T(8,128)(2,1)S(1)} %get-tuple-element.54.b0), channel_id=1, source_target_pairs={{0,64},{1,65},{2,66},{3,67},{4,68},{5,69},{6,70},{7,71},{8,72},{9,... | collective-permute-start | bytes 208904 | tf_op jit(solution)/shard_map/ppermute | solution.py:596
  63.3 5.8 %collective-permute-start.5 = (bf16[16,2176]{1,0:T(8,128)(2,1)S(1)}, bf16[16,2176]{1,0:T(8,128)(2,1)S(1)}, u32[]{:S(2)}, u32[]{:S(2)}) collective-permute-start(bf16[16,2176]{1,0:T(8,128)(2,1)S(1)} %get-tuple-element.54.b0), channel_id=1, source_target_pairs={{0,96},{1,97},{2,98},{3,99},{4,100},{5,101},{6,102},{7,103},{8,104... | collective-permute-start | bytes 208904 | tf_op jit(solution)/shard_map/ppermute | solution.py:596
  70.4 0.5 copy-start.8
  71.0 21.6 %all-to-all-start.2 = ((bf16[8,16,2176]{2,1,0:T(8,128)(2,1)}), bf16[8,16,2176]{2,1,0:T(8,128)(2,1)S(1)}, u32[]{:S(2)}, u32[]{:S(2)}) async-start(bf16[8,16,2176]{2,1,0:T(8,128)(2,1)} %get-tuple-element.57), calls=%async_computation.2 | async-start | bytes 1114112 | tf_op jit(solution)/shard_map/all_to_all | solution.py:581
  76.9 8.2 %collective-permute-start.10 = (bf16[4,16,2176]{2,1,0:T(8,128)(2,1)S(1)}, bf16[4,16,2176]{2,1,0:T(8,128)(2,1)S(1)}, u32[]{:S(2)}, u32[]{:S(2)}) collective-permute-start(bf16[4,16,2176]{2,1,0:T(8,128)(2,1)S(1)} %get-tuple-element.59.b0), channel_id=1, source_target_pairs={{0,2},{1,3},{2,4},{3,5},{4,6},{5,7},{6,0},{7,1},{8,10},{9,11},{10,... | collective-permute-start | bytes 835592 | tf_op jit(solution)/shard_map/ppermute | solution.py:596
  78.0 12.3 %collective-permute-start.9 = (bf16[4,16,2176]{2,1,0:T(8,128)(2,1)S(1)}, bf16[4,16,2176]{2,1,0:T(8,128)(2,1)S(1)}, u32[]{:S(2)}, u32[]{:S(2)}) collective-permute-start(bf16[4,16,2176]{2,1,0:T(8,128)(2,1)S(1)} %get-tuple-element.59.b0), channel_id=1, source_target_pairs={{0,4},{1,5},{2,6},{3,7},{4,0},{5,1},{6,2},{7,3},{8,12},{9,13},{10,... | collective-permute-start | bytes 835592 | tf_op jit(solution)/shard_map/ppermute | solution.py:596
  80.3 10.4 %collective-permute-start.8 = (bf16[4,16,2176]{2,1,0:T(8,128)(2,1)S(1)}, bf16[4,16,2176]{2,1,0:T(8,128)(2,1)S(1)}, u32[]{:S(2)}, u32[]{:S(2)}) collective-permute-start(bf16[4,16,2176]{2,1,0:T(8,128)(2,1)S(1)} %get-tuple-element.59.b0), channel_id=1, source_target_pairs={{0,6},{1,7},{2,0},{3,1},{4,2},{5,3},{6,4},{7,5},{8,14},{9,15},{10,... | collective-permute-start | bytes 835592 | tf_op jit(solution)/shard_map/ppermute | solution.py:596
  92.6 0.7 copy-start.7
  94.7 6.1 %copy-start.4 = (f32[2,2048]{1,0:T(2,128)S(1)}, f32[2,2048]{1,0:T(2,128)}, u32[]{:S(2)}) copy-start(f32[2,2048]{1,0:T(2,128)} %m_any.3) | copy-start | bytes 49156
  94.7 6.1 %copy-start.5 = (f32[2,2048]{1,0:T(2,128)S(1)}, f32[2,2048]{1,0:T(2,128)}, u32[]{:S(2)}) copy-start(f32[2,2048]{1,0:T(2,128)} %v_any.3) | copy-start | bytes 49156
  94.8 6.1 %copy-start.6 = (f32[2,8]{1,0:T(2,128)S(1)}, f32[2,8]{1,0:T(2,128)}, u32[]{:S(2)}) copy-start(f32[2,8]{1,0:T(2,128)} %bnm_any.3) | copy-start | bytes 196
  94.8 18.5 %all-to-all-start.3 = ((bf16[16,16,2176]{2,1,0:T(8,128)(2,1)}), bf16[16,16,2176]{2,1,0:T(8,128)(2,1)S(1)}, u32[]{:S(2)}, u32[]{:S(2)}) async-start(bf16[16,16,2176]{2,1,0:T(8,128)(2,1)} %get-tuple-element.61), calls=%async_computation.3 | async-start | bytes 2228224 | tf_op jit(solution)/shard_map/all_to_all | solution.py:581
  100.8 21.3 %copy-start.1 = (f32[2,2048]{1,0:T(2,128)S(1)}, f32[2,2048]{1,0:T(2,128)}, u32[]{:S(2)}) copy-start(f32[2,2048]{1,0:T(2,128)} %bn_v.1) | copy-start | bytes 49156
  102.7 17.1 %collective-permute-start.12 = (bf16[256,2176]{1,0:T(8,128)(2,1)S(1)}, bf16[256,2176]{1,0:T(8,128)(2,1)S(1)}, u32[]{:S(2)}, u32[]{:S(2)}) collective-permute-start(bf16[256,2176]{1,0:T(8,128)(2,1)S(1)} %bitcast.13), channel_id=1, source_target_pairs={{0,1},{1,0},{2,3},{3,2},{4,5},{5,4},{6,7},{7,6},{8,9},{9,8},{10,11... | collective-permute-start | bytes 3342344 | tf_op jit(solution)/shard_map/ppermute | solution.py:627
  113.3 8.8 %collective-permute-start.11 = (bf16[256,2176]{1,0:T(8,128)(2,1)S(1)}, bf16[256,2176]{1,0:T(8,128)(2,1)S(1)}, u32[]{:S(2)}, u32[]{:S(2)}) collective-permute-start(bf16[256,2176]{1,0:T(8,128)(2,1)S(1)} %bitcast.11), channel_id=1, source_target_pairs={{0,1},{1,0},{2,3},{3,2},{4,5},{5,4},{6,7},{7,6},{8,9},{9,8},{10,11... | collective-permute-start | bytes 3342344 | tf_op jit(solution)/shard_map/ppermute | solution.py:629

commit v4 on v3

v4 whole, which is shorter than its diff:
```python
import functools

import jax
import jax.numpy as jnp
from jax import lax
from jax.experimental import pallas as pl
from jax.experimental.pallas import tpu as pltpu
from jax.sharding import Mesh, PartitionSpec as P

eps_norm = 1e-05
momentum_rate = 0.9
learn_rate = 4.0
trust_coef = 0.001
decay_rate = 5e-05

AXES = ("zh", "x", "zl", "y", "c")
SIZES = (2, 4, 4, 4, 2)
GX = ("zh", "x")
XY = ("x", "y")
Z = ("zh", "zl")
BF = jnp.bfloat16
F32 = jnp.float32

ROWS = 392
CB = 512
C = 2048
EXT = 128
WIDE = C + EXT
PIECE = 2 * C + 2 * EXT
COLS = 512
STEPS = C // COLS
STAT_COLS = 1024
STAT_STEPS = C // STAT_COLS
COUNT = float(ROWS * 8)
TALL = 400
KEPT = 2 * TALL + CB // 4
VMEM_BYTES = 24 * 1024 * 1024
VMEM_ALL = 60 * 1024 * 1024


def sibling_pairs():
    return [(i, i ^ 1) for i in range(256)]


def natural_row(t, c):
    cc = c ^ (t >> 8)
    return (
        ((t >> 3) & 1) * 256
        + ((t >> 6) & 3) * 64
        + ((t >> 1) & 3) * 16
        + ((t >> 4) & 3) * 4
        + cc * 2
        + (t & 1)
    )


def hi_lo(v):
    hi = v.astype(BF).astype(F32)
    return hi, v - hi


def params(limit=VMEM_BYTES):
    return pltpu.CompilerParams(vmem_limit_bytes=limit)


ANY = pl.BlockSpec(memory_space=pl.ANY)
VMEM = pl.BlockSpec(memory_space=pltpu.VMEM)
SMEM = pl.BlockSpec(memory_space=pltpu.SMEM)
DMA = pltpu.SemaphoreType.DMA


TOKEN = jax.ShapeDtypeStruct((1,), jnp.int32)


def done(token_ref):
    token_ref[0] = 0


def copy(src, dst, sem):
    made = pltpu.make_async_copy(src, dst, sem)
    made.start()
    return made


def cols(j):
    return pl.ds(j * COLS, COLS)


def stat_cols(j):
    return pl.ds(j * STAT_COLS, STAT_COLS)


def place():
    at = lax.axis_index("zh")
    for axis, size in zip(AXES[1:], SIZES[1:]):
        at = at * size + lax.axis_index(axis)
    return at


def own_block(row, mine):
    block = jnp.zeros((2, EXT), F32)
    for q in range(16):
        block = jnp.where((mine >> 4) == q, row[:, EXT * q : EXT * q + EXT], block)
    return block


def stats_kernel(
    f_any, w_any, cot_any, pre_any, m_any, v_any, bn_any, bnm_any,
    stat_ref, base_ref,
    f, w, cot, pre, master, momentum, bn, bnm, sems,
):
    mine = place()
    first = copy(f_any, f, sems.at[0, STAT_STEPS])
    loads = []
    for j in range(STAT_STEPS):
        loads.append(
            [
                copy(w_any.at[:, stat_cols(j)], w.at[:, stat_cols(j)], sems.at[0, j]),
                copy(cot_any.at[:, stat_cols(j)], cot.at[:, stat_cols(j)], sems.at[1, j]),
                copy(pre_any.at[:, stat_cols(j)], pre.at[:, stat_cols(j)], sems.at[2, j]),
            ]
        )
    small = [
        copy(m_any, master, sems.at[1, STAT_STEPS]),
        copy(v_any, momentum, sems.at[2, STAT_STEPS]),
        copy(bn_any, bn, sems.at[3, STAT_STEPS]),
        copy(bnm_any, bnm, sems.at[4, 0]),
    ]
    first.wait()
    for j in range(STAT_STEPS):
        loads[j][0].wait()
        conv = jnp.dot(f[...], w[:, stat_cols(j)], preferred_element_type=F32)
        loads[j][1].wait()
        loads[j][2].wait()
        u = jnp.where(pre[:, stat_cols(j)].astype(F32) > 0, cot[:, stat_cols(j)].astype(F32), 0.0)
        stat = jnp.concatenate(
            [
                jnp.sum(conv, axis=0, keepdims=True),
                jnp.sum(conv * conv, axis=0, keepdims=True),
                jnp.sum(u, axis=0, keepdims=True),
                jnp.sum(u * conv, axis=0, keepdims=True),
            ],
            axis=0,
        )
        stat_ref[:, :, stat_cols(j)] = jnp.broadcast_to(stat[None], (8, 4, STAT_COLS))
    for load in small:
        load.wait()
    base_ref[:, 0:C] = master[...] - momentum_rate * momentum[...]
    base_ref[:, C : 2 * C] = master[...]
    own_bn = own_block(bn[...], mine)
    lane = lax.broadcasted_iota(jnp.int32, (2, EXT), 1)
    bn_base = own_bn - momentum_rate * jnp.concatenate([bnm[...]] * 16, axis=1)
    base_ref[:, 2 * C : 2 * C + EXT] = jnp.where((lane >> 3) == (mine & 15), bn_base, 0.0)
    square = jnp.sum(master[...] * master[...], axis=(0, 1), keepdims=True)
    row = lax.broadcasted_iota(jnp.int32, (2, EXT), 0)
    hi, lo = hi_lo(square)
    square = jnp.where(lane == 0, hi, jnp.where(lane == 1, lo, 0.0))
    base_ref[:, 2 * C + EXT :] = jnp.where(row == 0, square, 0.0)


def stats_call(features, weight, cotangent, pre_act, master, momentum, bn_params, bn_momentum):
    return pl.pallas_call(
        stats_kernel,
        in_specs=[ANY] * 8,
        out_specs=[VMEM, VMEM],
        out_shape=[
            jax.ShapeDtypeStruct((8, 4, C), F32),
            jax.ShapeDtypeStruct((2, PIECE), F32),
        ],
        scratch_shapes=[
            pltpu.VMEM((ROWS, CB), BF),
            pltpu.VMEM((CB, C), BF),
            pltpu.VMEM((ROWS, C), BF),
            pltpu.VMEM((ROWS, C), BF),
            pltpu.VMEM((2, C), F32),
            pltpu.VMEM((2, C), F32),
            pltpu.VMEM((2, C), F32),
            pltpu.VMEM((2, 8), F32),
            DMA((5, STAT_STEPS + 1)),
        ],
        compiler_params=params(VMEM_ALL),
        cost_estimate=pl.CostEstimate(flops=2 * ROWS * CB * C, bytes_accessed=7500000, transcendentals=0),
        name="stats",
    )(features, weight, cotangent, pre_act, master, momentum, bn_params, bn_momentum)


def prep_kernel(
    f_any, w_any, cot_any, pre_any, up_any, kept_any, f, w, cot, pre, up, tall, mid, ft, sems
):
    first = copy(f_any, f, sems.at[5, 0])
    loads = [
        [
            copy(w_any.at[:, cols(j)], w.at[:, cols(j)], sems.at[0, j]),
            copy(cot_any.at[:, cols(j)], cot.at[:, cols(j)], sems.at[1, j]),
            copy(pre_any.at[:, cols(j)], pre.at[:, cols(j)], sems.at[2, j]),
        ]
        for j in range(STEPS)
    ]
    t = lax.broadcasted_iota(jnp.int32, (CB, CB), 0)
    r = lax.broadcasted_iota(jnp.int32, (CB, CB), 1)
    sel = jnp.where(r == natural_row(t, lax.axis_index("c")), 1.0, 0.0).astype(BF)
    first.wait()
    ft[...] = jnp.zeros_like(ft)
    got = lax.dot_general(sel, f[...], (((1,), (1,)), ((), ())), preferred_element_type=F32).astype(BF)
    for b in range(4):
        ft[:, CB * b : CB * b + ROWS] = got[128 * b : 128 * b + 128]
    blank = jnp.zeros((TALL - ROWS, COLS), F32)
    stores = [copy(ft, kept_any.at[pl.ds(2 * TALL, CB // 4)], sems.at[5, 1])]
    for j in range(STEPS):
        loads[j][0].wait()
        conv = jnp.dot(f[...], w[:, cols(j)], preferred_element_type=F32)
        centre = jnp.sum(conv, axis=0, keepdims=True) / ROWS
        mid[:, cols(j)] = jnp.concatenate([conv - centre, blank], axis=0).astype(BF)
        stores.append(copy(mid.at[:, cols(j)], kept_any.at[pl.ds(TALL, TALL), cols(j)], sems.at[4, j]))
        loads[j][1].wait()
        loads[j][2].wait()
        u = jnp.where(pre[:, cols(j)].astype(F32) > 0, cot[:, cols(j)].astype(F32), 0.0)
        up[:, cols(j)] = u.astype(BF)
        stores.append(copy(up.at[:, cols(j)], up_any.at[:, cols(j)], sems.at[3, j]))
        tall[:, cols(j)] = jnp.concatenate([u, blank], axis=0).astype(BF)
        stores.append(copy(tall.at[:, cols(j)], kept_any.at[pl.ds(0, TALL), cols(j)], sems.at[6, j]))
    for store in stores:
        store.wait()


def prep_call(features, weight, cotangent, pre_act):
    return pl.pallas_call(
        prep_kernel,
        in_specs=[ANY] * 4,
        out_specs=[ANY, ANY],
        out_shape=[
            jax.ShapeDtypeStruct((ROWS, C), BF),
            jax.ShapeDtypeStruct((KEPT, C), BF),
        ],
        scratch_shapes=[
            pltpu.VMEM((ROWS, CB), BF),
            pltpu.VMEM((CB, C), BF),
            pltpu.VMEM((ROWS, C), BF),
            pltpu.VMEM((ROWS, C), BF),
            pltpu.VMEM((ROWS, C), BF),
            pltpu.VMEM((TALL, C), BF),
            pltpu.VMEM((TALL, C), BF),
            pltpu.VMEM((CB // 4, C), BF),
            DMA((7, STEPS)),
        ],
        compiler_params=params(VMEM_ALL),
        cost_estimate=pl.CostEstimate(flops=3 * ROWS * CB * C, bytes_accessed=9000000, transcendentals=0),
        name="prep",
    )(features, weight, cotangent, pre_act)


def grad_of(up, mid, coef):
    return (coef[0:1] * (up.astype(F32) - coef[1:2]) - (mid.astype(F32) + coef[2:3]) * coef[3:4]).astype(BF)


def grad_kernel(
    stat, kept, bn, p0, p1, send, own, near_ref, coef_ref, ext_send, ext_own
):
    c, zh = lax.axis_index("c"), lax.axis_index("zh")
    up = kept.at[0:TALL]
    mid = kept.at[TALL : 2 * TALL]
    low = jnp.where(zh == 0, p0[...], p1[...])
    high = jnp.where(zh == 0, p1[...], p0[...])
    near_ref[...] = jnp.concatenate([low, high], axis=0).astype(BF)
    sums = jnp.sum(stat[...], axis=0)
    mean = sums[0:1] / COUNT
    inv_std = lax.rsqrt(sums[1:2] / COUNT - mean * mean + eps_norm)
    sum_b = sums[2:3]
    sum_g = inv_std * (sums[3:4] - mean * sum_b)
    alpha = bn[0:1] * inv_std
    slope = alpha * inv_std * (sum_g / COUNT)
    shift = sum_b / COUNT
    centre = stat[4 * zh + lax.axis_index("x")][0:1] / ROWS
    coef = jnp.concatenate([alpha, shift, centre - mean, slope], axis=0)
    coef_ref[...] = coef
    scale_row = sum_g * 0.125
    shift_row = sum_b * 0.125
    mine = jnp.where(c == 0, scale_row, shift_row)
    other = jnp.where(c == 0, shift_row, scale_row)
    ext_send[...] = jnp.zeros_like(ext_send)
    ext_own[...] = jnp.zeros_like(ext_own)
    for q in range(16):
        ext_own[16 * q : 16 * q + 1, :] = mine[:, 128 * q : 128 * q + 128]
        ext_send[16 * q : 16 * q + 1, :] = other[:, 128 * q : 128 * q + 128]
    own[:, C:] = ext_own[...].astype(BF)
    send[:, C:] = ext_send[...].astype(BF)
    ft = jnp.concatenate([kept[2 * TALL :, CB * b : CB * b + TALL] for b in range(4)], axis=0)
    for j in range(STEPS):
        at = slice(j * COLS, j * COLS + COLS)
        g = jnp.dot(ft, grad_of(up[:, at], mid[:, at], coef[:, at]), preferred_element_type=F32)
        send[:, at] = g[CB // 2 :].astype(BF)
        own[:, at] = g[: CB // 2].astype(BF)


def grad_call(stats, kept, bn_params, pieces):
    return pl.pallas_call(
        grad_kernel,
        in_specs=[VMEM] * 5,
        out_specs=[VMEM] * 4,
        out_shape=[
            jax.ShapeDtypeStruct((CB // 2, WIDE), BF),
            jax.ShapeDtypeStruct((CB // 2, WIDE), BF),
            jax.ShapeDtypeStruct((4, PIECE), BF),
            jax.ShapeDtypeStruct((4, C), F32),
        ],
        scratch_shapes=[
            pltpu.VMEM((CB // 2, EXT), F32),
            pltpu.VMEM((CB // 2, EXT), F32),
        ],
        compiler_params=params(),
        cost_estimate=pl.CostEstimate(flops=2 * ROWS * CB * C, bytes_accessed=7000000, transcendentals=0),
        name="grad",
    )(stats, kept, bn_params, *pieces)


def input_kernel(w_any, kept_any, coef_any, after_ref, out_ref, token_ref, w, up, mid, coef, sems):
    done(token_ref)
    early = copy(coef_any, coef, sems.at[3, 0])
    loads = [
        [
            copy(w_any.at[:, cols(j)], w.at[:, cols(j)], sems.at[0, j]),
            copy(kept_any.at[pl.ds(0, TALL), cols(j)], up.at[:, cols(j)], sems.at[1, j]),
            copy(kept_any.at[pl.ds(TALL, TALL), cols(j)], mid.at[:, cols(j)], sems.at[2, j]),
        ]
        for j in range(STEPS)
    ]
    early.wait()
    total = None
    for j in range(STEPS):
        for load in loads[j]:
            load.wait()
        part = lax.dot_general(
            grad_of(up[:, cols(j)], mid[:, cols(j)], coef[:, cols(j)]),
            w[:, cols(j)],
            (((1,), (1,)), ((), ())),
            preferred_element_type=F32,
        )
        total = part if total is None else total + part
    out_ref[...] = total[:ROWS].astype(BF)


def input_call(weight, kept, coef, after):
    return pl.pallas_call(
        input_kernel,
        in_specs=[ANY] * 3 + [SMEM],
        out_specs=[VMEM, SMEM],
        out_shape=[jax.ShapeDtypeStruct((ROWS, CB), BF), TOKEN],
        scratch_shapes=[
            pltpu.VMEM((CB, C), BF),
            pltpu.VMEM((TALL, C), BF),
            pltpu.VMEM((TALL, C), BF),
            pltpu.VMEM((4, C), F32),
            DMA((4, STEPS)),
        ],
        compiler_params=params(VMEM_ALL),
        cost_estimate=pl.CostEstimate(flops=2 * ROWS * CB * C, bytes_accessed=5500000, transcendentals=0),
        name="ginput",
    )(weight, kept, coef, after)


def rows_kernel(n0, n1, n2, n3, after_ref, base_ref, w_any, four, w, sem):
    zl = lax.axis_index("zl")
    halves = []
    for high in range(2):
        for k, block in enumerate((n0, n1, n2, n3)):
            four[2 * k : 2 * k + 2, :] = block[...].astype(F32)[2 * high : 2 * high + 2]
        halves.append(pltpu.roll(four[...], 2 * zl, 0))
    both = jnp.concatenate(halves, axis=0)
    w[:, :C] = both[:, C : 2 * C]
    w[:, C:] = both[:, 2 * C + EXT :]
    store = copy(w, w_any, sem)
    base_ref[:, :C] = both[:, :C].astype(BF)
    base_ref[:, C:] = both[:, 2 * C : 2 * C + EXT].astype(BF)
    store.wait()


def rows_call(blocks, after):
    return pl.pallas_call(
        rows_kernel,
        in_specs=[VMEM] * 4 + [SMEM],
        out_specs=[VMEM, ANY],
        out_shape=[jax.ShapeDtypeStruct((16, WIDE), BF), jax.ShapeDtypeStruct((16, WIDE), F32)],
        scratch_shapes=[pltpu.VMEM((8, PIECE), F32), pltpu.VMEM((16, WIDE), F32), DMA],
        compiler_params=params(),
        cost_estimate=pl.CostEstimate(flops=16 * PIECE, bytes_accessed=500000, transcendentals=0),
        name="rows",
    )(*blocks, after)


def pair_kernel(own_ref, got_ref, out_ref, token_ref):
    done(token_ref)
    out_ref[...] = (own_ref[...].astype(F32) + got_ref[...].astype(F32)).astype(BF)


def pair_call(own, got):
    return pl.pallas_call(
        pair_kernel,
        in_specs=[VMEM] * 2,
        out_specs=[VMEM, SMEM],
        out_shape=[jax.ShapeDtypeStruct((256, WIDE), BF), TOKEN],
        compiler_params=params(),
        cost_estimate=pl.CostEstimate(flops=256 * WIDE, bytes_accessed=3300000, transcendentals=0),
        name="pair",
    )(own, got)


def plane_kernel(got_ref, b0, b1, b2, b3, out_ref, base_any, token_ref, sems):
    done(token_ref)
    x = lax.axis_index("x")
    stores = []
    for k, block in enumerate((b0, b1, b2, b3)):
        stores.append(copy(block, base_any.at[(x + k) & 3], sems.at[k]))
    total = jnp.sum(got_ref[...].astype(F32), axis=0).astype(BF)
    out_ref[...] = jnp.broadcast_to(total[None], out_ref.shape)
    for store in stores:
        store.wait()


def plane_call(got, bases):
    return pl.pallas_call(
        plane_kernel,
        in_specs=[VMEM] + [ANY] * 4,
        out_specs=[VMEM, ANY, SMEM],
        out_shape=[
            jax.ShapeDtypeStruct((8, 16, WIDE), BF),
            jax.ShapeDtypeStruct((4, 16, WIDE), BF),
            TOKEN,
        ],
        scratch_shapes=[DMA((4,))],
        compiler_params=params(),
        cost_estimate=pl.CostEstimate(flops=256 * WIDE, bytes_accessed=1700000, transcendentals=0),
        name="plane",
    )(got, *bases)


def column_kernel(got_ref, w_any, b1, b2, b3, after_ref, out_ref, own_ref, token_ref, w, sem):
    done(token_ref)
    load = copy(w_any, w, sem)
    z = 4 * lax.axis_index("zh") + lax.axis_index("zl")
    total = jnp.sum(got_ref[...].astype(F32), axis=0)
    g = total[:, :C]
    g_hi, g_lo = hi_lo(jnp.sum(g * g, axis=(0, 1), keepdims=True))
    load.wait()
    w_hi, w_lo = hi_lo(jnp.sum(w[:, C:], axis=(0, 1), keepdims=True))
    row = lax.broadcasted_iota(jnp.int32, (16, EXT), 0)
    lane = lax.broadcasted_iota(jnp.int32, (16, EXT), 1)
    bn_hi, bn_lo = hi_lo(total[0:1, C:])
    ext = jnp.where(row == 0, bn_hi, jnp.where(row == 1, bn_lo, 0.0))
    for k, value in enumerate((g_hi, g_lo, w_hi, w_lo)):
        ext = jnp.where((row == 2) & (lane == k), value, ext)
    step = (g + decay_rate * w[:, :C]).astype(BF)
    out_ref[:, :, :C] = jnp.broadcast_to(step[None], (16, 16, C))
    out_ref[:, :, C:] = jnp.broadcast_to(ext.astype(BF)[None], (16, 16, EXT))
    own_ref[...] = pltpu.roll(g, (16 - 2 * z) & 15, 0)[0:2]


def column_call(got, w_rows, bases, after):
    return pl.pallas_call(
        column_kernel,
        in_specs=[VMEM] + [ANY] * 4 + [SMEM],
        out_specs=[VMEM, VMEM, SMEM],
        out_shape=[
            jax.ShapeDtypeStruct((16, 16, WIDE), BF),
            jax.ShapeDtypeStruct((2, C), F32),
            TOKEN,
        ],
        scratch_shapes=[pltpu.VMEM((16, WIDE), F32), DMA],
        compiler_params=params(),
        cost_estimate=pl.CostEstimate(flops=128 * WIDE, bytes_accessed=1700000, transcendentals=0),
        name="column",
    )(got, w_rows, *bases, after)


def basis_kernel(b0, b1, b2, b3, m_any, v_any, bnm_any, after_ref, base_any, keep_ref, bnm, sems):
    y = lax.axis_index("y")
    stores = [
        copy(m_any, keep_ref.at[:, pl.ds(0, C)], sems.at[16]),
        copy(v_any, keep_ref.at[:, pl.ds(C, C)], sems.at[17]),
    ]
    load = copy(bnm_any, bnm, sems.at[18])
    for k, block in enumerate((b0, b1, b2, b3)):
        for x in range(4):
            stores.append(copy(block.at[x], base_any.at[4 * x + ((y + k) & 3)], sems.at[4 * k + x]))
    load.wait()
    keep_ref[:, 2 * C :] = jnp.concatenate([bnm[...]] * 16, axis=1)
    for store in stores:
        store.wait()


def basis_call(bases, master, momentum, bn_momentum, after):
    return pl.pallas_call(
        basis_kernel,
        in_specs=[ANY] * 7 + [SMEM],
        out_specs=[ANY, VMEM],
        out_shape=[jax.ShapeDtypeStruct((16, 16, WIDE), BF), jax.ShapeDtypeStruct((2, 2 * C + EXT), F32)],
        scratch_shapes=[pltpu.VMEM((2, 8), F32), DMA((19,))],
        compiler_params=params(),
        cost_estimate=pl.CostEstimate(flops=0, bytes_accessed=2200000, transcendentals=0),
        name="basis",
    )(*bases, master, momentum, bn_momentum, after)


def update_kernel(
    b0, b1, a0, a1, bn_v, g_v, keep,
    nw_any, nbn_ref, nm_ref, nv_ref, nbm_ref, nbv_ref,
    nw, sems,
):
    c = lax.axis_index("c")
    mine = place()
    rows = [pl.ds(64 * i, 64) for i in range(4)]
    r = lax.broadcasted_iota(jnp.int32, (128, 128), 0)
    t = lax.broadcasted_iota(jnp.int32, (128, 128), 1)
    want = (
        ((t >> 3) & 1) * 64 + ((t >> 1) & 3) * 16 + ((t >> 4) & 3) * 4 + (c ^ (t >> 6)) * 2 + (t & 1)
    )
    sel = jnp.where(r == want, 1.0, 0.0).astype(BF)

    e0 = b0[:, C:].astype(F32)
    e1 = b1[:, C:].astype(F32)
    row = lax.broadcasted_iota(jnp.int32, (256, EXT), 0) & 15
    lane = lax.broadcasted_iota(jnp.int32, (256, EXT), 1)
    both = jnp.where(row == 2, e0 + e1, 0.0)
    g_sq = jnp.sum(jnp.where(lane < 2, both, 0.0), axis=(0, 1), keepdims=True)
    w_sq = jnp.sum(jnp.where((lane == 2) | (lane == 3), both, 0.0), axis=(0, 1), keepdims=True)

    def rate_of(w_sq, g_sq):
        w_norm = jnp.sqrt(w_sq)
        return learn_rate * (trust_coef * w_norm / (jnp.sqrt(g_sq) + decay_rate * w_norm))

    rate = rate_of(w_sq, g_sq)
    stores = []
    for i in range(4):
        at = slice(64 * i, 64 * i + 64)
        new = jnp.concatenate(
            [
                (a0[at, :C].astype(F32) - rate * b0[at, :C].astype(F32)).astype(BF),
                (a1[at, :C].astype(F32) - rate * b1[at, :C].astype(F32)).astype(BF),
            ],
            axis=0,
        )
        new = jnp.dot(sel, new, preferred_element_type=F32).astype(BF)
        nw[at, :] = new[:64]
        nw[slice(256 + 64 * i, 320 + 64 * i), :] = new[64:]
        stores.append(copy(nw.at[rows[i]], nw_any.at[rows[i]], sems.at[0, i]))
        far_rows = pl.ds(256 + 64 * i, 64)
        stores.append(copy(nw.at[far_rows], nw_any.at[far_rows], sems.at[1, i]))

    def flat(e):
        return jnp.concatenate([e[16 * q : 16 * q + 1] + e[16 * q + 1 : 16 * q + 2] for q in range(16)], axis=1)

    near, far = flat(e0), flat(e1)
    bn_grad = jnp.concatenate([jnp.where(c == 0, near, far), jnp.where(c == 0, far, near)], axis=0)
    bn = bn_v[...]
    bn_rate = rate_of(
        jnp.sum(bn * bn, axis=1, keepdims=True), jnp.sum(bn_grad * bn_grad, axis=1, keepdims=True)
    )
    ends_a = a0[:, C:].astype(F32) + a1[:, C:].astype(F32)
    blocks = [None] * 16
    for x in range(4):
        rows_x = ends_a[64 * x : 64 * x + 16]
        for y in range(1, 4):
            rows_x = rows_x + ends_a[64 * x + 16 * y : 64 * x + 16 * y + 16]
        for high in range(2):
            for half in range(2):
                top = 8 * high + 4 * half
                blocks[8 * high + 2 * x + half] = rows_x[top : top + 2] + rows_x[top + 2 : top + 4]
    bn_base = jnp.concatenate(blocks, axis=1)
    nbn_ref[...] = (bn_base - bn_rate * (bn_grad + decay_rate * bn)).astype(BF)
    master = keep[:, 0:C]
    new_v = momentum_rate * keep[:, C : 2 * C] + rate * (g_v[...] + decay_rate * master)
    nv_ref[...] = new_v
    nm_ref[...] = master - new_v
    lane = lax.broadcasted_iota(jnp.int32, (2, EXT), 1)

    def own_eight(row):
        kept = jnp.where((lane >> 3) == (mine & 15), own_block(row, mine), 0.0)
        eight = kept[:, 0:8]
        for s in range(1, 16):
            eight = eight + kept[:, 8 * s : 8 * s + 8]
        return eight

    own_bn = own_eight(bn)
    new_bnv = momentum_rate * keep[:, 2 * C : 2 * C + 8] + bn_rate * (own_eight(bn_grad) + decay_rate * own_bn)
    nbv_ref[...] = new_bnv
    nbm_ref[...] = own_bn - new_bnv
    for store in stores:
        store.wait()


def update_call(b0, b1, a0, a1, bn_params, g_own, keep):
    small = [jax.ShapeDtypeStruct((2, C), F32)] * 2 + [jax.ShapeDtypeStruct((2, 8), F32)] * 2
    return pl.pallas_call(
        update_kernel,
        in_specs=[VMEM] * 7,
        out_specs=[ANY] + [VMEM] * 5,
        out_shape=[jax.ShapeDtypeStruct((CB, C), BF), jax.ShapeDtypeStruct((2, C), BF)] + small,
        scratch_shapes=[pltpu.VMEM((CB, C), BF), DMA((2, 4))],
        compiler_params=params(),
        cost_estimate=pl.CostEstimate(flops=2 * CB * 128 * C, bytes_accessed=6500000, transcendentals=0),
        name="update",
    )(b0, b1, a0, a1, bn_params, g_own, keep)


def exchange(block, axes):
    return lax.all_to_all(block, axes, 0, 0, tiled=True)


def shift_pairs(move):
    out = []
    for i in range(256):
        c, y, zl, x, zh = i & 1, (i >> 1) & 3, (i >> 3) & 3, (i >> 5) & 3, i >> 7
        x, y, z = move(x, y, 4 * zh + zl)
        out.append((i, ((((z >> 2) * 4 + x) * 4 + (z & 3)) * 4 + y) * 2 + c))
    return out


def ring(block, size, move):
    parts = [block]
    for k in range(1, size):
        parts.append(lax.ppermute(block, AXES, shift_pairs(functools.partial(move, size - k))))
    return parts


def shards(features, weight, cotangent, pre_act, bn_params, master, momentum, bn_momentum):
    swap = functools.partial(lax.ppermute, axis_name=AXES, perm=sibling_pairs())

    stats, piece = stats_call(
        features, weight, cotangent, pre_act, master, momentum, bn_params, bn_momentum
    )
    pieces = [piece, lax.ppermute(piece, AXES, shift_pairs(lambda x, y, z: (x, y, z ^ 4)))]
    later, stats = lax.optimization_barrier((features, stats))
    up, kept = prep_call(later, weight, cotangent, pre_act)
    stats = exchange(stats, GX)
    send, own, near, coef = grad_call(stats, kept, bn_params, pieces)
    half, token = pair_call(own, swap(send))
    blocks = ring(near, 4, lambda k, x, y, z: (x, y, (z & 4) + ((z + k) & 3)))
    base, w_rows = rows_call(blocks, token)
    bases = ring(base, 4, lambda k, x, y, z: ((x + k) % 4, y, z))
    part, base, token = plane_call(exchange(half.reshape(16, 16, WIDE), XY), bases)
    bases = ring(base, 4, lambda k, x, y, z: (x, (y + k) % 4, z))
    grad_input, token = input_call(weight, kept, coef, token)
    step, g_own, token = column_call(exchange(part, Z), w_rows, bases[1:], token)
    a0, keep = basis_call(bases, master, momentum, bn_momentum, token)
    a0 = a0.reshape(256, WIDE)
    a1 = swap(a0)
    b0 = exchange(step, XY).reshape(256, WIDE)
    b1 = swap(b0)
    new_weight, new_bn, new_master, new_momentum, new_bn_master, new_bn_momentum = update_call(
        b0, b1, a0, a1, bn_params, g_own, keep
    )
    return (grad_input, up, new_master, new_momentum, new_weight, new_bn_master, new_bn_momentum, new_bn)


def solution(mesh):
    fine = Mesh(mesh.devices.reshape(SIZES), AXES)
    rows = P(AXES, None)
    cols = P(None, AXES)
    return jax.shard_map(
        shards,
        mesh=fine,
        in_specs=(rows, P(), rows, rows, P(), rows, rows, cols),
        out_specs=(rows, rows, rows, rows, P(), cols, cols, P()),
        check_vma=False,
    )
```

time: 126 us -> 115 us (0.913)
  starting transfers between devices: 60.8 us -> 52.8 us
  Pallas kernels: 30.6 us -> 26.8 us
  waiting for transfers between devices: 28.5 us -> 31.9 us
  local copies, waits for them, and re-layouts: 4.02 us -> 2.1 us
    all_to_all x4, waiting for transfers between devices: 8.8 us -> 13.5 us  [exchange(): return lax.all_to_all(block, axes, 0, 0, tiled=True)]
    ppermute x2, waiting for transfers between devices: 7.06 us -> 2.38 us  [the longest x1 2.38 us: shards(): half, token = pair_call(own, swap(send))]
    pallas_call x10, Pallas kernels: 30.6 us -> 26.8 us  [the longest x1 5.12 us: prep_call(): pl.pallas_call(prep_kernel, in_specs=[ANY] * 4, out_specs=[ANY, ANY], out...]
    ppermute x9, waiting for transfers between devices: 10.3 us -> 13.6 us  [ring(): lax.ppermute(block, AXES, shift_pairs(functools.partial(move, size - k)))]
    ppermute x1, starting transfers between devices: 6.46 us -> 3.85 us  [shards(): b1 = swap(b0)]
    all_to_all x4, starting transfers between devices: 29.3 us -> 26.9 us  [exchange(): return lax.all_to_all(block, axes, 0, 0, tiled=True)]
    ppermute x9, starting transfers between devices: 12.9 us -> 11 us  [ring(): lax.ppermute(block, AXES, shift_pairs(functools.partial(move, size - k)))]
    unnamed x26 -> x14, local copies, waits for them, and re-layouts: 4.02 us -> 2.1 us
  transfers between devices with their start and end apart: 17 -> 17, of which waited for: 10 -> 11; matrix products, arithmetic and copies ran while one was open for 0% -> 0% of each run, Pallas kernels for 9% -> 11%
where the time goes in v4:
time: 115 us
  starting transfers between devices  52.8 us (46%)
  waiting for transfers between devices  31.9 us (28%)
  Pallas kernels  26.8 us (23%)
  local copies, waits for them, and re-layouts  2.1 us (2%)
    all_to_all x4, starting transfers between devices, exchange(): return lax.all_to_all(block, axes, 0, 0, tiled=True)  26.9 us
    ppermute x9, waiting for transfers between devices, ring(): lax.ppermute(block, AXES, shift_pairs(functools.partial(move, size - k)))  13.6 us
    all_to_all x4, waiting for transfers between devices, exchange(): return lax.all_to_all(block, axes, 0, 0, tiled=True)  13.5 us
    ppermute x9, starting transfers between devices, ring(): lax.ppermute(block, AXES, shift_pairs(functools.partial(move, size - k)))  11 us
    ppermute x1, starting transfers between devices, shards(): lax.ppermute(piece, AXES, shift_pairs(lambda x, y, z: (x, y, z ^ 4)))  5.36 us
    pallas_call x1, Pallas kernels, prep_call(): pl.pallas_call(prep_kernel, in_specs=[ANY] * 4, out_specs=[ANY, ANY], out...  5.12 us
    pallas_call x1, Pallas kernels, stats_call(): pl.pallas_call(stats_kernel, in_specs=[ANY] * 8, out_specs=[VMEM, VMEM],...  4.69 us
    pallas_call x1, Pallas kernels, input_call(): pl.pallas_call(input_kernel, in_specs=[ANY] * 3 + [SMEM], out_specs=[VMEM...  4.52 us
  transfers between devices with their start and end apart: 17, of which 11 were waited for; matrix products, arithmetic and copies ran while one was open for 0% of the time, Pallas kernels for 11%

profile of v4, /device:TPU:1, one launch (start us, length us, event | category | flops | bytes accessed | tf_op | source)
XLA Modules:
  0.0 114.7 jit_solution(8655448125431675785)
XLA Ops:
  0.6 4.7 %stats.1 = (f32[8,4,2048]{2,1,0:T(4,128)}, f32[2,4352]{1,0:T(2,128)}) custom-call(bf16[392,512]{1,0:T(8,128)(2,1)} %f_any.2, bf16[512,2048]{1,0:T(8,128)(2,1)} %w_any.5, bf16[392,2048]{1,0:T(8,128)(2,1)} %cot_any.3, bf16[392,2048]{1,0:T(8,128)(2,1)} %pre_any.3, f32[2,2048]{1,0:T(2,128)} %m_any.3, f32[2,2048]{1,0:T(2,128)} %v_any.3, f32[2,2048]{1,0:T(2,128)} %bn_v.1, ...), custom_call_target="tpu_custom_call" | custom-call | flops 822083584 | bytes 7500000 | tf_op jit(solution)/shard_map/stats/pallas_call | solution.py:162
  5.3 11.5 %all-to-all-start = ((f32[8,4,2048]{2,1,0:T(4,128)}), f32[8,4,2048]{2,1,0:T(4,128)S(1)}, u32[]{:S(2)}, u32[]{:S(2)}) async-start(f32[8,4,2048]{2,1,0:T(4,128)} %get-tuple-element.41), calls=%async_computation | async-start | bytes 524288 | tf_op jit(solution)/shard_map/all_to_all | solution.py:605
  16.8 0.0 copy-start.1
  16.8 0.0 copy-start.4
  16.8 5.4 %collective-permute-start = (f32[2,4352]{1,0:T(2,128)}, f32[2,4352]{1,0:T(2,128)S(1)}, u32[]{:S(2)}, u32[]{:S(2)}) collective-permute-start(f32[2,4352]{1,0:T(2,128)} %get-tuple-element.42.p0), channel_id=1, source_target_pairs={{0,128},{1,129},{2,130},{3,131},{4,132},{5,133},{6,134},{7,135},{8... | collective-permute-start | bytes 104456 | tf_op jit(solution)/shard_map/ppermute | solution.py:630
  22.2 5.1 %prep.1 = (bf16[392,2048]{1,0:T(8,128)(2,1)}, bf16[928,2048]{1,0:T(8,128)(2,1)}) custom-call(bf16[392,512]{1,0:T(8,128)(2,1)} %f_any.2, bf16[512,2048]{1,0:T(8,128)(2,1)} %w_any.5, bf16[392,2048]{1,0:T(8,128)(2,1)} %cot_any.3, bf16[392,2048]{1,0:T(8,128)(2,1)} %pre_any.3), custom_call_target="tpu_custom_call" | custom-call | flops 1233125376 | bytes 9000000 | tf_op jit(solution)/shard_map/prep/pallas_call | solution.py:227
  27.3 0.0 collective-permute-done.p1
  27.3 0.0 all-to-all-done.stat
  27.3 0.0 copy-done.1
  27.3 0.0 copy-done.4
  27.4 0.0 copy-start
  27.4 2.1 %copy-done = bf16[928,2048]{1,0:T(8,128)(2,1)S(1)} copy-done((bf16[928,2048]{1,0:T(8,128)(2,1)S(1)}, bf16[928,2048]{1,0:T(8,128)(2,1)}, u32[]{:S(2)}) %copy-start) | copy-done | bytes 3801112
  29.4 1.5 %grad.1 = (bf16[256,2176]{1,0:T(8,128)(2,1)S(1)}, bf16[256,2176]{1,0:T(8,128)(2,1)S(1)}, bf16[4,4352]{1,0:T(4,128)(2,1)S(1)}, f32[4,2048]{1,0:T(4,128)S(1)}) custom-call(f32[8,4,2048]{2,1,0:T(4,128)S(1)} %all-to-all-done.stat, bf16[928,2048]{1,0:T(8,128)(2,1)S(1)} %copy-done, f32[2,2048]{1,0:T(2,128)S(1)} %copy-done.1, f32[2,4352]{1,0:T(2,128)S(1)} %copy-done.4, ...), custom_call_target="tpu_custom_call" | custom-call | flops 822083584 | bytes 7000000 | tf_op jit(solution)/shard_map/grad/pallas_call | solution.py:296
  30.9 0.0 copy-start.5
  30.9 2.7 %collective-permute-start.1 = (bf16[256,2176]{1,0:T(8,128)(2,1)S(1)}, bf16[256,2176]{1,0:T(8,128)(2,1)S(1)}, u32[]{:S(2)}, u32[]{:S(2)}) collective-permute-start(bf16[256,2176]{1,0:T(8,128)(2,1)S(1)} %get-tuple-element.45), channel_id=1, source_target_pairs={{0,1},{1,0},{2,3},{3,2},{4,5},{5,4},{6,7},{7,6},{8,9},{9,8},{10,11... | collective-permute-start | bytes 3342344 | tf_op jit(solution)/shard_map/ppermute | solution.py:635
  33.6 2.4 %collective-permute-done.1.got_ref = bf16[256,2176]{1,0:T(8,128)(2,1)S(1)} collective-permute-done((bf16[256,2176]{1,0:T(8,128)(2,1)S(1)}, bf16[256,2176]{1,0:T(8,128)(2,1)S(1)}, u32[]{:S(2)}, u32[]{:S(2)}) %collective-permute-start.1) | collective-permute-done | bytes 1114144 | tf_op jit(solution)/shard_map/ppermute | solution.py:635
  36.0 1.3 %pair.1 = (bf16[256,2176]{1,0:T(8,128)(2,1)}, s32[1]{0:T(128)}) custom-call(bf16[256,2176]{1,0:T(8,128)(2,1)S(1)} %get-tuple-element.44.own_ref, bf16[256,2176]{1,0:T(8,128)(2,1)S(1)} %collective-permute-done.1.got_ref), custom_call_target="tpu_custom_call" | custom-call | flops 557056 | bytes 3300000 | tf_op jit(solution)/shard_map/pair/pallas_call | solution.py:396
  37.2 0.0 copy-done.5
  37.2 6.8 %all-to-all-start.1 = ((bf16[16,16,2176]{2,1,0:T(8,128)(2,1)}), bf16[16,16,2176]{2,1,0:T(8,128)(2,1)S(1)}, u32[]{:S(2)}, u32[]{:S(2)}) async-start(bf16[16,16,2176]{2,1,0:T(8,128)(2,1)} %bitcast), calls=%async_computation.1 | async-start | bytes 2228224 | tf_op jit(solution)/shard_map/all_to_all | solution.py:605
  44.0 1.7 %collective-permute-start.2 = (bf16[4,4352]{1,0:T(4,128)(2,1)S(1)}, bf16[4,4352]{1,0:T(4,128)(2,1)S(1)}, u32[]{:S(2)}, u32[]{:S(2)}) collective-permute-start(bf16[4,4352]{1,0:T(4,128)(2,1)S(1)} %get-tuple-element.47.n0), channel_id=1, source_target_pairs={{0,24},{1,25},{2,26},{3,27},{4,28},{5,29},{6,30},{7,31},{8,0},{9,1... | collective-permute-start | bytes 104456 | tf_op jit(solution)/shard_map/ppermute | solution.py:620
  45.7 1.5 %collective-permute-start.3 = (bf16[4,4352]{1,0:T(4,128)(2,1)S(1)}, bf16[4,4352]{1,0:T(4,128)(2,1)S(1)}, u32[]{:S(2)}, u32[]{:S(2)}) collective-permute-start(bf16[4,4352]{1,0:T(4,128)(2,1)S(1)} %get-tuple-element.47.n0), channel_id=1, source_target_pairs={{0,16},{1,17},{2,18},{3,19},{4,20},{5,21},{6,22},{7,23},{8,24},{9,... | collective-permute-start | bytes 104456 | tf_op jit(solution)/shard_map/ppermute | solution.py:620
  47.2 0.7 collective-permute-start.4
  47.9 0.0 collective-permute-done.2.n1
  47.9 2.3 %collective-permute-done.3.n2 = bf16[4,4352]{1,0:T(4,128)(2,1)S(1)} collective-permute-done((bf16[4,4352]{1,0:T(4,128)(2,1)S(1)}, bf16[4,4352]{1,0:T(4,128)(2,1)S(1)}, u32[]{:S(2)}, u32[]{:S(2)}) %collective-permute-start.3) | collective-permute-done | bytes 34848 | tf_op jit(solution)/shard_map/ppermute | solution.py:620
  50.2 1.5 %collective-permute-done.4.n3 = bf16[4,4352]{1,0:T(4,128)(2,1)S(1)} collective-permute-done((bf16[4,4352]{1,0:T(4,128)(2,1)S(1)}, bf16[4,4352]{1,0:T(4,128)(2,1)S(1)}, u32[]{:S(2)}, u32[]{:S(2)}) %collective-permute-start.4) | collective-permute-done | bytes 34848 | tf_op jit(solution)/shard_map/ppermute | solution.py:620
  51.8 0.9 rows.1
  52.7 2.9 %collective-permute-start.5 = (bf16[16,2176]{1,0:T(8,128)(2,1)S(1)}, bf16[16,2176]{1,0:T(8,128)(2,1)S(1)}, u32[]{:S(2)}, u32[]{:S(2)}) collective-permute-start(bf16[16,2176]{1,0:T(8,128)(2,1)S(1)} %get-tuple-element.49.b0), channel_id=1, source_target_pairs={{0,96},{1,97},{2,98},{3,99},{4,100},{5,101},{6,102},{7,103},{8,104... | collective-permute-start | bytes 208904 | tf_op jit(solution)/shard_map/ppermute | solution.py:620
  55.6 0.6 collective-permute-start.6
  56.2 0.6 collective-permute-start.7
  56.7 2.5 %collective-permute-done.5.b1 = bf16[16,2176]{1,0:T(8,128)(2,1)S(1)} collective-permute-done((bf16[16,2176]{1,0:T(8,128)(2,1)S(1)}, bf16[16,2176]{1,0:T(8,128)(2,1)S(1)}, u32[]{:S(2)}, u32[]{:S(2)}) %collective-permute-start.5) | collective-permute-done | bytes 69664 | tf_op jit(solution)/shard_map/ppermute | solution.py:620
  59.2 1.8 %collective-permute-done.6.b2 = bf16[16,2176]{1,0:T(8,128)(2,1)S(1)} collective-permute-done((bf16[16,2176]{1,0:T(8,128)(2,1)S(1)}, bf16[16,2176]{1,0:T(8,128)(2,1)S(1)}, u32[]{:S(2)}, u32[]{:S(2)}) %collective-permute-start.6) | collective-permute-done | bytes 69664 | tf_op jit(solution)/shard_map/ppermute | solution.py:620
  61.0 0.7 collective-permute-done.7.b3
  61.8 0.0 all-to-all-done.1.got_ref
  61.8 1.4 %plane.1 = (bf16[8,16,2176]{2,1,0:T(8,128)(2,1)}, bf16[4,16,2176]{2,1,0:T(8,128)(2,1)S(1)}, s32[1]{0:T(128)}) custom-call(bf16[16,16,2176]{2,1,0:T(8,128)(2,1)S(1)} %all-to-all-done.1.got_ref, bf16[16,2176]{1,0:T(8,128)(2,1)S(1)} %get-tuple-element.49.b0, bf16[16,2176]{1,0:T(8,128)(2,1)S(1)} %collective-permute-done.5.b1, ...), custom_call_target="tpu_custom_call" | custom-call | flops 557056 | bytes 1700000 | tf_op jit(solution)/shard_map/plane/pallas_call | solution.py:420
  63.1 4.5 %all-to-all-start.2 = ((bf16[8,16,2176]{2,1,0:T(8,128)(2,1)}), bf16[8,16,2176]{2,1,0:T(8,128)(2,1)S(1)}, u32[]{:S(2)}, u32[]{:S(2)}) async-start(bf16[8,16,2176]{2,1,0:T(8,128)(2,1)} %get-tuple-element.53), calls=%async_computation.2 | async-start | bytes 1114112 | tf_op jit(solution)/shard_map/all_to_all | solution.py:605
  67.6 1.2 %collective-permute-start.10 = (bf16[4,16,2176]{2,1,0:T(8,128)(2,1)S(1)}, bf16[4,16,2176]{2,1,0:T(8,128)(2,1)S(1)}, u32[]{:S(2)}, u32[]{:S(2)}) collective-permute-start(bf16[4,16,2176]{2,1,0:T(8,128)(2,1)S(1)} %get-tuple-element.55.b0), channel_id=1, source_target_pairs={{0,2},{1,3},{2,4},{3,5},{4,6},{5,7},{6,0},{7,1},{8,10},{9,11},{10,... | collective-permute-start | bytes 835592 | tf_op jit(solution)/shard_map/ppermute | solution.py:620
  68.8 1.5 %collective-permute-start.8 = (bf16[4,16,2176]{2,1,0:T(8,128)(2,1)S(1)}, bf16[4,16,2176]{2,1,0:T(8,128)(2,1)S(1)}, u32[]{:S(2)}, u32[]{:S(2)}) collective-permute-start(bf16[4,16,2176]{2,1,0:T(8,128)(2,1)S(1)} %get-tuple-element.55.b0), channel_id=1, source_target_pairs={{0,6},{1,7},{2,0},{3,1},{4,2},{5,3},{6,4},{7,5},{8,14},{9,15},{10,... | collective-permute-start | bytes 835592 | tf_op jit(solution)/shard_map/ppermute | solution.py:620
  70.3 0.4 collective-permute-start.9
  70.7 4.5 %ginput.1 = (bf16[392,512]{1,0:T(8,128)(2,1)}, s32[1]{0:T(128)}) custom-call(bf16[512,2048]{1,0:T(8,128)(2,1)} %w_any.5, bf16[928,2048]{1,0:T(8,128)(2,1)} %get-tuple-element.40.kept.kept_any, f32[4,2048]{1,0:T(4,128)} %copy-done.5, s32[1]{0:T(128)} %get-tuple-element.50.after_ref), custom_call_target="tpu_custom_call" | custom-call | flops 822083584 | bytes 5500000 | tf_op jit(solution)/shard_map/ginput/pallas_call | solution.py:343
  75.2 0.4 collective-permute-done.10.b3
  75.6 0.0 collective-permute-done.8.b1
  75.6 4.4 %collective-permute-done.9.b2 = bf16[4,16,2176]{2,1,0:T(8,128)(2,1)S(1)} collective-permute-done((bf16[4,16,2176]{2,1,0:T(8,128)(2,1)S(1)}, bf16[4,16,2176]{2,1,0:T(8,128)(2,1)S(1)}, u32[]{:S(2)}, u32[]{:S(2)}) %collective-permute-start.9) | collective-permute-done | bytes 278560 | tf_op jit(solution)/shard_map/ppermute | solution.py:620
  80.0 4.1 %all-to-all-done.2.got_ref = bf16[8,16,2176]{2,1,0:T(8,128)(2,1)S(1)} async-done(((bf16[8,16,2176]{2,1,0:T(8,128)(2,1)}), bf16[8,16,2176]{2,1,0:T(8,128)(2,1)S(1)}, u32[]{:S(2)}, u32[]{:S(2)}) %all-to-all-start.2) | async-done | bytes 557088 | tf_op jit(solution)/shard_map/all_to_all | solution.py:605
  84.1 2.2 %column.1 = (bf16[16,16,2176]{2,1,0:T(8,128)(2,1)}, f32[2,2048]{1,0:T(2,128)S(1)}, s32[1]{0:T(128)}) custom-call(bf16[8,16,2176]{2,1,0:T(8,128)(2,1)S(1)} %all-to-all-done.2.got_ref, f32[16,2176]{1,0:T(8,128)S(1)} %get-tuple-element.54.w_any, bf16[4,16,2176]{2,1,0:T(8,128)(2,1)S(1)} %collective-permute-done.8.b1, ...), custom_call_target="tpu_custom_call" | custom-call | flops 278528 | bytes 1700000 | tf_op jit(solution)/shard_map/column/pallas_call | solution.py:458
  86.3 0.0 copy-start.2
  86.3 0.0 copy-start.3
  86.3 0.0 copy-start.6
  86.4 4.1 %all-to-all-start.3 = ((bf16[16,16,2176]{2,1,0:T(8,128)(2,1)}), bf16[16,16,2176]{2,1,0:T(8,128)(2,1)S(1)}, u32[]{:S(2)}, u32[]{:S(2)}) async-start(bf16[16,16,2176]{2,1,0:T(8,128)(2,1)} %get-tuple-element.57), calls=%async_computation.3 | async-start | bytes 2228224 | tf_op jit(solution)/shard_map/all_to_all | solution.py:605
  90.5 0.0 copy-done.2
  90.5 0.0 copy-done.3
  90.5 0.0 copy-done.6
  90.5 2.4 %basis.1 = (bf16[16,16,2176]{2,1,0:T(8,128)(2,1)S(1)}, f32[2,4224]{1,0:T(2,128)S(1)}) custom-call(bf16[4,16,2176]{2,1,0:T(8,128)(2,1)S(1)} %get-tuple-element.55.b0, bf16[4,16,2176]{2,1,0:T(8,128)(2,1)S(1)} %collective-permute-done.8.b1, bf16[4,16,2176]{2,1,0:T(8,128)(2,1)S(1)} %collective-permute-done.9.b2, ...), custom_call_target="tpu_custom_call" | custom-call | bytes 2200000 | tf_op jit(solution)/shard_map/basis/pallas_call | solution.py:491
  92.9 3.1 %collective-permute-start.12 = (bf16[256,2176]{1,0:T(8,128)(2,1)S(1)}, bf16[256,2176]{1,0:T(8,128)(2,1)S(1)}, u32[]{:S(2)}, u32[]{:S(2)}) collective-permute-start(bf16[256,2176]{1,0:T(8,128)(2,1)S(1)} %bitcast.5), channel_id=1, source_target_pairs={{0,1},{1,0},{2,3},{3,2},{4,5},{5,4},{6,7},{7,6},{8,9},{9,8},{10,11... | collective-permute-start | bytes 3342344 | tf_op jit(solution)/shard_map/ppermute | solution.py:645
  96.0 9.4 %all-to-all-done.3 = bf16[16,16,2176]{2,1,0:T(8,128)(2,1)S(1)} async-done(((bf16[16,16,2176]{2,1,0:T(8,128)(2,1)}), bf16[16,16,2176]{2,1,0:T(8,128)(2,1)S(1)}, u32[]{:S(2)}, u32[]{:S(2)}) %all-to-all-start.3) | async-done | bytes 1114144 | tf_op jit(solution)/shard_map/all_to_all | solution.py:605
  105.4 3.8 %collective-permute-start.11 = (bf16[256,2176]{1,0:T(8,128)(2,1)S(1)}, bf16[256,2176]{1,0:T(8,128)(2,1)S(1)}, u32[]{:S(2)}, u32[]{:S(2)}) collective-permute-start(bf16[256,2176]{1,0:T(8,128)(2,1)S(1)} %bitcast.3), channel_id=1, source_target_pairs={{0,1},{1,0},{2,3},{3,2},{4,5},{5,4},{6,7},{7,6},{8,9},{9,8},{10,11... | collective-permute-start | bytes 3342344 | tf_op jit(solution)/shard_map/ppermute | solution.py:647
  109.3 0.0 collective-permute-done.12.a1
  109.3 2.4 %collective-permute-done.11.b1 = bf16[256,2176]{1,0:T(8,128)(2,1)S(1)} collective-permute-done((bf16[256,2176]{1,0:T(8,128)(2,1)S(1)}, bf16[256,2176]{1,0:T(8,128)(2,1)S(1)}, u32[]{:S(2)}, u32[]{:S(2)}) %collective-permute-start.11) | collective-permute-done | bytes 1114144 | tf_op jit(solution)/shard_map/ppermute | solution.py:647
  111.6 2.9 %update.1 = (bf16[512,2048]{1,0:T(8,128)(2,1)}, bf16[2,2048]{1,0:T(2,128)(2,1)}, f32[2,2048]{1,0:T(2,128)}, f32[2,2048]{1,0:T(2,128)}, f32[2,8]{1,0:T(2,128)}, /*index=5*/f32[2,8]{1,0:T(2,128)}) custom-call(bf16[256,2176]{1,0:T(8,128)(2,1)S(1)} %bitcast.4, bf16[256,2176]{1,0:T(8,128)(2,1)S(1)} %collective-permute-done.11.b1, bf16[256,2176]{1,0:T(8,128)(2,1)S(1)} %bitcast.6, ...), custom_call_target="tpu_custom_call" | custom-call | flops 268435456 | bytes 6500000 | tf_op jit(solution)/shard_map/update/pallas_call | solution.py:592
Async XLA Ops:
  5.3 22.0 %all-to-all-start = ((f32[8,4,2048]{2,1,0:T(4,128)}), f32[8,4,2048]{2,1,0:T(4,128)S(1)}, u32[]{:S(2)}, u32[]{:S(2)}) async-start(f32[8,4,2048]{2,1,0:T(4,128)} %get-tuple-element.41), calls=%async_computation | async-start | bytes 524288 | tf_op jit(solution)/shard_map/all_to_all | solution.py:605
  16.8 10.5 %copy-start.1 = (f32[2,2048]{1,0:T(2,128)S(1)}, f32[2,2048]{1,0:T(2,128)}, u32[]{:S(2)}) copy-start(f32[2,2048]{1,0:T(2,128)} %bn_v.1) | copy-start | bytes 49156
  16.8 10.5 %copy-start.4 = (f32[2,4352]{1,0:T(2,128)S(1)}, f32[2,4352]{1,0:T(2,128)}, u32[]{:S(2)}) copy-start(f32[2,4352]{1,0:T(2,128)} %get-tuple-element.42.p0) | copy-start | bytes 104452
  16.8 10.5 %collective-permute-start = (f32[2,4352]{1,0:T(2,128)}, f32[2,4352]{1,0:T(2,128)S(1)}, u32[]{:S(2)}, u32[]{:S(2)}) collective-permute-start(f32[2,4352]{1,0:T(2,128)} %get-tuple-element.42.p0), channel_id=1, source_target_pairs={{0,128},{1,129},{2,130},{3,131},{4,132},{5,133},{6,134},{7,135},{8... | collective-permute-start | bytes 104456 | tf_op jit(solution)/shard_map/ppermute | solution.py:630
  27.4 2.1 %copy-start = (bf16[928,2048]{1,0:T(8,128)(2,1)S(1)}, bf16[928,2048]{1,0:T(8,128)(2,1)}, u32[]{:S(2)}) copy-start(bf16[928,2048]{1,0:T(8,128)(2,1)} %get-tuple-element.40.kept.kept_any) | copy-start | bytes 11403268
  30.9 6.3 %copy-start.5 = (f32[4,2048]{1,0:T(4,128)}, f32[4,2048]{1,0:T(4,128)S(1)}, u32[]{:S(2)}) copy-start(f32[4,2048]{1,0:T(4,128)S(1)} %get-tuple-element.43.coef_any) | copy-start | bytes 98308
  30.9 5.0 %collective-permute-start.1 = (bf16[256,2176]{1,0:T(8,128)(2,1)S(1)}, bf16[256,2176]{1,0:T(8,128)(2,1)S(1)}, u32[]{:S(2)}, u32[]{:S(2)}) collective-permute-start(bf16[256,2176]{1,0:T(8,128)(2,1)S(1)} %get-tuple-element.45), channel_id=1, source_target_pairs={{0,1},{1,0},{2,3},{3,2},{4,5},{5,4},{6,7},{7,6},{8,9},{9,8},{10,11... | collective-permute-start | bytes 3342344 | tf_op jit(solution)/shard_map/ppermute | solution.py:635
  37.2 24.5 %all-to-all-start.1 = ((bf16[16,16,2176]{2,1,0:T(8,128)(2,1)}), bf16[16,16,2176]{2,1,0:T(8,128)(2,1)S(1)}, u32[]{:S(2)}, u32[]{:S(2)}) async-start(bf16[16,16,2176]{2,1,0:T(8,128)(2,1)} %bitcast), calls=%async_computation.1 | async-start | bytes 2228224 | tf_op jit(solution)/shard_map/all_to_all | solution.py:605
  44.0 3.9 %collective-permute-start.2 = (bf16[4,4352]{1,0:T(4,128)(2,1)S(1)}, bf16[4,4352]{1,0:T(4,128)(2,1)S(1)}, u32[]{:S(2)}, u32[]{:S(2)}) collective-permute-start(bf16[4,4352]{1,0:T(4,128)(2,1)S(1)} %get-tuple-element.47.n0), channel_id=1, source_target_pairs={{0,24},{1,25},{2,26},{3,27},{4,28},{5,29},{6,30},{7,31},{8,0},{9,1... | collective-permute-start | bytes 104456 | tf_op jit(solution)/shard_map/ppermute | solution.py:620
  45.7 4.5 %collective-permute-start.3 = (bf16[4,4352]{1,0:T(4,128)(2,1)S(1)}, bf16[4,4352]{1,0:T(4,128)(2,1)S(1)}, u32[]{:S(2)}, u32[]{:S(2)}) collective-permute-start(bf16[4,4352]{1,0:T(4,128)(2,1)S(1)} %get-tuple-element.47.n0), channel_id=1, source_target_pairs={{0,16},{1,17},{2,18},{3,19},{4,20},{5,21},{6,22},{7,23},{8,24},{9,... | collective-permute-start | bytes 104456 | tf_op jit(solution)/shard_map/ppermute | solution.py:620
  47.2 4.6 %collective-permute-start.4 = (bf16[4,4352]{1,0:T(4,128)(2,1)S(1)}, bf16[4,4352]{1,0:T(4,128)(2,1)S(1)}, u32[]{:S(2)}, u32[]{:S(2)}) collective-permute-start(bf16[4,4352]{1,0:T(4,128)(2,1)S(1)} %get-tuple-element.47.n0), channel_id=1, source_target_pairs={{0,8},{1,9},{2,10},{3,11},{4,12},{5,13},{6,14},{7,15},{8,16},{9,17... | collective-permute-start | bytes 104456 | tf_op jit(solution)/shard_map/ppermute | solution.py:620
  52.7 6.5 %collective-permute-start.5 = (bf16[16,2176]{1,0:T(8,128)(2,1)S(1)}, bf16[16,2176]{1,0:T(8,128)(2,1)S(1)}, u32[]{:S(2)}, u32[]{:S(2)}) collective-permute-start(bf16[16,2176]{1,0:T(8,128)(2,1)S(1)} %get-tuple-element.49.b0), channel_id=1, source_target_pairs={{0,96},{1,97},{2,98},{3,99},{4,100},{5,101},{6,102},{7,103},{8,104... | collective-permute-start | bytes 208904 | tf_op jit(solution)/shard_map/ppermute | solution.py:620
  55.6 5.4 %collective-permute-start.6 = (bf16[16,2176]{1,0:T(8,128)(2,1)S(1)}, bf16[16,2176]{1,0:T(8,128)(2,1)S(1)}, u32[]{:S(2)}, u32[]{:S(2)}) collective-permute-start(bf16[16,2176]{1,0:T(8,128)(2,1)S(1)} %get-tuple-element.49.b0), channel_id=1, source_target_pairs={{0,64},{1,65},{2,66},{3,67},{4,68},{5,69},{6,70},{7,71},{8,72},{9,... | collective-permute-start | bytes 208904 | tf_op jit(solution)/shard_map/ppermute | solution.py:620
  56.2 5.6 %collective-permute-start.7 = (bf16[16,2176]{1,0:T(8,128)(2,1)S(1)}, bf16[16,2176]{1,0:T(8,128)(2,1)S(1)}, u32[]{:S(2)}, u32[]{:S(2)}) collective-permute-start(bf16[16,2176]{1,0:T(8,128)(2,1)S(1)} %get-tuple-element.49.b0), channel_id=1, source_target_pairs={{0,32},{1,33},{2,34},{3,35},{4,36},{5,37},{6,38},{7,39},{8,40},{9,... | collective-permute-start | bytes 208904 | tf_op jit(solution)/shard_map/ppermute | solution.py:620
  63.1 21.0 %all-to-all-start.2 = ((bf16[8,16,2176]{2,1,0:T(8,128)(2,1)}), bf16[8,16,2176]{2,1,0:T(8,128)(2,1)S(1)}, u32[]{:S(2)}, u32[]{:S(2)}) async-start(bf16[8,16,2176]{2,1,0:T(8,128)(2,1)} %get-tuple-element.53), calls=%async_computation.2 | async-start | bytes 1114112 | tf_op jit(solution)/shard_map/all_to_all | solution.py:605
  67.6 8.0 %collective-permute-start.10 = (bf16[4,16,2176]{2,1,0:T(8,128)(2,1)S(1)}, bf16[4,16,2176]{2,1,0:T(8,128)(2,1)S(1)}, u32[]{:S(2)}, u32[]{:S(2)}) collective-permute-start(bf16[4,16,2176]{2,1,0:T(8,128)(2,1)S(1)} %get-tuple-element.55.b0), channel_id=1, source_target_pairs={{0,2},{1,3},{2,4},{3,5},{4,6},{5,7},{6,0},{7,1},{8,10},{9,11},{10,... | collective-permute-start | bytes 835592 | tf_op jit(solution)/shard_map/ppermute | solution.py:620
  68.8 6.8 %collective-permute-start.8 = (bf16[4,16,2176]{2,1,0:T(8,128)(2,1)S(1)}, bf16[4,16,2176]{2,1,0:T(8,128)(2,1)S(1)}, u32[]{:S(2)}, u32[]{:S(2)}) collective-permute-start(bf16[4,16,2176]{2,1,0:T(8,128)(2,1)S(1)} %get-tuple-element.55.b0), channel_id=1, source_target_pairs={{0,6},{1,7},{2,0},{3,1},{4,2},{5,3},{6,4},{7,5},{8,14},{9,15},{10,... | collective-permute-start | bytes 835592 | tf_op jit(solution)/shard_map/ppermute | solution.py:620
  70.3 9.7 %collective-permute-start.9 = (bf16[4,16,2176]{2,1,0:T(8,128)(2,1)S(1)}, bf16[4,16,2176]{2,1,0:T(8,128)(2,1)S(1)}, u32[]{:S(2)}, u32[]{:S(2)}) collective-permute-start(bf16[4,16,2176]{2,1,0:T(8,128)(2,1)S(1)} %get-tuple-element.55.b0), channel_id=1, source_target_pairs={{0,4},{1,5},{2,6},{3,7},{4,0},{5,1},{6,2},{7,3},{8,12},{9,13},{10,... | collective-permute-start | bytes 835592 | tf_op jit(solution)/shard_map/ppermute | solution.py:620
  86.3 4.2 %copy-start.2 = (f32[2,2048]{1,0:T(2,128)S(1)}, f32[2,2048]{1,0:T(2,128)}, u32[]{:S(2)}) copy-start(f32[2,2048]{1,0:T(2,128)} %m_any.3) | copy-start | bytes 49156
  86.3 4.2 %copy-start.3 = (f32[2,2048]{1,0:T(2,128)S(1)}, f32[2,2048]{1,0:T(2,128)}, u32[]{:S(2)}) copy-start(f32[2,2048]{1,0:T(2,128)} %v_any.3) | copy-start | bytes 49156
  86.3 4.2 %copy-start.6 = (f32[2,8]{1,0:T(2,128)S(1)}, f32[2,8]{1,0:T(2,128)}, u32[]{:S(2)}) copy-start(f32[2,8]{1,0:T(2,128)} %bnm_any.3) | copy-start | bytes 196
  86.4 19.1 %all-to-all-start.3 = ((bf16[16,16,2176]{2,1,0:T(8,128)(2,1)}), bf16[16,16,2176]{2,1,0:T(8,128)(2,1)S(1)}, u32[]{:S(2)}, u32[]{:S(2)}) async-start(bf16[16,16,2176]{2,1,0:T(8,128)(2,1)} %get-tuple-element.57), calls=%async_computation.3 | async-start | bytes 2228224 | tf_op jit(solution)/shard_map/all_to_all | solution.py:605
  92.9 16.3 %collective-permute-start.12 = (bf16[256,2176]{1,0:T(8,128)(2,1)S(1)}, bf16[256,2176]{1,0:T(8,128)(2,1)S(1)}, u32[]{:S(2)}, u32[]{:S(2)}) collective-permute-start(bf16[256,2176]{1,0:T(8,128)(2,1)S(1)} %bitcast.5), channel_id=1, source_target_pairs={{0,1},{1,0},{2,3},{3,2},{4,5},{5,4},{6,7},{7,6},{8,9},{9,8},{10,11... | collective-permute-start | bytes 3342344 | tf_op jit(solution)/shard_map/ppermute | solution.py:645
  105.4 6.2 %collective-permute-start.11 = (bf16[256,2176]{1,0:T(8,128)(2,1)S(1)}, bf16[256,2176]{1,0:T(8,128)(2,1)S(1)}, u32[]{:S(2)}, u32[]{:S(2)}) collective-permute-start(bf16[256,2176]{1,0:T(8,128)(2,1)S(1)} %bitcast.3), channel_id=1, source_target_pairs={{0,1},{1,0},{2,3},{3,2},{4,5},{5,4},{6,7},{7,6},{8,9},{9,8},{10,11... | collective-permute-start | bytes 3342344 | tf_op jit(solution)/shard_map/ppermute | solution.py:647

commit v5 on v4

--- a/solution.py
+++ b/solution.py
@@ -104,12 +104,22 @@
     return block
 
 
+def kept_part(pre, cot):
+    return jnp.where(pre > 0, cot, jnp.zeros_like(cot))
+
+
 def stats_kernel(
     f_any, w_any, cot_any, pre_any, m_any, v_any, bn_any, bnm_any,
     stat_ref, base_ref,
     f, w, cot, pre, master, momentum, bn, bnm, sems,
 ):
     mine = place()
+    small = [
+        copy(m_any, master, sems.at[1, STAT_STEPS]),
+        copy(v_any, momentum, sems.at[2, STAT_STEPS]),
+        copy(bn_any, bn, sems.at[3, STAT_STEPS]),
+        copy(bnm_any, bnm, sems.at[4, 0]),
+    ]
     first = copy(f_any, f, sems.at[0, STAT_STEPS])
     loads = []
     for j in range(STAT_STEPS):
@@ -120,19 +130,26 @@
                 copy(pre_any.at[:, stat_cols(j)], pre.at[:, stat_cols(j)], sems.at[2, j]),
             ]
         )
-    small = [
-        copy(m_any, master, sems.at[1, STAT_STEPS]),
-        copy(v_any, momentum, sems.at[2, STAT_STEPS]),
-        copy(bn_any, bn, sems.at[3, STAT_STEPS]),
-        copy(bnm_any, bnm, sems.at[4, 0]),
-    ]
+    for load in small:
+        load.wait()
+    base_ref[:, 0:C] = (master[...] - momentum_rate * momentum[...]).astype(BF)
+    base_ref[:, C : 2 * C] = master[...].astype(BF)
+    own_bn = own_block(bn[...], mine)
+    lane = lax.broadcasted_iota(jnp.int32, (2, EXT), 1)
+    bn_base = own_bn - momentum_rate * jnp.concatenate([bnm[...]] * 16, axis=1)
+    base_ref[:, 2 * C : 2 * C + EXT] = jnp.where((lane >> 3) == (mine & 15), bn_base, 0.0).astype(BF)
+    square = jnp.sum(master[...] * master[...], axis=(0, 1), keepdims=True)
+    row = lax.broadcasted_iota(jnp.int32, (2, EXT), 0)
+    hi, lo = hi_lo(square)
+    square = jnp.where(lane == 0, hi, jnp.where(lane == 1, lo, 0.0))
+    base_ref[:, 2 * C + EXT :] = jnp.where(row == 0, square, 0.0).astype(BF)
     first.wait()
     for j in range(STAT_STEPS):
         loads[j][0].wait()
         conv = jnp.dot(f[...], w[:, stat_cols(j)], preferred_element_type=F32)
         loads[j][1].wait()
         loads[j][2].wait()
-        u = jnp.where(pre[:, stat_cols(j)].astype(F32) > 0, cot[:, stat_cols(j)].astype(F32), 0.0)
+        u = kept_part(pre[:, stat_cols(j)], cot[:, stat_cols(j)]).astype(F32)
         stat = jnp.concatenate(
             [
                 jnp.sum(conv, axis=0, keepdims=True),
@@ -143,19 +160,6 @@
             axis=0,
         )
         stat_ref[:, :, stat_cols(j)] = jnp.broadcast_to(stat[None], (8, 4, STAT_COLS))
-    for load in small:
-        load.wait()
-    base_ref[:, 0:C] = master[...] - momentum_rate * momentum[...]
-    base_ref[:, C : 2 * C] = master[...]
-    own_bn = own_block(bn[...], mine)
-    lane = lax.broadcasted_iota(jnp.int32, (2, EXT), 1)
-    bn_base = own_bn - momentum_rate * jnp.concatenate([bnm[...]] * 16, axis=1)
-    base_ref[:, 2 * C : 2 * C + EXT] = jnp.where((lane >> 3) == (mine & 15), bn_base, 0.0)
-    square = jnp.sum(master[...] * master[...], axis=(0, 1), keepdims=True)
-    row = lax.broadcasted_iota(jnp.int32, (2, EXT), 0)
-    hi, lo = hi_lo(square)
-    square = jnp.where(lane == 0, hi, jnp.where(lane == 1, lo, 0.0))
-    base_ref[:, 2 * C + EXT :] = jnp.where(row == 0, square, 0.0)
 
 
 def stats_call(features, weight, cotangent, pre_act, master, momentum, bn_params, bn_momentum):
@@ -165,7 +169,7 @@
         out_specs=[VMEM, VMEM],
         out_shape=[
             jax.ShapeDtypeStruct((8, 4, C), F32),
-            jax.ShapeDtypeStruct((2, PIECE), F32),
+            jax.ShapeDtypeStruct((2, PIECE), BF),
         ],
         scratch_shapes=[
             pltpu.VMEM((ROWS, CB), BF),
@@ -214,10 +218,10 @@
         stores.append(copy(mid.at[:, cols(j)], kept_any.at[pl.ds(TALL, TALL), cols(j)], sems.at[4, j]))
         loads[j][1].wait()
         loads[j][2].wait()
-        u = jnp.where(pre[:, cols(j)].astype(F32) > 0, cot[:, cols(j)].astype(F32), 0.0)
-        up[:, cols(j)] = u.astype(BF)
+        u = kept_part(pre[:, cols(j)], cot[:, cols(j)])
+        up[:, cols(j)] = u
         stores.append(copy(up.at[:, cols(j)], up_any.at[:, cols(j)], sems.at[3, j]))
-        tall[:, cols(j)] = jnp.concatenate([u, blank], axis=0).astype(BF)
+        tall[:, cols(j)] = jnp.concatenate([u.astype(F32), blank], axis=0).astype(BF)
         stores.append(copy(tall.at[:, cols(j)], kept_any.at[pl.ds(0, TALL), cols(j)], sems.at[6, j]))
     for store in stores:
         store.wait()
@@ -259,8 +263,9 @@
     c, zh = lax.axis_index("c"), lax.axis_index("zh")
     up = kept.at[0:TALL]
     mid = kept.at[TALL : 2 * TALL]
-    low = jnp.where(zh == 0, p0[...], p1[...])
-    high = jnp.where(zh == 0, p1[...], p0[...])
+    mine, far = p0[...].astype(F32), p1[...].astype(F32)
+    low = jnp.where(zh == 0, mine, far)
+    high = jnp.where(zh == 0, far, mine)
     near_ref[...] = jnp.concatenate([low, high], axis=0).astype(BF)
     sums = jnp.sum(stat[...], axis=0)
     mean = sums[0:1] / COUNT
@@ -358,7 +363,7 @@
     )(weight, kept, coef, after)
 
 
-def rows_kernel(n0, n1, n2, n3, after_ref, base_ref, w_any, four, w, sem):
+def rows_kernel(n0, n1, n2, n3, after_ref, base_ref, w, four):
     zl = lax.axis_index("zl")
     halves = []
     for high in range(2):
@@ -368,19 +373,17 @@
     both = jnp.concatenate(halves, axis=0)
     w[:, :C] = both[:, C : 2 * C]
     w[:, C:] = both[:, 2 * C + EXT :]
-    store = copy(w, w_any, sem)
     base_ref[:, :C] = both[:, :C].astype(BF)
     base_ref[:, C:] = both[:, 2 * C : 2 * C + EXT].astype(BF)
-    store.wait()
 
 
 def rows_call(blocks, after):
     return pl.pallas_call(
         rows_kernel,
         in_specs=[VMEM] * 4 + [SMEM],
-        out_specs=[VMEM, ANY],
+        out_specs=[VMEM, VMEM],
         out_shape=[jax.ShapeDtypeStruct((16, WIDE), BF), jax.ShapeDtypeStruct((16, WIDE), F32)],
-        scratch_shapes=[pltpu.VMEM((8, PIECE), F32), pltpu.VMEM((16, WIDE), F32), DMA],
+        scratch_shapes=[pltpu.VMEM((8, PIECE), F32)],
         compiler_params=params(),
         cost_estimate=pl.CostEstimate(flops=16 * PIECE, bytes_accessed=500000, transcendentals=0),
         name="rows",
@@ -433,14 +436,12 @@
     )(got, *bases)
 
 
-def column_kernel(got_ref, w_any, b1, b2, b3, after_ref, out_ref, own_ref, token_ref, w, sem):
+def column_kernel(got_ref, w, b1, b2, b3, out_ref, own_ref, token_ref):
     done(token_ref)
-    load = copy(w_any, w, sem)
     z = 4 * lax.axis_index("zh") + lax.axis_index("zl")
     total = jnp.sum(got_ref[...].astype(F32), axis=0)
     g = total[:, :C]
     g_hi, g_lo = hi_lo(jnp.sum(g * g, axis=(0, 1), keepdims=True))
-    load.wait()
     w_hi, w_lo = hi_lo(jnp.sum(w[:, C:], axis=(0, 1), keepdims=True))
     row = lax.broadcasted_iota(jnp.int32, (16, EXT), 0)
     lane = lax.broadcasted_iota(jnp.int32, (16, EXT), 1)
@@ -454,24 +455,23 @@
     own_ref[...] = pltpu.roll(g, (16 - 2 * z) & 15, 0)[0:2]
 
 
-def column_call(got, w_rows, bases, after):
+def column_call(got, w_rows, bases):
     return pl.pallas_call(
         column_kernel,
-        in_specs=[VMEM] + [ANY] * 4 + [SMEM],
+        in_specs=[VMEM] * 2 + [ANY] * 3,
         out_specs=[VMEM, VMEM, SMEM],
         out_shape=[
             jax.ShapeDtypeStruct((16, 16, WIDE), BF),
             jax.ShapeDtypeStruct((2, C), F32),
             TOKEN,
         ],
-        scratch_shapes=[pltpu.VMEM((16, WIDE), F32), DMA],
         compiler_params=params(),
         cost_estimate=pl.CostEstimate(flops=128 * WIDE, bytes_accessed=1700000, transcendentals=0),
         name="column",
-    )(got, w_rows, *bases, after)
-
-
-def basis_kernel(b0, b1, b2, b3, m_any, v_any, bnm_any, after_ref, base_any, keep_ref, bnm, sems):
+    )(got, w_rows, *bases)
+
+
+def basis_kernel(b0, b1, b2, b3, m_any, v_any, bnm_any, after_ref, input_ref, base_any, keep_ref, bnm, sems):
     y = lax.axis_index("y")
     stores = [
         copy(m_any, keep_ref.at[:, pl.ds(0, C)], sems.at[16]),
@@ -487,17 +487,17 @@
         store.wait()
 
 
-def basis_call(bases, master, momentum, bn_momentum, after):
+def basis_call(bases, master, momentum, bn_momentum, *after):
     return pl.pallas_call(
         basis_kernel,
-        in_specs=[ANY] * 7 + [SMEM],
+        in_specs=[ANY] * 7 + [SMEM] * 2,
         out_specs=[ANY, VMEM],
         out_shape=[jax.ShapeDtypeStruct((16, 16, WIDE), BF), jax.ShapeDtypeStruct((2, 2 * C + EXT), F32)],
         scratch_shapes=[pltpu.VMEM((2, 8), F32), DMA((19,))],
         compiler_params=params(),
         cost_estimate=pl.CostEstimate(flops=0, bytes_accessed=2200000, transcendentals=0),
         name="basis",
-    )(*bases, master, momentum, bn_momentum, after)
+    )(*bases, master, momentum, bn_momentum, *after)
 
 
 def update_kernel(
@@ -638,9 +638,9 @@
     bases = ring(base, 4, lambda k, x, y, z: ((x + k) % 4, y, z))
     part, base, token = plane_call(exchange(half.reshape(16, 16, WIDE), XY), bases)
     bases = ring(base, 4, lambda k, x, y, z: (x, (y + k) % 4, z))
-    grad_input, token = input_call(weight, kept, coef, token)
-    step, g_own, token = column_call(exchange(part, Z), w_rows, bases[1:], token)
-    a0, keep = basis_call(bases, master, momentum, bn_momentum, token)
+    grad_input, ready = input_call(weight, kept, coef, token)
+    step, g_own, token = column_call(exchange(part, Z), w_rows, bases[1:])
+    a0, keep = basis_call(bases, master, momentum, bn_momentum, token, ready)
     a0 = a0.reshape(256, WIDE)
     a1 = swap(a0)
     b0 = exchange(step, XY).reshape(256, WIDE)

time: 115 us -> 114 us (level)
    all_to_all x4, waiting for transfers between devices: 13.5 us -> 8.5 us  [exchange(): return lax.all_to_all(block, axes, 0, 0, tiled=True)]
    ppermute x9, waiting for transfers between devices: 13.6 us -> 18.6 us  [ring(): lax.ppermute(block, AXES, shift_pairs(functools.partial(move, size - k)))]
  transfers between devices with their start and end apart: 17 -> 17, of which waited for: 11 -> 11; matrix products, arithmetic and copies ran while one was open for 0% -> 0% of each run, Pallas kernels for 11% -> 12%
where the time goes in v5:
time: 114 us; the launch traced here: 113 us
  starting transfers between devices  51.9 us (46%)
  waiting for transfers between devices  31.8 us (28%)
  Pallas kernels  26.2 us (23%)
  local copies, waits for them, and re-layouts  2.1 us (2%)
    all_to_all x4, starting transfers between devices, exchange(): return lax.all_to_all(block, axes, 0, 0, tiled=True)  26.8 us
    ppermute x9, waiting for transfers between devices, ring(): lax.ppermute(block, AXES, shift_pairs(functools.partial(move, size - k)))  18.6 us
    ppermute x9, starting transfers between devices, ring(): lax.ppermute(block, AXES, shift_pairs(functools.partial(move, size - k)))  10.8 us
    all_to_all x4, waiting for transfers between devices, exchange(): return lax.all_to_all(block, axes, 0, 0, tiled=True)  8.5 us
    ppermute x1, starting transfers between devices, shards(): lax.ppermute(piece, AXES, shift_pairs(lambda x, y, z: (x, y, z ^ 4)))  5.36 us
    pallas_call x1, Pallas kernels, prep_call(): pl.pallas_call(prep_kernel, in_specs=[ANY] * 4, out_specs=[ANY, ANY], out...  5.06 us
    pallas_call x1, Pallas kernels, stats_call(): pl.pallas_call(stats_kernel, in_specs=[ANY] * 8, out_specs=[VMEM, VMEM],...  4.57 us
    pallas_call x1, Pallas kernels, input_call(): pl.pallas_call(input_kernel, in_specs=[ANY] * 3 + [SMEM], out_specs=[VMEM...  4.53 us
  transfers between devices with their start and end apart: 17, of which 11 were waited for; matrix products, arithmetic and copies ran while one was open for 0% of the time, Pallas kernels for 12%

profile of v5, /device:TPU:1, one launch (start us, length us, event | category | flops | bytes accessed | tf_op | source)
XLA Modules:
  0.0 113.0 jit_solution(4232536163456512682)
XLA Ops:
  0.6 4.6 %stats.1 = (f32[8,4,2048]{2,1,0:T(4,128)}, bf16[2,4352]{1,0:T(2,128)(2,1)}) custom-call(bf16[392,512]{1,0:T(8,128)(2,1)} %f_any.2, bf16[512,2048]{1,0:T(8,128)(2,1)} %w_any.5, bf16[392,2048]{1,0:T(8,128)(2,1)} %cot_any.3, bf16[392,2048]{1,0:T(8,128)(2,1)} %pre_any.3, f32[2,2048]{1,0:T(2,128)} %m_any.3, f32[2,2048]{1,0:T(2,128)} %v_any.3, f32[2,2048]{1,0:T(2,128)} %bn_v.1, ...), custom_call_target="tpu_custom_call" | custom-call | flops 822083584 | bytes 7500000 | tf_op jit(solution)/shard_map/stats/pallas_call | solution.py:166
  5.2 11.5 %all-to-all-start = ((f32[8,4,2048]{2,1,0:T(4,128)}), f32[8,4,2048]{2,1,0:T(4,128)S(1)}, u32[]{:S(2)}, u32[]{:S(2)}) async-start(f32[8,4,2048]{2,1,0:T(4,128)} %get-tuple-element.41), calls=%async_computation | async-start | bytes 524288 | tf_op jit(solution)/shard_map/all_to_all | solution.py:605
  16.7 0.0 copy-start.1
  16.7 0.0 copy-start.5
  16.7 5.4 %collective-permute-start = (bf16[2,4352]{1,0:T(2,128)(2,1)}, bf16[2,4352]{1,0:T(2,128)(2,1)S(1)}, u32[]{:S(2)}, u32[]{:S(2)}) collective-permute-start(bf16[2,4352]{1,0:T(2,128)(2,1)} %get-tuple-element.42.p0), channel_id=1, source_target_pairs={{0,128},{1,129},{2,130},{3,131},{4,132},{5,133},{6,134},{7,135},{8... | collective-permute-start | bytes 52232 | tf_op jit(solution)/shard_map/ppermute | solution.py:630
  22.1 5.1 %prep.1 = (bf16[392,2048]{1,0:T(8,128)(2,1)}, bf16[928,2048]{1,0:T(8,128)(2,1)}) custom-call(bf16[392,512]{1,0:T(8,128)(2,1)} %f_any.2, bf16[512,2048]{1,0:T(8,128)(2,1)} %w_any.5, bf16[392,2048]{1,0:T(8,128)(2,1)} %cot_any.3, bf16[392,2048]{1,0:T(8,128)(2,1)} %pre_any.3), custom_call_target="tpu_custom_call" | custom-call | flops 1233125376 | bytes 9000000 | tf_op jit(solution)/shard_map/prep/pallas_call | solution.py:231
  27.1 0.0 collective-permute-done.p1
  27.1 0.0 all-to-all-done.stat
  27.2 0.0 copy-done.1
  27.2 0.0 copy-done.5
  27.2 0.0 copy-start
  27.2 2.1 %copy-done = bf16[928,2048]{1,0:T(8,128)(2,1)S(1)} copy-done((bf16[928,2048]{1,0:T(8,128)(2,1)S(1)}, bf16[928,2048]{1,0:T(8,128)(2,1)}, u32[]{:S(2)}) %copy-start) | copy-done | bytes 3801112
  29.3 1.5 %grad.1 = (bf16[256,2176]{1,0:T(8,128)(2,1)S(1)}, bf16[256,2176]{1,0:T(8,128)(2,1)S(1)}, bf16[4,4352]{1,0:T(4,128)(2,1)S(1)}, f32[4,2048]{1,0:T(4,128)S(1)}) custom-call(f32[8,4,2048]{2,1,0:T(4,128)S(1)} %all-to-all-done.stat, bf16[928,2048]{1,0:T(8,128)(2,1)S(1)} %copy-done, f32[2,2048]{1,0:T(2,128)S(1)} %copy-done.1, bf16[2,4352]{1,0:T(2,128)(2,1)S(1)} %copy-done.5, ...), custom_call_target="tpu_custom_call" | custom-call | flops 822083584 | bytes 7000000 | tf_op jit(solution)/shard_map/grad/pallas_call | solution.py:301
  30.7 0.0 copy-start.4
  30.7 2.2 %collective-permute-start.1 = (bf16[256,2176]{1,0:T(8,128)(2,1)S(1)}, bf16[256,2176]{1,0:T(8,128)(2,1)S(1)}, u32[]{:S(2)}, u32[]{:S(2)}) collective-permute-start(bf16[256,2176]{1,0:T(8,128)(2,1)S(1)} %get-tuple-element.45), channel_id=1, source_target_pairs={{0,1},{1,0},{2,3},{3,2},{4,5},{5,4},{6,7},{7,6},{8,9},{9,8},{10,11... | collective-permute-start | bytes 3342344 | tf_op jit(solution)/shard_map/ppermute | solution.py:635
  32.9 2.4 %collective-permute-done.1.got_ref = bf16[256,2176]{1,0:T(8,128)(2,1)S(1)} collective-permute-done((bf16[256,2176]{1,0:T(8,128)(2,1)S(1)}, bf16[256,2176]{1,0:T(8,128)(2,1)S(1)}, u32[]{:S(2)}, u32[]{:S(2)}) %collective-permute-start.1) | collective-permute-done | bytes 1114144 | tf_op jit(solution)/shard_map/ppermute | solution.py:635
  35.3 1.3 %pair.1 = (bf16[256,2176]{1,0:T(8,128)(2,1)}, s32[1]{0:T(128)}) custom-call(bf16[256,2176]{1,0:T(8,128)(2,1)S(1)} %get-tuple-element.44.own_ref, bf16[256,2176]{1,0:T(8,128)(2,1)S(1)} %collective-permute-done.1.got_ref), custom_call_target="tpu_custom_call" | custom-call | flops 557056 | bytes 3300000 | tf_op jit(solution)/shard_map/pair/pallas_call | solution.py:399
  36.6 0.0 copy-done.4
  36.6 6.8 %all-to-all-start.1 = ((bf16[16,16,2176]{2,1,0:T(8,128)(2,1)}), bf16[16,16,2176]{2,1,0:T(8,128)(2,1)S(1)}, u32[]{:S(2)}, u32[]{:S(2)}) async-start(bf16[16,16,2176]{2,1,0:T(8,128)(2,1)} %bitcast), calls=%async_computation.1 | async-start | bytes 2228224 | tf_op jit(solution)/shard_map/all_to_all | solution.py:605
  43.3 1.7 %collective-permute-start.2 = (bf16[4,4352]{1,0:T(4,128)(2,1)S(1)}, bf16[4,4352]{1,0:T(4,128)(2,1)S(1)}, u32[]{:S(2)}, u32[]{:S(2)}) collective-permute-start(bf16[4,4352]{1,0:T(4,128)(2,1)S(1)} %get-tuple-element.47.n0), channel_id=1, source_target_pairs={{0,24},{1,25},{2,26},{3,27},{4,28},{5,29},{6,30},{7,31},{8,0},{9,1... | collective-permute-start | bytes 104456 | tf_op jit(solution)/shard_map/ppermute | solution.py:620
  45.0 1.3 %collective-permute-start.3 = (bf16[4,4352]{1,0:T(4,128)(2,1)S(1)}, bf16[4,4352]{1,0:T(4,128)(2,1)S(1)}, u32[]{:S(2)}, u32[]{:S(2)}) collective-permute-start(bf16[4,4352]{1,0:T(4,128)(2,1)S(1)} %get-tuple-element.47.n0), channel_id=1, source_target_pairs={{0,16},{1,17},{2,18},{3,19},{4,20},{5,21},{6,22},{7,23},{8,24},{9,... | collective-permute-start | bytes 104456 | tf_op jit(solution)/shard_map/ppermute | solution.py:620
  46.3 0.7 collective-permute-start.4
  47.0 0.0 collective-permute-done.2.n1
  47.1 2.6 %collective-permute-done.3.n2 = bf16[4,4352]{1,0:T(4,128)(2,1)S(1)} collective-permute-done((bf16[4,4352]{1,0:T(4,128)(2,1)S(1)}, bf16[4,4352]{1,0:T(4,128)(2,1)S(1)}, u32[]{:S(2)}, u32[]{:S(2)}) %collective-permute-start.3) | collective-permute-done | bytes 34848 | tf_op jit(solution)/shard_map/ppermute | solution.py:620
  49.7 1.2 %collective-permute-done.4.n3 = bf16[4,4352]{1,0:T(4,128)(2,1)S(1)} collective-permute-done((bf16[4,4352]{1,0:T(4,128)(2,1)S(1)}, bf16[4,4352]{1,0:T(4,128)(2,1)S(1)}, u32[]{:S(2)}, u32[]{:S(2)}) %collective-permute-start.4) | collective-permute-done | bytes 34848 | tf_op jit(solution)/shard_map/ppermute | solution.py:620
  50.9 0.8 rows.1
  51.7 2.9 %collective-permute-start.5 = (bf16[16,2176]{1,0:T(8,128)(2,1)S(1)}, bf16[16,2176]{1,0:T(8,128)(2,1)S(1)}, u32[]{:S(2)}, u32[]{:S(2)}) collective-permute-start(bf16[16,2176]{1,0:T(8,128)(2,1)S(1)} %get-tuple-element.49.b0), channel_id=1, source_target_pairs={{0,96},{1,97},{2,98},{3,99},{4,100},{5,101},{6,102},{7,103},{8,104... | collective-permute-start | bytes 208904 | tf_op jit(solution)/shard_map/ppermute | solution.py:620
  54.5 0.6 collective-permute-start.6
  55.1 0.6 collective-permute-start.7
  55.7 2.9 %collective-permute-done.5.b1 = bf16[16,2176]{1,0:T(8,128)(2,1)S(1)} collective-permute-done((bf16[16,2176]{1,0:T(8,128)(2,1)S(1)}, bf16[16,2176]{1,0:T(8,128)(2,1)S(1)}, u32[]{:S(2)}, u32[]{:S(2)}) %collective-permute-start.5) | collective-permute-done | bytes 69664 | tf_op jit(solution)/shard_map/ppermute | solution.py:620
  58.5 1.8 %collective-permute-done.6.b2 = bf16[16,2176]{1,0:T(8,128)(2,1)S(1)} collective-permute-done((bf16[16,2176]{1,0:T(8,128)(2,1)S(1)}, bf16[16,2176]{1,0:T(8,128)(2,1)S(1)}, u32[]{:S(2)}, u32[]{:S(2)}) %collective-permute-start.6) | collective-permute-done | bytes 69664 | tf_op jit(solution)/shard_map/ppermute | solution.py:620
  60.3 0.8 collective-permute-done.7.b3
  61.1 0.0 all-to-all-done.1.got_ref
  61.1 1.4 %plane.1 = (bf16[8,16,2176]{2,1,0:T(8,128)(2,1)}, bf16[4,16,2176]{2,1,0:T(8,128)(2,1)S(1)}, s32[1]{0:T(128)}) custom-call(bf16[16,16,2176]{2,1,0:T(8,128)(2,1)S(1)} %all-to-all-done.1.got_ref, bf16[16,2176]{1,0:T(8,128)(2,1)S(1)} %get-tuple-element.49.b0, bf16[16,2176]{1,0:T(8,128)(2,1)S(1)} %collective-permute-done.5.b1, ...), custom_call_target="tpu_custom_call" | custom-call | flops 557056 | bytes 1700000 | tf_op jit(solution)/shard_map/plane/pallas_call | solution.py:423
  62.5 4.3 %all-to-all-start.2 = ((bf16[8,16,2176]{2,1,0:T(8,128)(2,1)}), bf16[8,16,2176]{2,1,0:T(8,128)(2,1)S(1)}, u32[]{:S(2)}, u32[]{:S(2)}) async-start(bf16[8,16,2176]{2,1,0:T(8,128)(2,1)} %get-tuple-element.53), calls=%async_computation.2 | async-start | bytes 1114112 | tf_op jit(solution)/shard_map/all_to_all | solution.py:605
  66.8 1.2 %collective-permute-start.10 = (bf16[4,16,2176]{2,1,0:T(8,128)(2,1)S(1)}, bf16[4,16,2176]{2,1,0:T(8,128)(2,1)S(1)}, u32[]{:S(2)}, u32[]{:S(2)}) collective-permute-start(bf16[4,16,2176]{2,1,0:T(8,128)(2,1)S(1)} %get-tuple-element.55.b0), channel_id=1, source_target_pairs={{0,2},{1,3},{2,4},{3,5},{4,6},{5,7},{6,0},{7,1},{8,10},{9,11},{10,... | collective-permute-start | bytes 835592 | tf_op jit(solution)/shard_map/ppermute | solution.py:620
  67.9 1.5 %collective-permute-start.8 = (bf16[4,16,2176]{2,1,0:T(8,128)(2,1)S(1)}, bf16[4,16,2176]{2,1,0:T(8,128)(2,1)S(1)}, u32[]{:S(2)}, u32[]{:S(2)}) collective-permute-start(bf16[4,16,2176]{2,1,0:T(8,128)(2,1)S(1)} %get-tuple-element.55.b0), channel_id=1, source_target_pairs={{0,6},{1,7},{2,0},{3,1},{4,2},{5,3},{6,4},{7,5},{8,14},{9,15},{10,... | collective-permute-start | bytes 835592 | tf_op jit(solution)/shard_map/ppermute | solution.py:620
  69.4 0.4 collective-permute-start.9
  69.8 4.9 %collective-permute-done.10.b3 = bf16[4,16,2176]{2,1,0:T(8,128)(2,1)S(1)} collective-permute-done((bf16[4,16,2176]{2,1,0:T(8,128)(2,1)S(1)}, bf16[4,16,2176]{2,1,0:T(8,128)(2,1)S(1)}, u32[]{:S(2)}, u32[]{:S(2)}) %collective-permute-start.10) | collective-permute-done | bytes 278560 | tf_op jit(solution)/shard_map/ppermute | solution.py:620
  74.8 0.0 collective-permute-done.8.b1
  74.8 4.4 %collective-permute-done.9.b2 = bf16[4,16,2176]{2,1,0:T(8,128)(2,1)S(1)} collective-permute-done((bf16[4,16,2176]{2,1,0:T(8,128)(2,1)S(1)}, bf16[4,16,2176]{2,1,0:T(8,128)(2,1)S(1)}, u32[]{:S(2)}, u32[]{:S(2)}) %collective-permute-start.9) | collective-permute-done | bytes 278560 | tf_op jit(solution)/shard_map/ppermute | solution.py:620
  79.2 4.1 %all-to-all-done.2.got_ref = bf16[8,16,2176]{2,1,0:T(8,128)(2,1)S(1)} async-done(((bf16[8,16,2176]{2,1,0:T(8,128)(2,1)}), bf16[8,16,2176]{2,1,0:T(8,128)(2,1)S(1)}, u32[]{:S(2)}, u32[]{:S(2)}) %all-to-all-start.2) | async-done | bytes 557088 | tf_op jit(solution)/shard_map/all_to_all | solution.py:605
  83.3 1.2 %column.1 = (bf16[16,16,2176]{2,1,0:T(8,128)(2,1)}, f32[2,2048]{1,0:T(2,128)S(1)}, s32[1]{0:T(128)}) custom-call(bf16[8,16,2176]{2,1,0:T(8,128)(2,1)S(1)} %all-to-all-done.2.got_ref, f32[16,2176]{1,0:T(8,128)S(1)} %get-tuple-element.54.w, bf16[4,16,2176]{2,1,0:T(8,128)(2,1)S(1)} %collective-permute-done.8.b1, ...), custom_call_target="tpu_custom_call" | custom-call | flops 278528 | bytes 1700000 | tf_op jit(solution)/shard_map/column/pallas_call | solution.py:459
  84.5 4.2 %all-to-all-start.3 = ((bf16[16,16,2176]{2,1,0:T(8,128)(2,1)}), bf16[16,16,2176]{2,1,0:T(8,128)(2,1)S(1)}, u32[]{:S(2)}, u32[]{:S(2)}) async-start(bf16[16,16,2176]{2,1,0:T(8,128)(2,1)} %get-tuple-element.56), calls=%async_computation.3 | async-start | bytes 2228224 | tf_op jit(solution)/shard_map/all_to_all | solution.py:605
  88.8 0.0 copy-start.2
  88.8 0.0 copy-start.3
  88.8 0.0 copy-start.6
  88.8 4.5 %ginput.1 = (bf16[392,512]{1,0:T(8,128)(2,1)}, s32[1]{0:T(128)}) custom-call(bf16[512,2048]{1,0:T(8,128)(2,1)} %w_any.5, bf16[928,2048]{1,0:T(8,128)(2,1)} %get-tuple-element.40.kept.kept_any, f32[4,2048]{1,0:T(4,128)} %copy-done.4, s32[1]{0:T(128)} %get-tuple-element.50.after_ref), custom_call_target="tpu_custom_call" | custom-call | flops 822083584 | bytes 5500000 | tf_op jit(solution)/shard_map/ginput/pallas_call | solution.py:348
  93.3 0.0 copy-done.2
  93.3 0.0 copy-done.3
  93.4 0.0 copy-done.6
  93.4 3.1 %basis.1 = (bf16[16,16,2176]{2,1,0:T(8,128)(2,1)S(1)}, f32[2,4224]{1,0:T(2,128)S(1)}) custom-call(bf16[4,16,2176]{2,1,0:T(8,128)(2,1)S(1)} %get-tuple-element.55.b0, bf16[4,16,2176]{2,1,0:T(8,128)(2,1)S(1)} %collective-permute-done.8.b1, bf16[4,16,2176]{2,1,0:T(8,128)(2,1)S(1)} %collective-permute-done.9.b2, ...), custom_call_target="tpu_custom_call" | custom-call | bytes 2200000 | tf_op jit(solution)/shard_map/basis/pallas_call | solution.py:491
  96.4 3.0 %collective-permute-start.12 = (bf16[256,2176]{1,0:T(8,128)(2,1)S(1)}, bf16[256,2176]{1,0:T(8,128)(2,1)S(1)}, u32[]{:S(2)}, u32[]{:S(2)}) collective-permute-start(bf16[256,2176]{1,0:T(8,128)(2,1)S(1)} %bitcast.5), channel_id=1, source_target_pairs={{0,1},{1,0},{2,3},{3,2},{4,5},{5,4},{6,7},{7,6},{8,9},{9,8},{10,11... | collective-permute-start | bytes 3342344 | tf_op jit(solution)/shard_map/ppermute | solution.py:645
  99.4 4.4 %all-to-all-done.3 = bf16[16,16,2176]{2,1,0:T(8,128)(2,1)S(1)} async-done(((bf16[16,16,2176]{2,1,0:T(8,128)(2,1)}), bf16[16,16,2176]{2,1,0:T(8,128)(2,1)S(1)}, u32[]{:S(2)}, u32[]{:S(2)}) %all-to-all-start.3) | async-done | bytes 1114144 | tf_op jit(solution)/shard_map/all_to_all | solution.py:605
  103.8 3.7 %collective-permute-start.11 = (bf16[256,2176]{1,0:T(8,128)(2,1)S(1)}, bf16[256,2176]{1,0:T(8,128)(2,1)S(1)}, u32[]{:S(2)}, u32[]{:S(2)}) collective-permute-start(bf16[256,2176]{1,0:T(8,128)(2,1)S(1)} %bitcast.3), channel_id=1, source_target_pairs={{0,1},{1,0},{2,3},{3,2},{4,5},{5,4},{6,7},{7,6},{8,9},{9,8},{10,11... | collective-permute-start | bytes 3342344 | tf_op jit(solution)/shard_map/ppermute | solution.py:647
  107.5 0.0 collective-permute-done.12.a1
  107.5 2.4 %collective-permute-done.11.b1 = bf16[256,2176]{1,0:T(8,128)(2,1)S(1)} collective-permute-done((bf16[256,2176]{1,0:T(8,128)(2,1)S(1)}, bf16[256,2176]{1,0:T(8,128)(2,1)S(1)}, u32[]{:S(2)}, u32[]{:S(2)}) %collective-permute-start.11) | collective-permute-done | bytes 1114144 | tf_op jit(solution)/shard_map/ppermute | solution.py:647
  109.9 2.9 %update.1 = (bf16[512,2048]{1,0:T(8,128)(2,1)}, bf16[2,2048]{1,0:T(2,128)(2,1)}, f32[2,2048]{1,0:T(2,128)}, f32[2,2048]{1,0:T(2,128)}, f32[2,8]{1,0:T(2,128)}, /*index=5*/f32[2,8]{1,0:T(2,128)}) custom-call(bf16[256,2176]{1,0:T(8,128)(2,1)S(1)} %bitcast.4, bf16[256,2176]{1,0:T(8,128)(2,1)S(1)} %collective-permute-done.11.b1, bf16[256,2176]{1,0:T(8,128)(2,1)S(1)} %bitcast.6, ...), custom_call_target="tpu_custom_call" | custom-call | flops 268435456 | bytes 6500000 | tf_op jit(solution)/shard_map/update/pallas_call | solution.py:592
Async XLA Ops:
  5.2 21.9 %all-to-all-start = ((f32[8,4,2048]{2,1,0:T(4,128)}), f32[8,4,2048]{2,1,0:T(4,128)S(1)}, u32[]{:S(2)}, u32[]{:S(2)}) async-start(f32[8,4,2048]{2,1,0:T(4,128)} %get-tuple-element.41), calls=%async_computation | async-start | bytes 524288 | tf_op jit(solution)/shard_map/all_to_all | solution.py:605
  16.7 10.5 %copy-start.1 = (f32[2,2048]{1,0:T(2,128)S(1)}, f32[2,2048]{1,0:T(2,128)}, u32[]{:S(2)}) copy-start(f32[2,2048]{1,0:T(2,128)} %bn_v.1) | copy-start | bytes 49156
  16.7 10.5 %copy-start.5 = (bf16[2,4352]{1,0:T(2,128)(2,1)S(1)}, bf16[2,4352]{1,0:T(2,128)(2,1)}, u32[]{:S(2)}) copy-start(bf16[2,4352]{1,0:T(2,128)(2,1)} %get-tuple-element.42.p0) | copy-start | bytes 52228
  16.7 10.4 %collective-permute-start = (bf16[2,4352]{1,0:T(2,128)(2,1)}, bf16[2,4352]{1,0:T(2,128)(2,1)S(1)}, u32[]{:S(2)}, u32[]{:S(2)}) collective-permute-start(bf16[2,4352]{1,0:T(2,128)(2,1)} %get-tuple-element.42.p0), channel_id=1, source_target_pairs={{0,128},{1,129},{2,130},{3,131},{4,132},{5,133},{6,134},{7,135},{8... | collective-permute-start | bytes 52232 | tf_op jit(solution)/shard_map/ppermute | solution.py:630
  27.2 2.1 %copy-start = (bf16[928,2048]{1,0:T(8,128)(2,1)S(1)}, bf16[928,2048]{1,0:T(8,128)(2,1)}, u32[]{:S(2)}) copy-start(bf16[928,2048]{1,0:T(8,128)(2,1)} %get-tuple-element.40.kept.kept_any) | copy-start | bytes 11403268
  30.7 5.8 %copy-start.4 = (f32[4,2048]{1,0:T(4,128)}, f32[4,2048]{1,0:T(4,128)S(1)}, u32[]{:S(2)}) copy-start(f32[4,2048]{1,0:T(4,128)S(1)} %get-tuple-element.43.coef_any) | copy-start | bytes 98308
  30.7 4.5 %collective-permute-start.1 = (bf16[256,2176]{1,0:T(8,128)(2,1)S(1)}, bf16[256,2176]{1,0:T(8,128)(2,1)S(1)}, u32[]{:S(2)}, u32[]{:S(2)}) collective-permute-start(bf16[256,2176]{1,0:T(8,128)(2,1)S(1)} %get-tuple-element.45), channel_id=1, source_target_pairs={{0,1},{1,0},{2,3},{3,2},{4,5},{5,4},{6,7},{7,6},{8,9},{9,8},{10,11... | collective-permute-start | bytes 3342344 | tf_op jit(solution)/shard_map/ppermute | solution.py:635
  36.6 24.5 %all-to-all-start.1 = ((bf16[16,16,2176]{2,1,0:T(8,128)(2,1)}), bf16[16,16,2176]{2,1,0:T(8,128)(2,1)S(1)}, u32[]{:S(2)}, u32[]{:S(2)}) async-start(bf16[16,16,2176]{2,1,0:T(8,128)(2,1)} %bitcast), calls=%async_computation.1 | async-start | bytes 2228224 | tf_op jit(solution)/shard_map/all_to_all | solution.py:605
  43.3 3.7 %collective-permute-start.2 = (bf16[4,4352]{1,0:T(4,128)(2,1)S(1)}, bf16[4,4352]{1,0:T(4,128)(2,1)S(1)}, u32[]{:S(2)}, u32[]{:S(2)}) collective-permute-start(bf16[4,4352]{1,0:T(4,128)(2,1)S(1)} %get-tuple-element.47.n0), channel_id=1, source_target_pairs={{0,24},{1,25},{2,26},{3,27},{4,28},{5,29},{6,30},{7,31},{8,0},{9,1... | collective-permute-start | bytes 104456 | tf_op jit(solution)/shard_map/ppermute | solution.py:620
  45.0 4.6 %collective-permute-start.3 = (bf16[4,4352]{1,0:T(4,128)(2,1)S(1)}, bf16[4,4352]{1,0:T(4,128)(2,1)S(1)}, u32[]{:S(2)}, u32[]{:S(2)}) collective-permute-start(bf16[4,4352]{1,0:T(4,128)(2,1)S(1)} %get-tuple-element.47.n0), channel_id=1, source_target_pairs={{0,16},{1,17},{2,18},{3,19},{4,20},{5,21},{6,22},{7,23},{8,24},{9,... | collective-permute-start | bytes 104456 | tf_op jit(solution)/shard_map/ppermute | solution.py:620
  46.3 4.6 %collective-permute-start.4 = (bf16[4,4352]{1,0:T(4,128)(2,1)S(1)}, bf16[4,4352]{1,0:T(4,128)(2,1)S(1)}, u32[]{:S(2)}, u32[]{:S(2)}) collective-permute-start(bf16[4,4352]{1,0:T(4,128)(2,1)S(1)} %get-tuple-element.47.n0), channel_id=1, source_target_pairs={{0,8},{1,9},{2,10},{3,11},{4,12},{5,13},{6,14},{7,15},{8,16},{9,17... | collective-permute-start | bytes 104456 | tf_op jit(solution)/shard_map/ppermute | solution.py:620
  51.7 6.9 %collective-permute-start.5 = (bf16[16,2176]{1,0:T(8,128)(2,1)S(1)}, bf16[16,2176]{1,0:T(8,128)(2,1)S(1)}, u32[]{:S(2)}, u32[]{:S(2)}) collective-permute-start(bf16[16,2176]{1,0:T(8,128)(2,1)S(1)} %get-tuple-element.49.b0), channel_id=1, source_target_pairs={{0,96},{1,97},{2,98},{3,99},{4,100},{5,101},{6,102},{7,103},{8,104... | collective-permute-start | bytes 208904 | tf_op jit(solution)/shard_map/ppermute | solution.py:620
  54.5 5.8 %collective-permute-start.6 = (bf16[16,2176]{1,0:T(8,128)(2,1)S(1)}, bf16[16,2176]{1,0:T(8,128)(2,1)S(1)}, u32[]{:S(2)}, u32[]{:S(2)}) collective-permute-start(bf16[16,2176]{1,0:T(8,128)(2,1)S(1)} %get-tuple-element.49.b0), channel_id=1, source_target_pairs={{0,64},{1,65},{2,66},{3,67},{4,68},{5,69},{6,70},{7,71},{8,72},{9,... | collective-permute-start | bytes 208904 | tf_op jit(solution)/shard_map/ppermute | solution.py:620
  55.1 6.0 %collective-permute-start.7 = (bf16[16,2176]{1,0:T(8,128)(2,1)S(1)}, bf16[16,2176]{1,0:T(8,128)(2,1)S(1)}, u32[]{:S(2)}, u32[]{:S(2)}) collective-permute-start(bf16[16,2176]{1,0:T(8,128)(2,1)S(1)} %get-tuple-element.49.b0), channel_id=1, source_target_pairs={{0,32},{1,33},{2,34},{3,35},{4,36},{5,37},{6,38},{7,39},{8,40},{9,... | collective-permute-start | bytes 208904 | tf_op jit(solution)/shard_map/ppermute | solution.py:620
  62.5 20.8 %all-to-all-start.2 = ((bf16[8,16,2176]{2,1,0:T(8,128)(2,1)}), bf16[8,16,2176]{2,1,0:T(8,128)(2,1)S(1)}, u32[]{:S(2)}, u32[]{:S(2)}) async-start(bf16[8,16,2176]{2,1,0:T(8,128)(2,1)} %get-tuple-element.53), calls=%async_computation.2 | async-start | bytes 1114112 | tf_op jit(solution)/shard_map/all_to_all | solution.py:605
  66.8 8.0 %collective-permute-start.10 = (bf16[4,16,2176]{2,1,0:T(8,128)(2,1)S(1)}, bf16[4,16,2176]{2,1,0:T(8,128)(2,1)S(1)}, u32[]{:S(2)}, u32[]{:S(2)}) collective-permute-start(bf16[4,16,2176]{2,1,0:T(8,128)(2,1)S(1)} %get-tuple-element.55.b0), channel_id=1, source_target_pairs={{0,2},{1,3},{2,4},{3,5},{4,6},{5,7},{6,0},{7,1},{8,10},{9,11},{10,... | collective-permute-start | bytes 835592 | tf_op jit(solution)/shard_map/ppermute | solution.py:620
  67.9 6.8 %collective-permute-start.8 = (bf16[4,16,2176]{2,1,0:T(8,128)(2,1)S(1)}, bf16[4,16,2176]{2,1,0:T(8,128)(2,1)S(1)}, u32[]{:S(2)}, u32[]{:S(2)}) collective-permute-start(bf16[4,16,2176]{2,1,0:T(8,128)(2,1)S(1)} %get-tuple-element.55.b0), channel_id=1, source_target_pairs={{0,6},{1,7},{2,0},{3,1},{4,2},{5,3},{6,4},{7,5},{8,14},{9,15},{10,... | collective-permute-start | bytes 835592 | tf_op jit(solution)/shard_map/ppermute | solution.py:620
  69.4 9.7 %collective-permute-start.9 = (bf16[4,16,2176]{2,1,0:T(8,128)(2,1)S(1)}, bf16[4,16,2176]{2,1,0:T(8,128)(2,1)S(1)}, u32[]{:S(2)}, u32[]{:S(2)}) collective-permute-start(bf16[4,16,2176]{2,1,0:T(8,128)(2,1)S(1)} %get-tuple-element.55.b0), channel_id=1, source_target_pairs={{0,4},{1,5},{2,6},{3,7},{4,0},{5,1},{6,2},{7,3},{8,12},{9,13},{10,... | collective-permute-start | bytes 835592 | tf_op jit(solution)/shard_map/ppermute | solution.py:620
  84.5 19.3 %all-to-all-start.3 = ((bf16[16,16,2176]{2,1,0:T(8,128)(2,1)}), bf16[16,16,2176]{2,1,0:T(8,128)(2,1)S(1)}, u32[]{:S(2)}, u32[]{:S(2)}) async-start(bf16[16,16,2176]{2,1,0:T(8,128)(2,1)} %get-tuple-element.56), calls=%async_computation.3 | async-start | bytes 2228224 | tf_op jit(solution)/shard_map/all_to_all | solution.py:605
  88.8 4.6 %copy-start.2 = (f32[2,2048]{1,0:T(2,128)S(1)}, f32[2,2048]{1,0:T(2,128)}, u32[]{:S(2)}) copy-start(f32[2,2048]{1,0:T(2,128)} %m_any.3) | copy-start | bytes 49156
  88.8 4.6 %copy-start.3 = (f32[2,2048]{1,0:T(2,128)S(1)}, f32[2,2048]{1,0:T(2,128)}, u32[]{:S(2)}) copy-start(f32[2,2048]{1,0:T(2,128)} %v_any.3) | copy-start | bytes 49156
  88.8 4.6 %copy-start.6 = (f32[2,8]{1,0:T(2,128)S(1)}, f32[2,8]{1,0:T(2,128)}, u32[]{:S(2)}) copy-start(f32[2,8]{1,0:T(2,128)} %bnm_any.3) | copy-start | bytes 196
  96.4 11.1 %collective-permute-start.12 = (bf16[256,2176]{1,0:T(8,128)(2,1)S(1)}, bf16[256,2176]{1,0:T(8,128)(2,1)S(1)}, u32[]{:S(2)}, u32[]{:S(2)}) collective-permute-start(bf16[256,2176]{1,0:T(8,128)(2,1)S(1)} %bitcast.5), channel_id=1, source_target_pairs={{0,1},{1,0},{2,3},{3,2},{4,5},{5,4},{6,7},{7,6},{8,9},{9,8},{10,11... | collective-permute-start | bytes 3342344 | tf_op jit(solution)/shard_map/ppermute | solution.py:645
  103.8 6.1 %collective-permute-start.11 = (bf16[256,2176]{1,0:T(8,128)(2,1)S(1)}, bf16[256,2176]{1,0:T(8,128)(2,1)S(1)}, u32[]{:S(2)}, u32[]{:S(2)}) collective-permute-start(bf16[256,2176]{1,0:T(8,128)(2,1)S(1)} %bitcast.3), channel_id=1, source_target_pairs={{0,1},{1,0},{2,3},{3,2},{4,5},{5,4},{6,7},{7,6},{8,9},{9,8},{10,11... | collective-permute-start | bytes 3342344 | tf_op jit(solution)/shard_map/ppermute | solution.py:647

commit v6 on v5

--- a/solution.py
+++ b/solution.py
@@ -264,8 +264,9 @@
     up = kept.at[0:TALL]
     mid = kept.at[TALL : 2 * TALL]
     mine, far = p0[...].astype(F32), p1[...].astype(F32)
-    low = jnp.where(zh == 0, mine, far)
-    high = jnp.where(zh == 0, far, mine)
+    even = (lax.axis_index("zl") & 1) == 0
+    low = jnp.where(even, mine, far)
+    high = jnp.where(even, far, mine)
     near_ref[...] = jnp.concatenate([low, high], axis=0).astype(BF)
     sums = jnp.sum(stat[...], axis=0)
     mean = sums[0:1] / COUNT
@@ -364,13 +365,10 @@
 
 
 def rows_kernel(n0, n1, n2, n3, after_ref, base_ref, w, four):
-    zl = lax.axis_index("zl")
-    halves = []
-    for high in range(2):
-        for k, block in enumerate((n0, n1, n2, n3)):
-            four[2 * k : 2 * k + 2, :] = block[...].astype(F32)[2 * high : 2 * high + 2]
-        halves.append(pltpu.roll(four[...], 2 * zl, 0))
-    both = jnp.concatenate(halves, axis=0)
+    for k, block in enumerate((n0, n1, n2, n3)):
+        four[4 * k : 4 * k + 4, :] = block[...].astype(F32)
+    pair = 2 * lax.axis_index("zh") + (lax.axis_index("zl") >> 1)
+    both = pltpu.roll(four[...], 4 * pair, 0)
     w[:, :C] = both[:, C : 2 * C]
     w[:, C:] = both[:, 2 * C + EXT :]
     base_ref[:, :C] = both[:, :C].astype(BF)
@@ -383,7 +381,7 @@
         in_specs=[VMEM] * 4 + [SMEM],
         out_specs=[VMEM, VMEM],
         out_shape=[jax.ShapeDtypeStruct((16, WIDE), BF), jax.ShapeDtypeStruct((16, WIDE), F32)],
-        scratch_shapes=[pltpu.VMEM((8, PIECE), F32)],
+        scratch_shapes=[pltpu.VMEM((16, PIECE), F32)],
         compiler_params=params(),
         cost_estimate=pl.CostEstimate(flops=16 * PIECE, bytes_accessed=500000, transcendentals=0),
         name="rows",
@@ -627,13 +625,13 @@
     stats, piece = stats_call(
         features, weight, cotangent, pre_act, master, momentum, bn_params, bn_momentum
     )
-    pieces = [piece, lax.ppermute(piece, AXES, shift_pairs(lambda x, y, z: (x, y, z ^ 4)))]
+    pieces = [piece, lax.ppermute(piece, AXES, shift_pairs(lambda x, y, z: (x, y, z ^ 1)))]
     later, stats = lax.optimization_barrier((features, stats))
     up, kept = prep_call(later, weight, cotangent, pre_act)
     stats = exchange(stats, GX)
     send, own, near, coef = grad_call(stats, kept, bn_params, pieces)
     half, token = pair_call(own, swap(send))
-    blocks = ring(near, 4, lambda k, x, y, z: (x, y, (z & 4) + ((z + k) & 3)))
+    blocks = ring(near, 4, lambda k, x, y, z: (x, y, (z + 2 * k) & 7))
     base, w_rows = rows_call(blocks, token)
     bases = ring(base, 4, lambda k, x, y, z: ((x + k) % 4, y, z))
     part, base, token = plane_call(exchange(half.reshape(16, 16, WIDE), XY), bases)

time: 114 us -> 113 us (level)
  waiting for transfers between devices: 31.8 us -> 28.8 us
  starting transfers between devices: 51.9 us -> 54 us
    ppermute x1, starting transfers between devices: 5.36 us -> 0.83 us  [shards(): lax.ppermute(piece, AXES, shift_pairs(lambda x, y, z: (x, y, z ^ 1)))]
    ppermute x9, starting transfers between devices: 10.8 us -> 14.2 us  [ring(): lax.ppermute(block, AXES, shift_pairs(functools.partial(move, size - k)))]
    all_to_all x4, waiting for transfers between devices: 8.5 us -> 5.21 us  [exchange(): return lax.all_to_all(block, axes, 0, 0, tiled=True)]
    ppermute x1, starting transfers between devices: 3.75 us -> 6.3 us  [shards(): b1 = swap(b0)]
    ppermute x1, starting transfers between devices: 2.97 us -> 4.88 us  [shards(): a1 = swap(a0)]
    all_to_all x4, starting transfers between devices: 26.8 us -> 25.4 us  [exchange(): return lax.all_to_all(block, axes, 0, 0, tiled=True)]
  transfers between devices with their start and end apart: 17 -> 17, of which waited for: 11 -> 12; matrix products, arithmetic and copies ran while one was open for 0% -> 0% of each run, Pallas kernels for 12% -> 12%
where the time goes in v6:
time: 113 us; the launch traced here: 112 us
  starting transfers between devices  54 us (48%)
  waiting for transfers between devices  28.8 us (25%)
  Pallas kernels  26.2 us (23%)
  local copies, waits for them, and re-layouts  2.11 us (2%)
    all_to_all x4, starting transfers between devices, exchange(): return lax.all_to_all(block, axes, 0, 0, tiled=True)  25.4 us
    ppermute x9, waiting for transfers between devices, ring(): lax.ppermute(block, AXES, shift_pairs(functools.partial(move, size - k)))  17.9 us
    ppermute x9, starting transfers between devices, ring(): lax.ppermute(block, AXES, shift_pairs(functools.partial(move, size - k)))  14.2 us
    ppermute x1, starting transfers between devices, shards(): b1 = swap(b0)  6.3 us
    all_to_all x4, waiting for transfers between devices, exchange(): return lax.all_to_all(block, axes, 0, 0, tiled=True)  5.21 us
    pallas_call x1, Pallas kernels, prep_call(): pl.pallas_call(prep_kernel, in_specs=[ANY] * 4, out_specs=[ANY, ANY], out...  5.06 us
    ppermute x1, starting transfers between devices, shards(): a1 = swap(a0)  4.88 us
    pallas_call x1, Pallas kernels, stats_call(): pl.pallas_call(stats_kernel, in_specs=[ANY] * 8, out_specs=[VMEM, VMEM],...  4.57 us
  transfers between devices with their start and end apart: 17, of which 12 were waited for; matrix products, arithmetic and copies ran while one was open for 0% of the time, Pallas kernels for 12%

profile of v6, /device:TPU:1, one launch (start us, length us, event | category | flops | bytes accessed | tf_op | source)
XLA Modules:
  0.0 112.0 jit_solution(13885641591461038560)
XLA Ops:
  0.6 4.6 %stats.1 = (f32[8,4,2048]{2,1,0:T(4,128)}, bf16[2,4352]{1,0:T(2,128)(2,1)}) custom-call(bf16[392,512]{1,0:T(8,128)(2,1)} %f_any.2, bf16[512,2048]{1,0:T(8,128)(2,1)} %w_any.5, bf16[392,2048]{1,0:T(8,128)(2,1)} %cot_any.3, bf16[392,2048]{1,0:T(8,128)(2,1)} %pre_any.3, f32[2,2048]{1,0:T(2,128)} %m_any.3, f32[2,2048]{1,0:T(2,128)} %v_any.3, f32[2,2048]{1,0:T(2,128)} %bn_v.1, ...), custom_call_target="tpu_custom_call" | custom-call | flops 822083584 | bytes 7500000 | tf_op jit(solution)/shard_map/stats/pallas_call | solution.py:166
  5.2 11.5 %all-to-all-start = ((f32[8,4,2048]{2,1,0:T(4,128)}), f32[8,4,2048]{2,1,0:T(4,128)S(1)}, u32[]{:S(2)}, u32[]{:S(2)}) async-start(f32[8,4,2048]{2,1,0:T(4,128)} %get-tuple-element.41), calls=%async_computation | async-start | bytes 524288 | tf_op jit(solution)/shard_map/all_to_all | solution.py:603
  16.7 0.0 copy-start.1
  16.7 0.0 copy-start.5
  16.7 0.8 collective-permute-start
  17.5 5.1 %prep.1 = (bf16[392,2048]{1,0:T(8,128)(2,1)}, bf16[928,2048]{1,0:T(8,128)(2,1)}) custom-call(bf16[392,512]{1,0:T(8,128)(2,1)} %f_any.2, bf16[512,2048]{1,0:T(8,128)(2,1)} %w_any.5, bf16[392,2048]{1,0:T(8,128)(2,1)} %cot_any.3, bf16[392,2048]{1,0:T(8,128)(2,1)} %pre_any.3), custom_call_target="tpu_custom_call" | custom-call | flops 1233125376 | bytes 9000000 | tf_op jit(solution)/shard_map/prep/pallas_call | solution.py:231
  22.6 0.9 collective-permute-done.p1
  23.6 3.2 %all-to-all-done.stat = f32[8,4,2048]{2,1,0:T(4,128)S(1)} async-done(((f32[8,4,2048]{2,1,0:T(4,128)}), f32[8,4,2048]{2,1,0:T(4,128)S(1)}, u32[]{:S(2)}, u32[]{:S(2)}) %all-to-all-start) | async-done | bytes 262176 | tf_op jit(solution)/shard_map/all_to_all | solution.py:603
  26.8 0.0 copy-done.1
  26.8 0.0 copy-done.5
  26.8 0.0 copy-start
  26.8 2.1 %copy-done = bf16[928,2048]{1,0:T(8,128)(2,1)S(1)} copy-done((bf16[928,2048]{1,0:T(8,128)(2,1)S(1)}, bf16[928,2048]{1,0:T(8,128)(2,1)}, u32[]{:S(2)}) %copy-start) | copy-done | bytes 3801112
  28.9 1.5 %grad.1 = (bf16[256,2176]{1,0:T(8,128)(2,1)S(1)}, bf16[256,2176]{1,0:T(8,128)(2,1)S(1)}, bf16[4,4352]{1,0:T(4,128)(2,1)S(1)}, f32[4,2048]{1,0:T(4,128)S(1)}) custom-call(f32[8,4,2048]{2,1,0:T(4,128)S(1)} %all-to-all-done.stat, bf16[928,2048]{1,0:T(8,128)(2,1)S(1)} %copy-done, f32[2,2048]{1,0:T(2,128)S(1)} %copy-done.1, bf16[2,4352]{1,0:T(2,128)(2,1)S(1)} %copy-done.5, ...), custom_call_target="tpu_custom_call" | custom-call | flops 822083584 | bytes 7000000 | tf_op jit(solution)/shard_map/grad/pallas_call | solution.py:302
  30.3 0.0 copy-start.4
  30.3 2.5 %collective-permute-start.1 = (bf16[256,2176]{1,0:T(8,128)(2,1)S(1)}, bf16[256,2176]{1,0:T(8,128)(2,1)S(1)}, u32[]{:S(2)}, u32[]{:S(2)}) collective-permute-start(bf16[256,2176]{1,0:T(8,128)(2,1)S(1)} %get-tuple-element.45), channel_id=1, source_target_pairs={{0,1},{1,0},{2,3},{3,2},{4,5},{5,4},{6,7},{7,6},{8,9},{9,8},{10,11... | collective-permute-start | bytes 3342344 | tf_op jit(solution)/shard_map/ppermute | solution.py:633
  32.8 2.4 %collective-permute-done.1.got_ref = bf16[256,2176]{1,0:T(8,128)(2,1)S(1)} collective-permute-done((bf16[256,2176]{1,0:T(8,128)(2,1)S(1)}, bf16[256,2176]{1,0:T(8,128)(2,1)S(1)}, u32[]{:S(2)}, u32[]{:S(2)}) %collective-permute-start.1) | collective-permute-done | bytes 1114144 | tf_op jit(solution)/shard_map/ppermute | solution.py:633
  35.2 1.3 %pair.1 = (bf16[256,2176]{1,0:T(8,128)(2,1)}, s32[1]{0:T(128)}) custom-call(bf16[256,2176]{1,0:T(8,128)(2,1)S(1)} %get-tuple-element.44.own_ref, bf16[256,2176]{1,0:T(8,128)(2,1)S(1)} %collective-permute-done.1.got_ref), custom_call_target="tpu_custom_call" | custom-call | flops 557056 | bytes 3300000 | tf_op jit(solution)/shard_map/pair/pallas_call | solution.py:397
  36.4 0.0 copy-done.4
  36.5 5.5 %all-to-all-start.1 = ((bf16[16,16,2176]{2,1,0:T(8,128)(2,1)}), bf16[16,16,2176]{2,1,0:T(8,128)(2,1)S(1)}, u32[]{:S(2)}, u32[]{:S(2)}) async-start(bf16[16,16,2176]{2,1,0:T(8,128)(2,1)} %bitcast), calls=%async_computation.1 | async-start | bytes 2228224 | tf_op jit(solution)/shard_map/all_to_all | solution.py:603
  42.0 1.3 %collective-permute-start.2 = (bf16[4,4352]{1,0:T(4,128)(2,1)S(1)}, bf16[4,4352]{1,0:T(4,128)(2,1)S(1)}, u32[]{:S(2)}, u32[]{:S(2)}) collective-permute-start(bf16[4,4352]{1,0:T(4,128)(2,1)S(1)} %get-tuple-element.47.n0), channel_id=1, source_target_pairs={{0,144},{1,145},{2,146},{3,147},{4,148},{5,149},{6,150},{7,151},{8... | collective-permute-start | bytes 104456 | tf_op jit(solution)/shard_map/ppermute | solution.py:618
  43.3 5.0 %collective-permute-start.3 = (bf16[4,4352]{1,0:T(4,128)(2,1)S(1)}, bf16[4,4352]{1,0:T(4,128)(2,1)S(1)}, u32[]{:S(2)}, u32[]{:S(2)}) collective-permute-start(bf16[4,4352]{1,0:T(4,128)(2,1)S(1)} %get-tuple-element.47.n0), channel_id=1, source_target_pairs={{0,128},{1,129},{2,130},{3,131},{4,132},{5,133},{6,134},{7,135},{8... | collective-permute-start | bytes 104456 | tf_op jit(solution)/shard_map/ppermute | solution.py:618
  48.3 0.0 collective-permute-start.4
  48.3 0.0 collective-permute-done.2.n1
  48.3 1.8 %collective-permute-done.3.n2 = bf16[4,4352]{1,0:T(4,128)(2,1)S(1)} collective-permute-done((bf16[4,4352]{1,0:T(4,128)(2,1)S(1)}, bf16[4,4352]{1,0:T(4,128)(2,1)S(1)}, u32[]{:S(2)}, u32[]{:S(2)}) %collective-permute-start.3) | collective-permute-done | bytes 34848 | tf_op jit(solution)/shard_map/ppermute | solution.py:618
  50.1 3.4 %collective-permute-done.4.n3 = bf16[4,4352]{1,0:T(4,128)(2,1)S(1)} collective-permute-done((bf16[4,4352]{1,0:T(4,128)(2,1)S(1)}, bf16[4,4352]{1,0:T(4,128)(2,1)S(1)}, u32[]{:S(2)}, u32[]{:S(2)}) %collective-permute-start.4) | collective-permute-done | bytes 34848 | tf_op jit(solution)/shard_map/ppermute | solution.py:618
  53.5 0.7 rows.1
  54.2 2.6 %collective-permute-start.5 = (bf16[16,2176]{1,0:T(8,128)(2,1)S(1)}, bf16[16,2176]{1,0:T(8,128)(2,1)S(1)}, u32[]{:S(2)}, u32[]{:S(2)}) collective-permute-start(bf16[16,2176]{1,0:T(8,128)(2,1)S(1)} %get-tuple-element.49.b0), channel_id=1, source_target_pairs={{0,96},{1,97},{2,98},{3,99},{4,100},{5,101},{6,102},{7,103},{8,104... | collective-permute-start | bytes 208904 | tf_op jit(solution)/shard_map/ppermute | solution.py:618
  56.8 0.4 collective-permute-start.6
  57.2 0.4 collective-permute-start.7
  57.7 0.5 collective-permute-done.5.b1
  58.2 3.4 %collective-permute-done.6.b2 = bf16[16,2176]{1,0:T(8,128)(2,1)S(1)} collective-permute-done((bf16[16,2176]{1,0:T(8,128)(2,1)S(1)}, bf16[16,2176]{1,0:T(8,128)(2,1)S(1)}, u32[]{:S(2)}, u32[]{:S(2)}) %collective-permute-start.6) | collective-permute-done | bytes 69664 | tf_op jit(solution)/shard_map/ppermute | solution.py:618
  61.5 0.7 collective-permute-done.7.b3
  62.2 0.0 all-to-all-done.1.got_ref
  62.2 1.4 %plane.1 = (bf16[8,16,2176]{2,1,0:T(8,128)(2,1)}, bf16[4,16,2176]{2,1,0:T(8,128)(2,1)S(1)}, s32[1]{0:T(128)}) custom-call(bf16[16,16,2176]{2,1,0:T(8,128)(2,1)S(1)} %all-to-all-done.1.got_ref, bf16[16,2176]{1,0:T(8,128)(2,1)S(1)} %get-tuple-element.49.b0, bf16[16,2176]{1,0:T(8,128)(2,1)S(1)} %collective-permute-done.5.b1, ...), custom_call_target="tpu_custom_call" | custom-call | flops 557056 | bytes 1700000 | tf_op jit(solution)/shard_map/plane/pallas_call | solution.py:421
  63.6 3.5 %all-to-all-start.2 = ((bf16[8,16,2176]{2,1,0:T(8,128)(2,1)}), bf16[8,16,2176]{2,1,0:T(8,128)(2,1)S(1)}, u32[]{:S(2)}, u32[]{:S(2)}) async-start(bf16[8,16,2176]{2,1,0:T(8,128)(2,1)} %get-tuple-element.53), calls=%async_computation.2 | async-start | bytes 1114112 | tf_op jit(solution)/shard_map/all_to_all | solution.py:603
  67.2 1.4 %collective-permute-start.10 = (bf16[4,16,2176]{2,1,0:T(8,128)(2,1)S(1)}, bf16[4,16,2176]{2,1,0:T(8,128)(2,1)S(1)}, u32[]{:S(2)}, u32[]{:S(2)}) collective-permute-start(bf16[4,16,2176]{2,1,0:T(8,128)(2,1)S(1)} %get-tuple-element.55.b0), channel_id=1, source_target_pairs={{0,2},{1,3},{2,4},{3,5},{4,6},{5,7},{6,0},{7,1},{8,10},{9,11},{10,... | collective-permute-start | bytes 835592 | tf_op jit(solution)/shard_map/ppermute | solution.py:618
  68.6 1.5 %collective-permute-start.8 = (bf16[4,16,2176]{2,1,0:T(8,128)(2,1)S(1)}, bf16[4,16,2176]{2,1,0:T(8,128)(2,1)S(1)}, u32[]{:S(2)}, u32[]{:S(2)}) collective-permute-start(bf16[4,16,2176]{2,1,0:T(8,128)(2,1)S(1)} %get-tuple-element.55.b0), channel_id=1, source_target_pairs={{0,6},{1,7},{2,0},{3,1},{4,2},{5,3},{6,4},{7,5},{8,14},{9,15},{10,... | collective-permute-start | bytes 835592 | tf_op jit(solution)/shard_map/ppermute | solution.py:618
  70.1 1.5 %collective-permute-start.9 = (bf16[4,16,2176]{2,1,0:T(8,128)(2,1)S(1)}, bf16[4,16,2176]{2,1,0:T(8,128)(2,1)S(1)}, u32[]{:S(2)}, u32[]{:S(2)}) collective-permute-start(bf16[4,16,2176]{2,1,0:T(8,128)(2,1)S(1)} %get-tuple-element.55.b0), channel_id=1, source_target_pairs={{0,4},{1,5},{2,6},{3,7},{4,0},{5,1},{6,2},{7,3},{8,12},{9,13},{10,... | collective-permute-start | bytes 835592 | tf_op jit(solution)/shard_map/ppermute | solution.py:618
  71.5 2.5 %collective-permute-done.10.b3 = bf16[4,16,2176]{2,1,0:T(8,128)(2,1)S(1)} collective-permute-done((bf16[4,16,2176]{2,1,0:T(8,128)(2,1)S(1)}, bf16[4,16,2176]{2,1,0:T(8,128)(2,1)S(1)}, u32[]{:S(2)}, u32[]{:S(2)}) %collective-permute-start.10) | collective-permute-done | bytes 278560 | tf_op jit(solution)/shard_map/ppermute | solution.py:618
  74.0 0.0 collective-permute-done.8.b1
  74.0 5.7 %collective-permute-done.9.b2 = bf16[4,16,2176]{2,1,0:T(8,128)(2,1)S(1)} collective-permute-done((bf16[4,16,2176]{2,1,0:T(8,128)(2,1)S(1)}, bf16[4,16,2176]{2,1,0:T(8,128)(2,1)S(1)}, u32[]{:S(2)}, u32[]{:S(2)}) %collective-permute-start.9) | collective-permute-done | bytes 278560 | tf_op jit(solution)/shard_map/ppermute | solution.py:618
  79.7 2.0 %all-to-all-done.2.got_ref = bf16[8,16,2176]{2,1,0:T(8,128)(2,1)S(1)} async-done(((bf16[8,16,2176]{2,1,0:T(8,128)(2,1)}), bf16[8,16,2176]{2,1,0:T(8,128)(2,1)S(1)}, u32[]{:S(2)}, u32[]{:S(2)}) %all-to-all-start.2) | async-done | bytes 557088 | tf_op jit(solution)/shard_map/all_to_all | solution.py:603
  81.7 1.2 %column.1 = (bf16[16,16,2176]{2,1,0:T(8,128)(2,1)}, f32[2,2048]{1,0:T(2,128)S(1)}, s32[1]{0:T(128)}) custom-call(bf16[8,16,2176]{2,1,0:T(8,128)(2,1)S(1)} %all-to-all-done.2.got_ref, f32[16,2176]{1,0:T(8,128)S(1)} %get-tuple-element.54.w, bf16[4,16,2176]{2,1,0:T(8,128)(2,1)S(1)} %collective-permute-done.8.b1, ...), custom_call_target="tpu_custom_call" | custom-call | flops 278528 | bytes 1700000 | tf_op jit(solution)/shard_map/column/pallas_call | solution.py:457
  82.9 4.8 %all-to-all-start.3 = ((bf16[16,16,2176]{2,1,0:T(8,128)(2,1)}), bf16[16,16,2176]{2,1,0:T(8,128)(2,1)S(1)}, u32[]{:S(2)}, u32[]{:S(2)}) async-start(bf16[16,16,2176]{2,1,0:T(8,128)(2,1)} %get-tuple-element.56), calls=%async_computation.3 | async-start | bytes 2228224 | tf_op jit(solution)/shard_map/all_to_all | solution.py:603
  87.8 0.0 copy-start.2
  87.8 0.0 copy-start.3
  87.8 0.0 copy-start.6
  87.8 4.5 %ginput.1 = (bf16[392,512]{1,0:T(8,128)(2,1)}, s32[1]{0:T(128)}) custom-call(bf16[512,2048]{1,0:T(8,128)(2,1)} %w_any.5, bf16[928,2048]{1,0:T(8,128)(2,1)} %get-tuple-element.40.kept.kept_any, f32[4,2048]{1,0:T(4,128)} %copy-done.4, s32[1]{0:T(128)} %get-tuple-element.50.after_ref), custom_call_target="tpu_custom_call" | custom-call | flops 822083584 | bytes 5500000 | tf_op jit(solution)/shard_map/ginput/pallas_call | solution.py:349
  92.3 0.0 copy-done.2
  92.3 0.0 copy-done.3
  92.4 0.0 copy-done.6
  92.4 3.1 %basis.1 = (bf16[16,16,2176]{2,1,0:T(8,128)(2,1)S(1)}, f32[2,4224]{1,0:T(2,128)S(1)}) custom-call(bf16[4,16,2176]{2,1,0:T(8,128)(2,1)S(1)} %get-tuple-element.55.b0, bf16[4,16,2176]{2,1,0:T(8,128)(2,1)S(1)} %collective-permute-done.8.b1, bf16[4,16,2176]{2,1,0:T(8,128)(2,1)S(1)} %collective-permute-done.9.b2, ...), custom_call_target="tpu_custom_call" | custom-call | bytes 2200000 | tf_op jit(solution)/shard_map/basis/pallas_call | solution.py:489
  95.4 4.9 %collective-permute-start.12 = (bf16[256,2176]{1,0:T(8,128)(2,1)S(1)}, bf16[256,2176]{1,0:T(8,128)(2,1)S(1)}, u32[]{:S(2)}, u32[]{:S(2)}) collective-permute-start(bf16[256,2176]{1,0:T(8,128)(2,1)S(1)} %bitcast.5), channel_id=1, source_target_pairs={{0,1},{1,0},{2,3},{3,2},{4,5},{5,4},{6,7},{7,6},{8,9},{9,8},{10,11... | collective-permute-start | bytes 3342344 | tf_op jit(solution)/shard_map/ppermute | solution.py:643
  100.3 0.0 all-to-all-done.3
  100.3 6.3 %collective-permute-start.11 = (bf16[256,2176]{1,0:T(8,128)(2,1)S(1)}, bf16[256,2176]{1,0:T(8,128)(2,1)S(1)}, u32[]{:S(2)}, u32[]{:S(2)}) collective-permute-start(bf16[256,2176]{1,0:T(8,128)(2,1)S(1)} %bitcast.3), channel_id=1, source_target_pairs={{0,1},{1,0},{2,3},{3,2},{4,5},{5,4},{6,7},{7,6},{8,9},{9,8},{10,11... | collective-permute-start | bytes 3342344 | tf_op jit(solution)/shard_map/ppermute | solution.py:645
  106.6 0.0 collective-permute-done.12.a1
  106.6 2.4 %collective-permute-done.11.b1 = bf16[256,2176]{1,0:T(8,128)(2,1)S(1)} collective-permute-done((bf16[256,2176]{1,0:T(8,128)(2,1)S(1)}, bf16[256,2176]{1,0:T(8,128)(2,1)S(1)}, u32[]{:S(2)}, u32[]{:S(2)}) %collective-permute-start.11) | collective-permute-done | bytes 1114144 | tf_op jit(solution)/shard_map/ppermute | solution.py:645
  109.0 2.9 %update.1 = (bf16[512,2048]{1,0:T(8,128)(2,1)}, bf16[2,2048]{1,0:T(2,128)(2,1)}, f32[2,2048]{1,0:T(2,128)}, f32[2,2048]{1,0:T(2,128)}, f32[2,8]{1,0:T(2,128)}, /*index=5*/f32[2,8]{1,0:T(2,128)}) custom-call(bf16[256,2176]{1,0:T(8,128)(2,1)S(1)} %bitcast.4, bf16[256,2176]{1,0:T(8,128)(2,1)S(1)} %collective-permute-done.11.b1, bf16[256,2176]{1,0:T(8,128)(2,1)S(1)} %bitcast.6, ...), custom_call_target="tpu_custom_call" | custom-call | flops 268435456 | bytes 6500000 | tf_op jit(solution)/shard_map/update/pallas_call | solution.py:590
Async XLA Ops:
  5.2 21.6 %all-to-all-start = ((f32[8,4,2048]{2,1,0:T(4,128)}), f32[8,4,2048]{2,1,0:T(4,128)S(1)}, u32[]{:S(2)}, u32[]{:S(2)}) async-start(f32[8,4,2048]{2,1,0:T(4,128)} %get-tuple-element.41), calls=%async_computation | async-start | bytes 524288 | tf_op jit(solution)/shard_map/all_to_all | solution.py:603
  16.7 10.1 %copy-start.1 = (f32[2,2048]{1,0:T(2,128)S(1)}, f32[2,2048]{1,0:T(2,128)}, u32[]{:S(2)}) copy-start(f32[2,2048]{1,0:T(2,128)} %bn_v.1) | copy-start | bytes 49156
  16.7 10.1 %copy-start.5 = (bf16[2,4352]{1,0:T(2,128)(2,1)S(1)}, bf16[2,4352]{1,0:T(2,128)(2,1)}, u32[]{:S(2)}) copy-start(bf16[2,4352]{1,0:T(2,128)(2,1)} %get-tuple-element.42.p0) | copy-start | bytes 52228
  16.7 6.8 %collective-permute-start = (bf16[2,4352]{1,0:T(2,128)(2,1)}, bf16[2,4352]{1,0:T(2,128)(2,1)S(1)}, u32[]{:S(2)}, u32[]{:S(2)}) collective-permute-start(bf16[2,4352]{1,0:T(2,128)(2,1)} %get-tuple-element.42.p0), channel_id=1, source_target_pairs={{0,8},{1,9},{2,10},{3,11},{4,12},{5,13},{6,14},{7,15},{8,0},{9,1},... | collective-permute-start | bytes 52232 | tf_op jit(solution)/shard_map/ppermute | solution.py:628
  26.8 2.1 %copy-start = (bf16[928,2048]{1,0:T(8,128)(2,1)S(1)}, bf16[928,2048]{1,0:T(8,128)(2,1)}, u32[]{:S(2)}) copy-start(bf16[928,2048]{1,0:T(8,128)(2,1)} %get-tuple-element.40.kept.kept_any) | copy-start | bytes 11403268
  30.3 6.1 %copy-start.4 = (f32[4,2048]{1,0:T(4,128)}, f32[4,2048]{1,0:T(4,128)S(1)}, u32[]{:S(2)}) copy-start(f32[4,2048]{1,0:T(4,128)S(1)} %get-tuple-element.43.coef_any) | copy-start | bytes 98308
  30.3 4.8 %collective-permute-start.1 = (bf16[256,2176]{1,0:T(8,128)(2,1)S(1)}, bf16[256,2176]{1,0:T(8,128)(2,1)S(1)}, u32[]{:S(2)}, u32[]{:S(2)}) collective-permute-start(bf16[256,2176]{1,0:T(8,128)(2,1)S(1)} %get-tuple-element.45), channel_id=1, source_target_pairs={{0,1},{1,0},{2,3},{3,2},{4,5},{5,4},{6,7},{7,6},{8,9},{9,8},{10,11... | collective-permute-start | bytes 3342344 | tf_op jit(solution)/shard_map/ppermute | solution.py:633
  36.5 25.8 %all-to-all-start.1 = ((bf16[16,16,2176]{2,1,0:T(8,128)(2,1)}), bf16[16,16,2176]{2,1,0:T(8,128)(2,1)S(1)}, u32[]{:S(2)}, u32[]{:S(2)}) async-start(bf16[16,16,2176]{2,1,0:T(8,128)(2,1)} %bitcast), calls=%async_computation.1 | async-start | bytes 2228224 | tf_op jit(solution)/shard_map/all_to_all | solution.py:603
  42.0 6.3 %collective-permute-start.2 = (bf16[4,4352]{1,0:T(4,128)(2,1)S(1)}, bf16[4,4352]{1,0:T(4,128)(2,1)S(1)}, u32[]{:S(2)}, u32[]{:S(2)}) collective-permute-start(bf16[4,4352]{1,0:T(4,128)(2,1)S(1)} %get-tuple-element.47.n0), channel_id=1, source_target_pairs={{0,144},{1,145},{2,146},{3,147},{4,148},{5,149},{6,150},{7,151},{8... | collective-permute-start | bytes 104456 | tf_op jit(solution)/shard_map/ppermute | solution.py:618
  43.3 6.8 %collective-permute-start.3 = (bf16[4,4352]{1,0:T(4,128)(2,1)S(1)}, bf16[4,4352]{1,0:T(4,128)(2,1)S(1)}, u32[]{:S(2)}, u32[]{:S(2)}) collective-permute-start(bf16[4,4352]{1,0:T(4,128)(2,1)S(1)} %get-tuple-element.47.n0), channel_id=1, source_target_pairs={{0,128},{1,129},{2,130},{3,131},{4,132},{5,133},{6,134},{7,135},{8... | collective-permute-start | bytes 104456 | tf_op jit(solution)/shard_map/ppermute | solution.py:618
  48.3 5.2 %collective-permute-start.4 = (bf16[4,4352]{1,0:T(4,128)(2,1)S(1)}, bf16[4,4352]{1,0:T(4,128)(2,1)S(1)}, u32[]{:S(2)}, u32[]{:S(2)}) collective-permute-start(bf16[4,4352]{1,0:T(4,128)(2,1)S(1)} %get-tuple-element.47.n0), channel_id=1, source_target_pairs={{0,16},{1,17},{2,18},{3,19},{4,20},{5,21},{6,22},{7,23},{8,24},{9,... | collective-permute-start | bytes 104456 | tf_op jit(solution)/shard_map/ppermute | solution.py:618
  54.2 4.0 %collective-permute-start.5 = (bf16[16,2176]{1,0:T(8,128)(2,1)S(1)}, bf16[16,2176]{1,0:T(8,128)(2,1)S(1)}, u32[]{:S(2)}, u32[]{:S(2)}) collective-permute-start(bf16[16,2176]{1,0:T(8,128)(2,1)S(1)} %get-tuple-element.49.b0), channel_id=1, source_target_pairs={{0,96},{1,97},{2,98},{3,99},{4,100},{5,101},{6,102},{7,103},{8,104... | collective-permute-start | bytes 208904 | tf_op jit(solution)/shard_map/ppermute | solution.py:618
  56.8 4.7 %collective-permute-start.6 = (bf16[16,2176]{1,0:T(8,128)(2,1)S(1)}, bf16[16,2176]{1,0:T(8,128)(2,1)S(1)}, u32[]{:S(2)}, u32[]{:S(2)}) collective-permute-start(bf16[16,2176]{1,0:T(8,128)(2,1)S(1)} %get-tuple-element.49.b0), channel_id=1, source_target_pairs={{0,64},{1,65},{2,66},{3,67},{4,68},{5,69},{6,70},{7,71},{8,72},{9,... | collective-permute-start | bytes 208904 | tf_op jit(solution)/shard_map/ppermute | solution.py:618
  57.2 5.0 %collective-permute-start.7 = (bf16[16,2176]{1,0:T(8,128)(2,1)S(1)}, bf16[16,2176]{1,0:T(8,128)(2,1)S(1)}, u32[]{:S(2)}, u32[]{:S(2)}) collective-permute-start(bf16[16,2176]{1,0:T(8,128)(2,1)S(1)} %get-tuple-element.49.b0), channel_id=1, source_target_pairs={{0,32},{1,33},{2,34},{3,35},{4,36},{5,37},{6,38},{7,39},{8,40},{9,... | collective-permute-start | bytes 208904 | tf_op jit(solution)/shard_map/ppermute | solution.py:618
  63.6 18.1 %all-to-all-start.2 = ((bf16[8,16,2176]{2,1,0:T(8,128)(2,1)}), bf16[8,16,2176]{2,1,0:T(8,128)(2,1)S(1)}, u32[]{:S(2)}, u32[]{:S(2)}) async-start(bf16[8,16,2176]{2,1,0:T(8,128)(2,1)} %get-tuple-element.53), calls=%async_computation.2 | async-start | bytes 1114112 | tf_op jit(solution)/shard_map/all_to_all | solution.py:603
  67.2 6.9 %collective-permute-start.10 = (bf16[4,16,2176]{2,1,0:T(8,128)(2,1)S(1)}, bf16[4,16,2176]{2,1,0:T(8,128)(2,1)S(1)}, u32[]{:S(2)}, u32[]{:S(2)}) collective-permute-start(bf16[4,16,2176]{2,1,0:T(8,128)(2,1)S(1)} %get-tuple-element.55.b0), channel_id=1, source_target_pairs={{0,2},{1,3},{2,4},{3,5},{4,6},{5,7},{6,0},{7,1},{8,10},{9,11},{10,... | collective-permute-start | bytes 835592 | tf_op jit(solution)/shard_map/ppermute | solution.py:618
  68.6 5.4 %collective-permute-start.8 = (bf16[4,16,2176]{2,1,0:T(8,128)(2,1)S(1)}, bf16[4,16,2176]{2,1,0:T(8,128)(2,1)S(1)}, u32[]{:S(2)}, u32[]{:S(2)}) collective-permute-start(bf16[4,16,2176]{2,1,0:T(8,128)(2,1)S(1)} %get-tuple-element.55.b0), channel_id=1, source_target_pairs={{0,6},{1,7},{2,0},{3,1},{4,2},{5,3},{6,4},{7,5},{8,14},{9,15},{10,... | collective-permute-start | bytes 835592 | tf_op jit(solution)/shard_map/ppermute | solution.py:618
  70.1 9.6 %collective-permute-start.9 = (bf16[4,16,2176]{2,1,0:T(8,128)(2,1)S(1)}, bf16[4,16,2176]{2,1,0:T(8,128)(2,1)S(1)}, u32[]{:S(2)}, u32[]{:S(2)}) collective-permute-start(bf16[4,16,2176]{2,1,0:T(8,128)(2,1)S(1)} %get-tuple-element.55.b0), channel_id=1, source_target_pairs={{0,4},{1,5},{2,6},{3,7},{4,0},{5,1},{6,2},{7,3},{8,12},{9,13},{10,... | collective-permute-start | bytes 835592 | tf_op jit(solution)/shard_map/ppermute | solution.py:618
  82.9 17.4 %all-to-all-start.3 = ((bf16[16,16,2176]{2,1,0:T(8,128)(2,1)}), bf16[16,16,2176]{2,1,0:T(8,128)(2,1)S(1)}, u32[]{:S(2)}, u32[]{:S(2)}) async-start(bf16[16,16,2176]{2,1,0:T(8,128)(2,1)} %get-tuple-element.56), calls=%async_computation.3 | async-start | bytes 2228224 | tf_op jit(solution)/shard_map/all_to_all | solution.py:603
  87.8 4.6 %copy-start.2 = (f32[2,2048]{1,0:T(2,128)S(1)}, f32[2,2048]{1,0:T(2,128)}, u32[]{:S(2)}) copy-start(f32[2,2048]{1,0:T(2,128)} %m_any.3) | copy-start | bytes 49156
  87.8 4.6 %copy-start.3 = (f32[2,2048]{1,0:T(2,128)S(1)}, f32[2,2048]{1,0:T(2,128)}, u32[]{:S(2)}) copy-start(f32[2,2048]{1,0:T(2,128)} %v_any.3) | copy-start | bytes 49156
  87.8 4.6 %copy-start.6 = (f32[2,8]{1,0:T(2,128)S(1)}, f32[2,8]{1,0:T(2,128)}, u32[]{:S(2)}) copy-start(f32[2,8]{1,0:T(2,128)} %bnm_any.3) | copy-start | bytes 196
  95.4 11.2 %collective-permute-start.12 = (bf16[256,2176]{1,0:T(8,128)(2,1)S(1)}, bf16[256,2176]{1,0:T(8,128)(2,1)S(1)}, u32[]{:S(2)}, u32[]{:S(2)}) collective-permute-start(bf16[256,2176]{1,0:T(8,128)(2,1)S(1)} %bitcast.5), channel_id=1, source_target_pairs={{0,1},{1,0},{2,3},{3,2},{4,5},{5,4},{6,7},{7,6},{8,9},{9,8},{10,11... | collective-permute-start | bytes 3342344 | tf_op jit(solution)/shard_map/ppermute | solution.py:643
  100.3 8.7 %collective-permute-start.11 = (bf16[256,2176]{1,0:T(8,128)(2,1)S(1)}, bf16[256,2176]{1,0:T(8,128)(2,1)S(1)}, u32[]{:S(2)}, u32[]{:S(2)}) collective-permute-start(bf16[256,2176]{1,0:T(8,128)(2,1)S(1)} %bitcast.3), channel_id=1, source_target_pairs={{0,1},{1,0},{2,3},{3,2},{4,5},{5,4},{6,7},{7,6},{8,9},{9,8},{10,11... | collective-permute-start | bytes 3342344 | tf_op jit(solution)/shard_map/ppermute | solution.py:645
